TPU v7x, 128 devices: a whole 4x4x4 slice. The times are simulated.
128 devices in a mesh: tm: 16 (over z_lo, y, core), space: 8 (over z_hi, x).
Axes of the slice: x: 4, y: 4, z: 4 (z_hi: 2, z_lo: 2; z = z_hi * 2 + z_lo), core: 2. Of those that a mesh axis runs over, the one named last changes fastest.
Arguments:
- initial_states: float32 [16, 1024, 2048], P('tm', 'space'), may hold values from -6 to 6
- sources: float32 [16, 1024, 2048], P('tm', 'space'), may hold values from -4 to 4
- tile_class: int32 [8, 16], replicated, may hold values from 0 to 7
- coeff_sets: float32 [3, 8], replicated, may hold values from -0.5 to 0.5, as said below
- coarse_maps: float32 [16, 512, 512], P('tm'), may hold values from -1 to 1
Outputs:
- final_states: float32 [16, 1024, 2048], P('tm', 'space')
Inputs may be any that keep to these rules, and one draw needn't show every extreme that they name: `tile_class`: which of the 8 coefficient sets each 128 x 128 tile of cells uses. `coeff_sets`: row 0 holds positive diffusivities up to 0.12, rows 1 and 2 velocities along columns and along rows.
All inputs are finite; a program needn't handle non-finite values.
Results may differ from a plain program's by a relative error of at most 0.00019.
Values sent between devices are 32-bit elements; how exact they have to be, the bound alone decides.
No kernel may reach another device: no remote copies, remote signals or barrier semaphores. Data moves between devices by JAX's collectives and lax.ppermute only.
A program may use at most 64 MiB of HBM per device.

v0:
```python
import jax
import jax.numpy as jnp
from jax import lax
from jax.sharding import PartitionSpec as P

TILE = 128
BLK = 64
STEPS = 8
ITERS = 2


step_size = 0.6


def extended(x, sides, width):
    for axis, dim in sides:
        devices, length = (lax.axis_size(axis), x.shape[dim])
        up = [(i, (i + 1) % devices) for i in range(devices)]
        down = [(j, i) for i, j in up]
        last = lax.slice_in_dim(x, length - width, length, axis=dim)
        initial = lax.slice_in_dim(x, 0, width, axis=dim)
        before = lax.ppermute(last, axis, up)
        after = lax.ppermute(initial, axis, down)
        x = jnp.concatenate([before, x, after], axis=dim)
    return x


def shifted(value, axis, steps):
    count = lax.axis_size(axis)
    pairs = [(source, (source + steps) % count) for source in range(count)]
    return lax.ppermute(value, axis, pairs)


def advance(center, upper_rows, lower_rows, diffusivity, speed_cols, speed_rows, source):
    left_cells = jnp.roll(center, 1, axis=1)
    right_cells = jnp.roll(center, -1, axis=1)
    laplace = upper_rows + lower_rows + left_cells + right_cells - 4.0 * center
    transport = (
        jnp.maximum(speed_cols, 0.0) * (center - left_cells)
        + jnp.minimum(speed_cols, 0.0) * (right_cells - center)
        + jnp.maximum(speed_rows, 0.0) * (center - upper_rows)
        + jnp.minimum(speed_rows, 0.0) * (lower_rows - center)
    )
    return center + step_size * (diffusivity * laplace - transport + source)


def cell_fields(tile_class, coeff_sets, first_row, row_count, col_count, total_rows):
    global_rows = (first_row + jnp.arange(row_count, dtype=jnp.int32)) % total_rows
    row_tiles = global_rows // TILE
    selector = (
        row_tiles[:, None] == jnp.arange(tile_class.shape[0], dtype=jnp.int32)[None, :]
    ).astype(jnp.float32)
    class_rows = jnp.dot(
        selector, tile_class.astype(jnp.float32), preferred_element_type=jnp.float32
    )
    classes = jnp.repeat(class_rows, TILE, axis=1)
    fields = []
    for which_row in range(3):
        summed = jnp.zeros((row_count, col_count), jnp.float32)
        for class_label in range(8):
            summed = summed + jnp.where(
                classes == class_label, coeff_sets[which_row, class_label], 0.0
            )
        fields.append(summed)
    return (fields[0], fields[1], fields[2])


def per_device(initial_states, sources, tile_class, coeff_sets, coarse_maps):
    current_state = initial_states[0]
    source = sources[0]
    window_map = coarse_maps[0]
    row_count, col_count = current_state.shape
    strip_index = lax.axis_index("space")
    windows = lax.axis_size("tm")
    total_rows = row_count * lax.axis_size("space")
    coarse_local = row_count // BLK * (col_count // BLK)
    highest = lax.Precision.HIGHEST
    diffusivity, speed_cols, speed_rows = cell_fields(
        tile_class, coeff_sets, strip_index * row_count, row_count, col_count, total_rows
    )
    for outer_index in range(ITERS):

        def single_step(turn_index, carried):
            padded = extended(carried, (("space", 0),), 1)
            return advance(
                padded[1:-1], padded[:-2], padded[2:], diffusivity, speed_cols, speed_rows, source
            )

        finished = lax.fori_loop(0, STEPS, single_step, current_state)
        previous = shifted(finished, "tm", 1)
        defect = previous - current_state
        local_coarse = (
            defect.reshape(row_count // BLK, BLK, col_count // BLK, BLK)
            .mean(axis=(1, 3))
            .reshape(coarse_local)
        )
        coarse_defect = lax.all_gather(local_coarse, "space", axis=0, tiled=True)

        def link_step(turn_index, carried):
            mapped = jnp.dot(window_map, coarse_defect + carried, precision=highest)
            return shifted(mapped, "tm", 1)

        correction = lax.fori_loop(0, 2 * windows, link_step, jnp.zeros_like(coarse_defect))
        local_correction = lax.dynamic_slice_in_dim(
            correction, strip_index * coarse_local, coarse_local
        )
        blocks = local_correction.reshape(row_count // BLK, 1, col_count // BLK, 1)
        spread = jnp.broadcast_to(blocks, (row_count // BLK, BLK, col_count // BLK, BLK)).reshape(
            row_count, col_count
        )
        current_state = previous + spread
    return current_state[None]


def solution(mesh):
    placed = (P("tm", "space", None), P("tm", "space", None), P(), P(), P("tm", None, None))
    return jax.shard_map(
        per_device, mesh=mesh, in_specs=placed, out_specs=P("tm", "space", None), check_vma=False
    )
```

profile of v0, /device:TPU:1, one launch (start us, length us, event | category | flops | bytes accessed | tf_op | source)
XLA Modules:
  0.0 717.8 jit_solution(4893362110274449825)
XLA Ops:
  3.6 5.9 add_add_fusion
  22.4 100.1 %while.44 = (s32[]{:T(128)}, f32[128,2048]{1,0:T(8,128)}, f32[128,2048]{1,0:T(8,128)}, f32[128,16]{1,0:T(8,128)S(1)}, f32[128,16]{1,0:T(8,128)S(1)}, /*index=5*/f32[128,16]{1,0:T(8,128)S(1)}, s32[]{:T(128)}) while((s32[]{:T(128)}, f32[128,2048]{1,0:T(8,128)}, f32[128,2048]{1,0:T(8,128)}, f32[128,16]{1,0:T(8,128)S(1)}, ...), condition=%wide.region_1.2_spmd.clone, body=%wide.region_0.1_spmd.clone.sunk | while | flops 7602178 | bytes 22159544 | solution.py:89
  23.6 6.7 collective-permute-start.2
  31.1 5.3 collective-permute-done.3
  122.5 11.3 %collective-permute-start.6 = (f32[128,2048]{1,0:T(8,128)}, f32[128,2048]{1,0:T(8,128)S(1)}, u32[]{:S(2)}, u32[]{:S(2)}) collective-permute-start(f32[128,2048]{1,0:T(8,128)} %get-tuple-element.113), channel_id=1, source_target_pairs={{0,8},{8,16},{16,24},{24,32},{32,40},{40,48},{48,56},{56,64},{64,7... | collective-permute-start | bytes 3145736 | tf_op jit(solution)/shard_map/ppermute | solution.py:31
  135.1 10.7 %collective-permute-done.6 = f32[128,2048]{1,0:T(8,128)S(1)} collective-permute-done((f32[128,2048]{1,0:T(8,128)}, f32[128,2048]{1,0:T(8,128)S(1)}, u32[]{:S(2)}, u32[]{:S(2)}) %collective-permute-start.6) | collective-permute-done | bytes 1048608 | tf_op jit(solution)/shard_map/ppermute | solution.py:31
  151.8 15.6 %all-reduce = f32[512]{0:T(512)S(1)} all-reduce(f32[512]{0:T(512)S(1)} %dynamic-update-slice), channel_id=1, replica_groups=mesh['tm'=16,'space'=8] {'space'}, use_global_device_ids=true, to_apply=%add | all-reduce | flops 512 | bytes 4096
  167.4 197.5 %while.42 = (s32[]{:T(128)}, f32[512]{0:T(512)S(1)}, f32[512]{0:T(512)S(1)}, f32[512,512]{1,0:T(8,128)S(1)}, s32[]{:T(128)}) while((s32[]{:T(128)}, f32[512]{0:T(512)S(1)}, f32[512]{0:T(512)S(1)}, f32[512,512]{1,0:T(8,128)S(1)}, s32[]{:T(128)}) %tuple.125), condition=%wide.region_4.5_spmd, body=%wide.region_3.4_spmd.sunk | while | flops 3146242 | bytes 1067109 | solution.py:103
  168.4 5.9 collective-permute-start
  182.9 5.1 collective-permute-done
  189.0 5.1 collective-permute-done
  195.1 5.1 collective-permute-done
  201.2 5.1 collective-permute-done
  207.3 5.1 collective-permute-done
  237.8 5.1 collective-permute-done
  262.2 5.1 collective-permute-done
  286.6 5.1 collective-permute-done
  311.0 5.1 collective-permute-done
  353.7 5.1 collective-permute-done
  370.6 100.6 %while.45 = (s32[]{:T(128)}, f32[128,2048]{1,0:T(8,128)}, f32[128,2048]{1,0:T(8,128)}, f32[128,16]{1,0:T(8,128)S(1)}, f32[128,16]{1,0:T(8,128)S(1)}, /*index=5*/f32[128,16]{1,0:T(8,128)S(1)}, s32[]{:T(128)}) while((s32[]{:T(128)}, f32[128,2048]{1,0:T(8,128)}, f32[128,2048]{1,0:T(8,128)}, f32[128,16]{1,0:T(8,128)S(1)}, ...), condition=%wide.region_6.7_spmd.clone, body=%wide.region_5.6_spmd.clone.sunk | while | flops 7602178 | bytes 26351828 | solution.py:89
  474.4 12.1 %collective-permute-done.7 = f32[128,2048]{1,0:T(8,128)S(1)} collective-permute-done((f32[128,2048]{1,0:T(8,128)}, f32[128,2048]{1,0:T(8,128)S(1)}, u32[]{:S(2)}, u32[]{:S(2)}) %collective-permute-start.7) | collective-permute-done | bytes 1048608 | tf_op jit(solution)/shard_map/ppermute | solution.py:31
  492.4 15.5 %all-reduce.1 = f32[512]{0:T(512)S(1)} all-reduce(f32[512]{0:T(512)S(1)} %dynamic-update-slice.1), channel_id=1, replica_groups=mesh['tm'=16,'space'=8] {'space'}, use_global_device_ids=true, to_apply=%add.1 | all-reduce | flops 512 | bytes 4096
  507.8 205.5 %while.43 = (s32[]{:T(128)}, f32[512]{0:T(512)S(1)}, f32[512]{0:T(512)S(1)}, f32[512,512]{1,0:T(8,128)S(1)}, s32[]{:T(128)}) while((s32[]{:T(128)}, f32[512]{0:T(512)S(1)}, f32[512]{0:T(512)S(1)}, f32[512,512]{1,0:T(8,128)S(1)}, s32[]{:T(128)}) %tuple.126), condition=%wide.region_9.10_spmd, body=%wide.region_8.9_spmd.sunk | while | flops 3146242 | bytes 1067109 | solution.py:103
  508.8 6.2 collective-permute-start.1
  515.0 9.3 %collective-permute-done.1 = f32[512]{0:T(512)S(1)} collective-permute-done((f32[512]{0:T(512)S(1)}, f32[512]{0:T(512)S(1)}, u32[]{:S(2)}, u32[]{:S(2)}) %collective-permute-start.1) | collective-permute-done | bytes 2080 | tf_op jit(solution)/shard_map/while/body/eval_jaxpr/ppermute | solution.py:31
  543.6 5.1 collective-permute-done.1
  568.0 5.1 collective-permute-done.1
  592.3 5.1 collective-permute-done.1
  635.0 5.1 collective-permute-done.1
  659.4 5.1 collective-permute-done.1
  683.8 5.1 collective-permute-done.1
  708.2 5.1 collective-permute-done.1
  (524 shorter events, 524.5 us)
Async XLA Ops:
  23.6 7.5 %collective-permute-start.2 = (f32[1,2048]{1,0:T(1,128)S(1)}, f32[1,2048]{1,0:T(1,128)S(1)}, u32[]{:S(2)}, u32[]{:S(2)}) collective-permute-start(f32[1,2048]{1,0:T(1,128)S(1)} %get-tuple-element.382), channel_id=1, source_target_pairs={{1,0},{2,1},{3,2},{4,3},{5,4},{6,5},{7,6},{0,7},{9,8},{10,9},{11,1... | collective-permute-start | bytes 24584 | tf_op jit(solution)/shard_map/while/body/eval_jaxpr/ppermute | solution.py:23
  30.3 6.1 collective-permute-start.3
  41.9 6.2 collective-permute-start.3
  53.6 6.2 collective-permute-start.3
  65.3 6.2 collective-permute-start.3
  77.0 6.2 collective-permute-start.3
  88.7 6.2 collective-permute-start.3
  100.4 6.2 collective-permute-start.3
  112.1 6.2 collective-permute-start.3
  122.5 23.4 %collective-permute-start.6 = (f32[128,2048]{1,0:T(8,128)}, f32[128,2048]{1,0:T(8,128)S(1)}, u32[]{:S(2)}, u32[]{:S(2)}) collective-permute-start(f32[128,2048]{1,0:T(8,128)} %get-tuple-element.113), channel_id=1, source_target_pairs={{0,8},{8,16},{16,24},{24,32},{32,40},{40,48},{48,56},{56,64},{64,7... | collective-permute-start | bytes 3145736 | tf_op jit(solution)/shard_map/ppermute | solution.py:31
  168.4 7.4 %collective-permute-start = (f32[512]{0:T(512)S(1)}, f32[512]{0:T(512)S(1)}, u32[]{:S(2)}, u32[]{:S(2)}) collective-permute-start(f32[512]{0:T(512)S(1)} %bitcast.176), channel_id=1, source_target_pairs={{0,8},{8,16},{16,24},{24,32},{32,40},{40,48},{48,56},{56,64},{64,7... | collective-permute-start | bytes 6152 | tf_op jit(solution)/shard_map/while/body/eval_jaxpr/ppermute | solution.py:31
  176.8 5.1 collective-permute-start
  182.9 5.1 collective-permute-start
  189.0 5.1 collective-permute-start
  195.1 5.1 collective-permute-start
  201.2 5.1 collective-permute-start
  286.6 5.1 collective-permute-start
  311.0 5.1 collective-permute-start
  373.7 6.1 collective-permute-start.5
  386.1 6.1 collective-permute-start.5
  398.6 6.1 collective-permute-start.5
  411.1 6.1 collective-permute-start.5
  423.5 6.1 collective-permute-start.5
  436.0 6.1 collective-permute-start.5
  448.5 6.1 collective-permute-start.5
  460.9 6.1 collective-permute-start.5
  471.2 15.3 %collective-permute-start.7 = (f32[128,2048]{1,0:T(8,128)}, f32[128,2048]{1,0:T(8,128)S(1)}, u32[]{:S(2)}, u32[]{:S(2)}) collective-permute-start(f32[128,2048]{1,0:T(8,128)} %get-tuple-element.115), channel_id=1, source_target_pairs={{0,8},{8,16},{16,24},{24,32},{32,40},{40,48},{48,56},{56,64},{64,7... | collective-permute-start | bytes 3145736 | tf_op jit(solution)/shard_map/ppermute | solution.py:31
  508.8 15.5 %collective-permute-start.1 = (f32[512]{0:T(512)S(1)}, f32[512]{0:T(512)S(1)}, u32[]{:S(2)}, u32[]{:S(2)}) collective-permute-start(f32[512]{0:T(512)S(1)} %bitcast.177), channel_id=1, source_target_pairs={{0,8},{8,16},{16,24},{24,32},{32,40},{40,48},{48,56},{56,64},{64,7... | collective-permute-start | bytes 6152 | tf_op jit(solution)/shard_map/while/body/eval_jaxpr/ppermute | solution.py:31
  568.0 5.1 collective-permute-start.1
  592.3 5.1 collective-permute-start.1
  683.8 5.1 collective-permute-start.1
  708.2 5.1 collective-permute-start.1
  (96 other events, 565.7 us)
where the time goes:
time: 722 us; the launch traced here: 718 us
  waiting for transfers between devices  420 us (58%)
  local copies, waits for them, and re-layouts  70.4 us (10%)
  other arithmetic  69.9 us (10%)
  matrix products  67.1 us (9%)
  starting transfers between devices  58.2 us (8%)
  blocking collectives  31.1 us (4%)
    ppermute x66, waiting for transfers between devices, shifted(): return lax.ppermute(value, axis, pairs)  351 us
    ppermute x16, waiting for transfers between devices, extended(): before = lax.ppermute(last, axis, up)  64.2 us
    dot_general x64, matrix products, link_step(): mapped = jnp.dot(window_map, coarse_defect + carried, precision=highest)  61.2 us
    add x16, other arithmetic, advance(): return center + step_size * (diffusivity * laplace - transport + source)  50.3 us
    unnamed x2, blocking collectives  31.1 us
    ppermute x66, starting transfers between devices, shifted(): return lax.ppermute(value, axis, pairs)  28.2 us
    while x64, local copies, waits for them, and re-layouts  19.7 us
    broadcast_in_dim x48, local copies, waits for them, and re-layouts, cell_fields(): classes = jnp.repeat(class_rows, TILE, axis=1)  16.1 us
  transfers between devices with their start and end apart: 98, of which 90 were waited for; matrix products, arithmetic and copies ran while one was open for 2% of the time, Pallas kernels for 0%

commit v1 on v0

v1 whole, which is shorter than its diff:
```python
import functools

import jax
import jax.numpy as jnp
from jax import lax
from jax.experimental import pallas as pl
from jax.experimental.pallas import tpu as pltpu
from jax.sharding import PartitionSpec as P

TILE = 128
BLK = 64
STEPS = 8
ROWS = 128
COLS = 2048
COARSE = 512
HALF = COARSE // 2
TILES = COLS // TILE
EXT = ROWS + 2 * STEPS
LINES = EXT // 8
LOCAL = 64
WIDTH = COARSE + TILE
STEP = 0.6

HIGHEST = lax.Precision.HIGHEST
ANY = pl.BlockSpec(memory_space=pl.ANY)
SMEM = pl.BlockSpec(memory_space=pltpu.SMEM)
VMEM = pl.BlockSpec(memory_space=pltpu.VMEM)


def place(device):
    tm, space = divmod(device, 8)
    z_lo, rest = divmod(tm, 8)
    y, core = divmod(rest, 2)
    z_hi, x = divmod(space, 4)
    return x, y, 2 * z_hi + z_lo, core


def device_at(x, y, z, core):
    x, y, z, core = x % 4, y % 4, z % 4, core % 2
    return ((z % 2) * 8 + y * 2 + core) * 8 + (z // 2) * 4 + x


def moved(value, route):
    pairs = [(i, device_at(*route(*place(i)))) for i in range(128)]
    return lax.ppermute(value, ("tm", "space"), pairs)


def shifted(value, windows, strips=0):
    pairs = [
        (tm * 8 + sp, (tm + windows) % 16 * 8 + (sp + strips) % 8)
        for tm in range(16)
        for sp in range(8)
    ]
    return lax.ppermute(value, ("tm", "space"), pairs)


def iota(shape, axis):
    return lax.broadcasted_iota(jnp.int32, shape, axis)


def packed_means(sums):
    lane = iota((32, TILE), 1)
    row = iota((32, TILE), 0)
    low = jnp.sum(jnp.where(lane < BLK, sums, 0.0), axis=1, keepdims=True)
    high = jnp.sum(jnp.where(lane < BLK, 0.0, sums), axis=1, keepdims=True)
    slot = lane & (LOCAL - 1)
    spread = jnp.where(slot == 2 * row, low, 0.0) + jnp.where(slot == 2 * row + 1, high, 0.0)
    return jnp.sum(spread, axis=0, keepdims=True) * (1.0 / (BLK * BLK))


def means_kernel(u_ref, out_ref, sums_ref):
    for k in range(TILES):
        cols = slice(k * TILE, (k + 1) * TILE)
        for br in range(2):
            part = u_ref[br * BLK : (br + 1) * BLK, cols]
            sums_ref[br * TILES + k : br * TILES + k + 1, :] = jnp.sum(part, axis=0, keepdims=True)
    out_ref[...] = packed_means(sums_ref[...])


def block_means(u):
    return pl.pallas_call(
        means_kernel,
        out_shape=jax.ShapeDtypeStruct((1, TILE), jnp.float32),
        in_specs=[VMEM],
        out_specs=VMEM,
        scratch_shapes=[pltpu.VMEM((32, TILE), jnp.float32)],
        compiler_params=pltpu.CompilerParams(vmem_limit_bytes=16 << 20),
    )(u)


def pair_kernel(ids_ref, own_ref, other_ref, half_ref, columns_ref, late, early, sems):
    strip, core = ids_ref[0], ids_ref[1]

    def both(first, second):
        a = pltpu.make_async_copy(first, late, sems.at[0])
        b = pltpu.make_async_copy(second, early, sems.at[1])
        a.start()
        b.start()
        a.wait()
        b.wait()

    @pl.when(core == 1)
    def _():
        both(own_ref, other_ref)

    @pl.when(core == 0)
    def _():
        both(other_ref, own_ref)

    rows = late[pl.ds(pl.multiple_of(core * HALF, HALF), HALF), :]
    half_ref[...] = jnp.dot(rows, early[...], precision=HIGHEST, preferred_element_type=jnp.float32)
    pick = (iota((LOCAL, COARSE), 1) == iota((LOCAL, COARSE), 0) + strip * LOCAL).astype(jnp.float32)
    contract = (((1,), (1,)), ((), ()))
    taken = lax.dot_general(pick, early[...], contract, precision=HIGHEST, preferred_element_type=jnp.float32)
    taken = jnp.where(core == 1, pick, taken)
    columns_ref[...] = lax.dot_general(
        taken, late[...], contract, precision=HIGHEST, preferred_element_type=jnp.float32
    )


def pair_product(ids, own, other):
    return pl.pallas_call(
        pair_kernel,
        out_shape=(
            jax.ShapeDtypeStruct((HALF, COARSE), jnp.float32),
            jax.ShapeDtypeStruct((LOCAL, COARSE), jnp.float32),
        ),
        in_specs=[SMEM, ANY, ANY],
        out_specs=(VMEM, VMEM),
        scratch_shapes=[
            pltpu.VMEM((COARSE, COARSE), jnp.float32),
            pltpu.VMEM((COARSE, COARSE), jnp.float32),
            pltpu.SemaphoreType.DMA((2,)),
        ],
        compiler_params=pltpu.CompilerParams(vmem_limit_bytes=24 << 20),
    )(ids, own, other)


def fine_kernel(corrected, ids_ref, class_ref, sets_ref, *refs):
    if corrected:
        c_ref, *refs = refs
    (u_ref, up_ref, down_ref, f_ref, f_up_ref, f_down_ref) = refs[:6]
    fin_ref, means_ref = refs[6:8]
    u_ext, f_ext, first, second, force, coef, sums_ref, sems = refs[8:]
    strip = ids_ref[0]
    copies = []
    for n, (source, target, start, rows) in enumerate(
        (
            (u_ref, u_ext, STEPS, ROWS),
            (f_ref, f_ext, STEPS, ROWS),
            (up_ref, u_ext, 0, STEPS),
            (down_ref, u_ext, STEPS + ROWS, STEPS),
            (f_up_ref, f_ext, 0, STEPS),
            (f_down_ref, f_ext, STEPS + ROWS, STEPS),
        )
    ):
        for k in range(TILES):
            cols = pl.ds(k * TILE, TILE)
            copy = pltpu.make_async_copy(source.at[:, cols], target.at[k, pl.ds(start, rows)], sems.at[n, k])
            copy.start()
            copies.append(copy)

    sub = iota((8, TILE), 0)
    lane = iota((8, TILE), 1)
    strips = (lax.rem(strip + 7, 8), strip, lax.rem(strip + 1, 8))

    def weights(row, k):
        label = class_ref[row, k]
        spread, along_cols, along_rows = sets_ref[0, label], sets_ref[1, label], sets_ref[2, label]
        left = STEP * (spread + jnp.maximum(along_cols, 0.0))
        right = STEP * (spread - jnp.minimum(along_cols, 0.0))
        above = STEP * (spread + jnp.maximum(along_rows, 0.0))
        below = STEP * (spread - jnp.minimum(along_rows, 0.0))
        return 1.0 - (left + right + above + below), left, right, above, below

    for k in range(TILES):
        upper, inner, lower = (weights(row, k) for row in strips)
        for w in range(5):
            whole = jnp.full((8, TILE), inner[w], jnp.float32)
            coef[k, w] = jnp.where(sub == 0, upper[w], whole)
            coef[k, 5 + w] = whole
            coef[k, 10 + w] = jnp.where(sub == 7, lower[w], whole)

    for copy in copies:
        copy.wait()

    for k in range(TILES):
        if corrected:
            added = []
            for line in range(4):
                block_row = lax.rem(2 * strip + 15 + line, 16)
                added.append(
                    jnp.where(
                        lane < BLK,
                        c_ref[0, block_row * 32 + 2 * k],
                        c_ref[0, block_row * 32 + 2 * k + 1],
                    )
                )
        for i in range(LINES):
            value = u_ext[k, pl.ds(i, 8, stride=LINES), :]
            if corrected:
                row = sub * LINES + i
                addend = jnp.where(row < STEPS + BLK, added[1], added[2])
                addend = jnp.where(row < STEPS, added[0], addend)
                addend = jnp.where(row >= STEPS + ROWS, added[3], addend)
                value = value + addend
            first[k, pl.ds(i * 8, 8), :] = value
            force[k, pl.ds(i * 8, 8), :] = STEP * f_ext[k, pl.ds(i, 8, stride=LINES), :]

    def tile_step(old, new, k):
        before = lax.rem(k + TILES - 1, TILES)
        after = lax.rem(k + 1, TILES)
        line = [old[k, pl.ds(i * 8, 8), :] for i in range(LINES)]
        top = pltpu.roll(line[-1], 1, 0)
        bottom = pltpu.roll(line[0], 7, 0)
        for i in range(LINES):
            kind = 0 if i < STEPS else (1 if i < LINES - STEPS else 2)
            centre, w_left, w_right, w_above, w_below = (coef[k, 5 * kind + w] for w in range(5))
            rows = pl.ds(i * 8, 8)
            left = pltpu.roll(jnp.where(lane == TILE - 1, old[before, rows, :], line[i]), 1, 1)
            right = pltpu.roll(jnp.where(lane == 0, old[after, rows, :], line[i]), TILE - 1, 1)
            above = line[i - 1] if i else top
            below = line[i + 1] if i + 1 < LINES else bottom
            new[k, rows, :] = (
                (centre * line[i] + force[k, rows, :])
                + (w_left * left + w_right * right)
                + (w_above * above + w_below * below)
            )

    def two_steps(_, carry):
        def there(k, carry):
            tile_step(first, second, k)
            return carry

        def back(k, carry):
            tile_step(second, first, k)
            return carry

        lax.fori_loop(0, TILES, there, 0)
        lax.fori_loop(0, TILES, back, 0)
        return carry

    lax.fori_loop(0, STEPS // 2, two_steps, 0)

    results = []
    for k in range(TILES):
        for i in range(LINES):
            u_ext[k, pl.ds(i, 8, stride=LINES), :] = first[k, pl.ds(i * 8, 8), :]
        cols = pl.ds(k * TILE, TILE)
        result = pltpu.make_async_copy(u_ext.at[k, pl.ds(STEPS, ROWS)], fin_ref.at[:, cols], sems.at[0, k])
        result.start()
        results.append(result)
        for br in range(2):
            part = u_ext[k, STEPS + br * BLK : STEPS + (br + 1) * BLK, :]
            sums_ref[br * TILES + k : br * TILES + k + 1, :] = jnp.sum(part, axis=0, keepdims=True)
    means_ref[...] = packed_means(sums_ref[...])
    for result in results:
        result.wait()


def fine_sweep(ids, tile_class, coeff_sets, state, sources, correction=None):
    corrected = correction is not None
    field = pltpu.VMEM((TILES, EXT, TILE), jnp.float32)
    return pl.pallas_call(
        functools.partial(fine_kernel, corrected),
        out_shape=(
            jax.ShapeDtypeStruct((ROWS, COLS), jnp.float32),
            jax.ShapeDtypeStruct((1, TILE), jnp.float32),
        ),
        in_specs=[SMEM, SMEM, SMEM] + [SMEM] * corrected + [ANY] * 6,
        out_specs=(ANY, VMEM),
        scratch_shapes=[
            field,
            field,
            field,
            field,
            field,
            pltpu.VMEM((TILES, 15, 8, TILE), jnp.float32),
            pltpu.VMEM((32, TILE), jnp.float32),
            pltpu.SemaphoreType.DMA((6, TILES)),
        ],
        compiler_params=pltpu.CompilerParams(vmem_limit_bytes=32 << 20),
    )(ids, tile_class, coeff_sets, *([correction] * corrected), *state, *sources)


def message_kernel(ids_ref, means_ref, base_ref, columns_ref, out_ref):
    defect = means_ref[...] - base_ref[...]
    lane = iota((1, TILE), 1)
    pushed = jnp.dot(
        jnp.broadcast_to(defect, (8, TILE))[:, :LOCAL],
        columns_ref[...],
        precision=HIGHEST,
        preferred_element_type=jnp.float32,
    )
    odd = lax.rem(ids_ref[0], 2)
    raw = jnp.where((lane >= LOCAL) == (odd == 1), defect, 0.0)
    raw = jnp.broadcast_to(raw, (8, TILE))
    for n in range(16):
        out_ref[n * 8 : (n + 1) * 8, 0:COARSE] = pushed
        out_ref[n * 8 : (n + 1) * 8, COARSE:WIDTH] = raw


def message(ids, means, base, columns):
    return pl.pallas_call(
        message_kernel,
        out_shape=jax.ShapeDtypeStruct((128, WIDTH), jnp.float32),
        in_specs=[SMEM, VMEM, VMEM, VMEM],
        out_specs=VMEM,
        compiler_params=pltpu.CompilerParams(vmem_limit_bytes=16 << 20),
    )(ids, means, base, columns)


def chain_kernel(ids_ref, got_ref, other_ref, *refs):
    halves = refs[:16]
    out_ref = refs[16]
    maps, early, sems = refs[17:]
    strip, core, chip, y = ids_ref[0], ids_ref[1], ids_ref[2], ids_ref[3]

    def fetch(slot, which):
        mine, theirs = halves[2 * which], halves[2 * which + 1]
        for part, (source, at) in enumerate(((mine, core), (theirs, 1 - core))):
            rows = pl.ds(pl.multiple_of(at * HALF, HALF), HALF)
            pltpu.make_async_copy(source, maps.at[slot, rows], sems.at[slot, part]).start()

    def landed(slot):
        for part in range(2):
            rows = pl.ds(0, HALF)
            pltpu.make_async_copy(halves[0], maps.at[slot, rows], sems.at[slot, part]).wait()

    for ahead in range(1, 4):
        wraps = y + ahead >= 4

        @pl.when(wraps)
        def _():
            fetch(ahead, 4 + ahead)

        @pl.when(jnp.logical_not(wraps))
        def _():
            fetch(ahead, ahead)

    fetch(4, 4)
    for ahead in range(1, 4):
        wraps = y + ahead >= 4

        @pl.when(wraps)
        def _():
            fetch(4 + ahead, ahead)

        @pl.when(jnp.logical_not(wraps))
        def _():
            fetch(4 + ahead, 4 + ahead)

    fetch(0, 0)
    last = pltpu.make_async_copy(other_ref, early, sems.at[8, 0])
    last.start()

    diagonal = iota((TILE, TILE), 0) == iota((TILE, TILE), 1)

    def into_row(column):
        pieces = [
            jnp.sum(jnp.where(diagonal, column[q * TILE : (q + 1) * TILE], 0.0), axis=0, keepdims=True)
            for q in range(4)
        ]
        return jnp.concatenate(pieces, axis=1)

    def applied(matrix, vector):
        return into_row(jnp.sum(matrix * vector, axis=1, keepdims=True))

    def group(window):
        start = pl.multiple_of(lax.rem(window + 16, 16) * 8, 8)
        return jnp.sum(got_ref[pl.ds(start, 8), 0:COARSE], axis=0, keepdims=True)

    def pushed(step):
        at = 2 * lax.rem(chip + step, 8)
        return group(at - 1) + group(at)

    value = jnp.where(core == 1, group(2 * chip), pushed(0))

    def arriving(step, value):
        landed(step)
        return applied(maps[step], value) + pushed(step)

    value = lax.fori_loop(1, 8, arriving, value)
    landed(0)

    def again(step, value):
        return applied(maps[step], value) + pushed(step)

    value = lax.fori_loop(0, 8, again, value)
    last.wait()
    raw = got_ref[pl.ds(pl.multiple_of(lax.rem(2 * chip + 15, 16) * 8, 8), 8), COARSE:WIDTH]
    defect = jnp.concatenate([raw[2 * q : 2 * q + 1] + raw[2 * q + 1 : 2 * q + 2] for q in range(4)], axis=1)
    out_ref[...] = jnp.where(core == 1, applied(early[...], value + defect), value)


def chain(ids, got, other, halves):
    return pl.pallas_call(
        chain_kernel,
        out_shape=jax.ShapeDtypeStruct((1, COARSE), jnp.float32),
        in_specs=[SMEM, VMEM] + [ANY] * 17,
        out_specs=VMEM,
        scratch_shapes=[
            pltpu.VMEM((8, COARSE, COARSE), jnp.float32),
            pltpu.VMEM((COARSE, COARSE), jnp.float32),
            pltpu.SemaphoreType.DMA((9, 2)),
        ],
        compiler_params=pltpu.CompilerParams(vmem_limit_bytes=32 << 20),
    )(ids, got, other, *halves)


def finish_kernel(ids_ref, c_ref, u_ref, out_ref):
    strip = ids_ref[0]
    lane = iota((8, TILE), 1)
    for k in range(TILES):
        cols = slice(k * TILE, (k + 1) * TILE)
        for br in range(2):
            at = (2 * strip + br) * 32 + 2 * k
            added = jnp.where(lane < BLK, c_ref[0, at], c_ref[0, at + 1])
            for n in range(BLK // 8):
                rows = slice(br * BLK + n * 8, br * BLK + (n + 1) * 8)
                out_ref[rows, cols] = u_ref[rows, cols] + added


def finish(ids, correction, previous):
    return pl.pallas_call(
        finish_kernel,
        out_shape=jax.ShapeDtypeStruct((ROWS, COLS), jnp.float32),
        in_specs=[SMEM, SMEM, VMEM],
        out_specs=VMEM,
        compiler_params=pltpu.CompilerParams(vmem_limit_bytes=16 << 20),
    )(ids, correction, previous)


def exchanged(block):
    return lax.all_to_all(block, ("tm", "space"), 0, 0, tiled=True)


def swapped(value):
    return moved(value, lambda x, y, z, core: (x, y, z, 1 - core))


def across(value):
    return moved(value, lambda x, y, z, core: (x, y, z + 1 - 2 * core, core))


def per_device(initial_states, sources, tile_class, coeff_sets, coarse_maps):
    state, source, own_map = initial_states[0], sources[0], coarse_maps[0]
    window = lax.axis_index("tm").astype(jnp.int32)
    strip = lax.axis_index("space").astype(jnp.int32)
    ids = jnp.stack([strip, window % 2, window // 2, (window // 2) % 4])

    other_map = swapped(own_map)
    edges_last = jnp.concatenate([state[-STEPS:], source[-STEPS:]], axis=0)
    edges_first = jnp.concatenate([state[:STEPS], source[:STEPS]], axis=0)
    upper = shifted(edges_last, 0, 1)
    lower = shifted(edges_first, 0, -1)
    start_means = shifted(block_means(state), -1)

    half, columns = pair_product(ids, own_map, other_map)
    below = moved(half, lambda x, y, z, core: (x, y + 1, z, core))
    above = moved(half, lambda x, y, z, core: (x, y - 1, z, core))
    opposite = across(half)
    columns = shifted(columns, -1)

    source_parts = (source, upper[STEPS:], lower[STEPS:])
    finished, means = fine_sweep(
        ids, tile_class, coeff_sets, (state, upper[:STEPS], lower[:STEPS]), source_parts
    )
    previous = shifted(finished, 1)
    previous_up = shifted(finished[-STEPS:], 1, 1)
    previous_down = shifted(finished[:STEPS], 1, -1)

    second = moved(above, lambda x, y, z, core: (x, y - 1, z, core))
    far_second = moved(above, lambda x, y, z, core: (x, y - 1, z + 1 - 2 * core, core))
    far_below = across(below)
    far_above = across(above)

    got = exchanged(message(ids, means, start_means, columns))

    mine = [half, above, second, below, opposite, far_above, far_second, far_below]
    halves = []
    for part in mine:
        halves += [part, swapped(part)]
    correction = chain(ids, got, other_map, halves)

    local = lax.dynamic_slice(correction, (0, strip * LOCAL), (1, LOCAL))
    base = means + shifted(jnp.concatenate([local, local], axis=1), -1)
    finished, means = fine_sweep(
        ids, tile_class, coeff_sets, (previous, previous_up, previous_down), source_parts, correction
    )
    previous = shifted(finished, 1)
    got = exchanged(message(ids, means, base, columns))
    correction = chain(ids, got, other_map, halves)
    return finish(ids, correction, previous)[None]


def solution(mesh):
    placed = (P("tm", "space", None), P("tm", "space", None), P(), P(), P("tm", None, None))
    return jax.shard_map(
        per_device, mesh=mesh, in_specs=placed, out_specs=P("tm", "space", None), check_vma=False
    )
```

time: 722 us -> 152 us (0.21)
  waiting for transfers between devices: 420 us -> 19 us
  other arithmetic: 69.9 us -> 0.17 us
  matrix products: 67.1 us -> 0 us
  Pallas kernels: 0 us -> 54.1 us
  local copies, waits for them, and re-layouts: 70.4 us -> 20.3 us
  starting transfers between devices: 58.2 us -> 39 us
  blocking collectives: 31.1 us -> 18.5 us
    ppermute x98 -> x25, waiting for transfers between devices: 420 us -> 16.6 us  [the longest x16 9.25 us: moved(): return lax.ppermute(value, ('tm', 'space'), pairs)]
    dot_general x65 -> x0, matrix products: 67.1 us -> none  [the longest x64 61.2 us: link_step(): mapped = jnp.dot(window_map, coarse_defect + carried, precision=highest)]
    add x83 -> x1, other arithmetic: 62.4 us -> 0.01 us  [per_device(): base = means + shifted(jnp.concatenate([local, local], axis=1), -1)]
    pallas_call x0 -> x9, Pallas kernels: none -> 54.1 us  [the longest x2 37.4 us: fine_sweep(): pl.pallas_call(functools.partial(fine_kernel, corrected), out_shape=(jax....]
    unnamed x2 -> x0, blocking collectives: 31.1 us -> none
    ppermute x98 -> x25, starting transfers between devices: 58.2 us -> 33.9 us  [the longest x16 18.5 us: moved(): return lax.ppermute(value, ('tm', 'space'), pairs)]
    while x64 -> x0, local copies, waits for them, and re-layouts: 19.7 us -> none
    all_to_all x0 -> x1, blocking collectives: none -> 18.5 us  [exchanged(): return lax.all_to_all(block, ('tm', 'space'), 0, 0, tiled=True)]
  transfers between devices with their start and end apart: 98 -> 26, of which waited for: 90 -> 7; matrix products, arithmetic and copies ran while one was open for 2% -> 4% of each run, Pallas kernels for 0% -> 19%
where the time goes in v1:
time: 152 us; the launch traced here: 151 us
  Pallas kernels  54.1 us (36%)
  starting transfers between devices  39 us (26%)
  local copies, waits for them, and re-layouts  20.3 us (13%)
  waiting for transfers between devices  19 us (12%)
  blocking collectives  18.5 us (12%)
    pallas_call x2, Pallas kernels, fine_sweep(): pl.pallas_call(functools.partial(fine_kernel, corrected), out_shape=(jax....  37.4 us
    ppermute x16, starting transfers between devices, moved(): return lax.ppermute(value, ('tm', 'space'), pairs)  18.5 us
    all_to_all x1, blocking collectives, exchanged(): return lax.all_to_all(block, ('tm', 'space'), 0, 0, tiled=True)  18.5 us
    unnamed x56, local copies, waits for them, and re-layouts  15.5 us
    ppermute x9, starting transfers between devices, shifted(): return lax.ppermute(value, ('tm', 'space'), pairs)  15.4 us
    ppermute x16, waiting for transfers between devices, moved(): return lax.ppermute(value, ('tm', 'space'), pairs)  9.25 us
    pallas_call x2, Pallas kernels, chain(): pl.pallas_call(chain_kernel, out_shape=jax.ShapeDtypeStruct((1, COARSE),...  9.12 us
    ppermute x9, waiting for transfers between devices, shifted(): return lax.ppermute(value, ('tm', 'space'), pairs)  7.31 us
  transfers between devices with their start and end apart: 26, of which 7 were waited for; matrix products, arithmetic and copies ran while one was open for 4% of the time, Pallas kernels for 19%

profile of v1, /device:TPU:1, one launch (start us, length us, event | category | flops | bytes accessed | tf_op | source)
XLA Modules:
  0.0 151.5 jit_solution(6104795771887153138)
XLA Ops:
  0.0 1.4 collective-permute-start.3
  3.9 1.2 copy-done.20
  5.1 3.7 %shard_map.57 = (f32[256,512]{1,0:T(8,128)S(1)}, f32[64,512]{1,0:T(8,128)S(1)}) custom-call(s32[4]{0:T(128)S(1)} %pad_add_fusion.ids_ref, f32[512,512]{1,0:T(8,128)S(1)} %bitcast.33, f32[512,512]{1,0:T(8,128)S(1)} %collective-permute-done.3.other_ref), custom_call_target="tpu_custom_call" | custom-call | tf_op jit(solution)/shard_map/pallas_call | solution.py:122
  8.8 3.9 %collective-permute-start.12 = (f32[256,512]{1,0:T(8,128)S(1)}, f32[256,512]{1,0:T(8,128)S(1)}, u32[]{:S(2)}, u32[]{:S(2)}) collective-permute-start(f32[256,512]{1,0:T(8,128)S(1)} %get-tuple-element.13.refs_0_), channel_id=1, source_target_pairs={{0,64},{1,65},{2,66},{3,67},{4,68},{5,69},{6,70},{7,71},{8,76},{9,... | collective-permute-start | bytes 1572872 | tf_op jit(solution)/shard_map/ppermute | solution.py:45
  12.7 1.3 collective-permute-start.10
  14.1 1.3 collective-permute-start
  15.3 3.9 %collective-permute-start.1 = (f32[16,2048]{1,0:T(8,128)S(1)}, f32[16,2048]{1,0:T(8,128)S(1)}, u32[]{:S(2)}, u32[]{:S(2)}) collective-permute-start(f32[16,2048]{1,0:T(8,128)S(1)} %pad_maximum_fusion.1), channel_id=1, source_target_pairs={{0,7},{1,0},{2,1},{3,2},{4,3},{5,4},{6,5},{7,6},{8,15},{9,8},{10,9... | collective-permute-start | bytes 393224 | tf_op jit(solution)/shard_map/ppermute | solution.py:54
  19.5 3.2 %collective-permute-done.2.base_ref = f32[1,128]{1,0:T(1,128)S(1)} collective-permute-done((f32[1,128]{1,0:T(1,128)S(1)}, f32[1,128]{1,0:T(1,128)S(1)}, u32[]{:S(2)}, u32[]{:S(2)}) %collective-permute-start.2) | collective-permute-done | bytes 544 | tf_op jit(solution)/shard_map/ppermute | solution.py:54
  22.8 3.3 %collective-permute-start.6 = (f32[256,512]{1,0:T(8,128)S(1)}, f32[256,512]{1,0:T(8,128)S(1)}, u32[]{:S(2)}, u32[]{:S(2)}) collective-permute-start(f32[256,512]{1,0:T(8,128)S(1)} %get-tuple-element.13.refs_0_), channel_id=1, source_target_pairs={{0,48},{1,49},{2,50},{3,51},{4,52},{5,53},{6,54},{7,55},{8,56},{9,... | collective-permute-start | bytes 1572872 | tf_op jit(solution)/shard_map/ppermute | solution.py:45
  27.4 1.1 collective-permute-done.4.columns_ref
  29.0 8.3 %collective-permute-done.6.refs_2_ = f32[256,512]{1,0:T(8,128)S(1)} collective-permute-done((f32[256,512]{1,0:T(8,128)S(1)}, f32[256,512]{1,0:T(8,128)S(1)}, u32[]{:S(2)}, u32[]{:S(2)}) %collective-permute-start.6) | collective-permute-done | bytes 524320 | tf_op jit(solution)/shard_map/ppermute | solution.py:45
  37.3 3.2 %collective-permute-start.16 = (f32[256,512]{1,0:T(8,128)S(1)}, f32[256,512]{1,0:T(8,128)}, u32[]{:S(2)}, u32[]{:S(2)}) collective-permute-start(f32[256,512]{1,0:T(8,128)S(1)} %collective-permute-done.6.refs_2_), channel_id=1, source_target_pairs={{0,112},{1,113},{2,114},{3,115},{4,116},{5,117},{6,118},{7,119},{8... | collective-permute-start | bytes 1572872 | tf_op jit(solution)/shard_map/ppermute | solution.py:45
  42.5 2.5 %collective-permute-start.7 = (f32[256,512]{1,0:T(8,128)S(1)}, f32[256,512]{1,0:T(8,128)S(1)}, u32[]{:S(2)}, u32[]{:S(2)}) collective-permute-start(f32[256,512]{1,0:T(8,128)S(1)} %collective-permute-done.6.refs_2_), channel_id=1, source_target_pairs={{0,8},{1,9},{2,10},{3,11},{4,12},{5,13},{6,14},{7,15},{8,0},{9,1},... | collective-permute-start | bytes 1572872 | tf_op jit(solution)/shard_map/ppermute | solution.py:45
  45.7 18.5 %shard_map.55 = (f32[128,2048]{1,0:T(8,128)}, f32[1,128]{1,0:T(1,128)S(1)}) custom-call(s32[4]{0:T(128)S(1)} %pad_add_fusion.ids_ref, s32[8,16]{1,0:T(8,128)S(1)} %copy-done.21, f32[3,8]{1,0:T(4,128)S(1)} %copy-done.22, f32[128,2048]{1,0:T(8,128)S(1)} %bitcast.25, f32[8,2048]{1,0:T(8,128)S(1)} %get-tuple-element.26.refs_1_, ...), custom_call_target="tpu_custom_call" | custom-call | tf_op jit(solution)/shard_map/pallas_call | solution.py:264
  65.1 1.6 %collective-permute-start.20 = (f32[128,2048]{1,0:T(8,128)}, f32[128,2048]{1,0:T(8,128)}, u32[]{:S(2)}, u32[]{:S(2)}) collective-permute-start(f32[128,2048]{1,0:T(8,128)} %get-tuple-element.14), channel_id=1, source_target_pairs={{0,8},{1,9},{2,10},{3,11},{4,12},{5,13},{6,14},{7,15},{8,16},{9,17... | collective-permute-start | bytes 3145736 | tf_op jit(solution)/shard_map/ppermute | solution.py:54
  70.0 1.1 copy.6
  71.0 5.1 %all-to-all-start = ((f32[128,1,640]{2,1,0:T(1,128)}), f32[128,1,640]{2,1,0:T(1,128)}, u32[]{:S(2)}, u32[]{:S(2)}) async-start(f32[128,1,640]{2,1,0:T(1,128)} %copy.6), calls=%async_computation | async-start | bytes 655360 | tf_op jit(solution)/shard_map/all_to_all | solution.py:435
  76.2 1.5 %fusion = (f32[8,2048]{1,0:T(8,128)}, f32[8,2048]{1,0:T(8,128)}) fusion(f32[128,2048]{1,0:T(8,128)} %get-tuple-element.14), kind=kLoop, calls=%fused_computation.11 | loop fusion | bytes 262144 | tf_op jit(solution)/shard_map/slice | solution.py:471
  77.7 6.7 %collective-permute-start.22 = (f32[8,2048]{1,0:T(8,128)}, f32[8,2048]{1,0:T(8,128)S(1)}, u32[]{:S(2)}, u32[]{:S(2)}) collective-permute-start(f32[8,2048]{1,0:T(8,128)} %get-tuple-element.17), channel_id=1, source_target_pairs={{0,15},{1,8},{2,9},{3,10},{4,11},{5,12},{6,13},{7,14},{8,23},{9,16... | collective-permute-start | bytes 196616 | tf_op jit(solution)/shard_map/ppermute | solution.py:54
  84.4 2.5 %all-to-all-done = f32[128,1,640]{2,1,0:T(1,128)} async-done(((f32[128,1,640]{2,1,0:T(1,128)}), f32[128,1,640]{2,1,0:T(1,128)}, u32[]{:S(2)}, u32[]{:S(2)}) %all-to-all-start) | async-done | bytes 327712 | tf_op jit(solution)/shard_map/all_to_all | solution.py:435
  86.9 1.1 copy.13
  88.0 1.0 copy-done.6
  89.1 1.0 copy-done.9
  90.1 1.0 copy-done.12
  91.1 1.0 copy-done.15
  93.2 4.6 %shard_map.59.refs_0_ = f32[1,512]{1,0:T(1,128)S(1)} custom-call(s32[4]{0:T(128)S(1)} %pad_add_fusion.ids_ref, f32[128,640]{1,0:T(8,128)S(1)} %bitcast.29, f32[512,512]{1,0:T(8,128)S(1)} %collective-permute-done.3.other_ref, f32[256,512]{1,0:T(8,128)S(1)} %get-tuple-element.13.refs_0_, f32[256,512]{1,0:T(8,128)S(1)} %copy-done.9, f32[256,512]{1,0:T(8,128)S(1)} %copy-done.6, ...), custom_call_target="tpu_custom_call" | custom-call | tf_op jit(solution)/shard_map/pallas_call | solution.py:397
  97.8 18.8 %shard_map.60 = (f32[128,2048]{1,0:T(8,128)}, f32[1,128]{1,0:T(1,128)S(1)}) custom-call(s32[4]{0:T(128)S(1)} %pad_add_fusion.ids_ref, s32[8,16]{1,0:T(8,128)S(1)} %copy-done.21, f32[3,8]{1,0:T(4,128)S(1)} %copy-done.22, f32[1,512]{1,0:T(1,128)S(1)} %shard_map.59.refs_0_, f32[128,2048]{1,0:T(8,128)} %collective-permute-done.20.refs_1_, ...), custom_call_target="tpu_custom_call" | custom-call | tf_op jit(solution)/shard_map/pallas_call | solution.py:264
  117.2 1.8 %collective-permute-start.24 = (f32[128,2048]{1,0:T(8,128)}, f32[128,2048]{1,0:T(8,128)}, u32[]{:S(2)}, u32[]{:S(2)}) collective-permute-start(f32[128,2048]{1,0:T(8,128)} %get-tuple-element.16), channel_id=1, source_target_pairs={{0,8},{1,9},{2,10},{3,11},{4,12},{5,13},{6,14},{7,15},{8,16},{9,17... | collective-permute-start | bytes 3145736 | tf_op jit(solution)/shard_map/ppermute | solution.py:54
  119.2 3.0 %collective-permute-done.23 = f32[1,128]{1,0:T(1,128)S(1)} collective-permute-done((f32[1,128]{1,0:T(1,128)S(1)}, f32[1,128]{1,0:T(1,128)S(1)}, u32[]{:S(2)}, u32[]{:S(2)}) %collective-permute-start.23) | collective-permute-done | bytes 544 | tf_op jit(solution)/shard_map/ppermute | solution.py:54
  124.0 18.5 %all_to_all.22 = f32[128,1,640]{2,1,0:T(1,128)S(1)} all-to-all(f32[128,1,640]{2,1,0:T(1,128)S(1)} %copy.7), channel_id=1, replica_groups=mesh['tm'=16,'space'=8] {'tm','space'}, dimensions={0} | all-to-all | bytes 655360 | tf_op jit(solution)/shard_map/all_to_all | solution.py:435
  144.6 4.6 %shard_map.62.c_ref = f32[1,512]{1,0:T(1,128)S(1)} custom-call(s32[4]{0:T(128)S(1)} %pad_add_fusion.ids_ref, f32[128,640]{1,0:T(8,128)S(1)} %bitcast.28, f32[512,512]{1,0:T(8,128)S(1)} %collective-permute-done.3.other_ref, f32[256,512]{1,0:T(8,128)S(1)} %get-tuple-element.13.refs_0_, f32[256,512]{1,0:T(8,128)S(1)} %copy-done.10, f32[256,512]{1,0:T(8,128)S(1)} %copy-done.7, ...), custom_call_target="tpu_custom_call" | custom-call | tf_op jit(solution)/shard_map/pallas_call | solution.py:397
  149.1 2.3 %shard_map.63 = f32[128,2048]{1,0:T(8,128)} custom-call(s32[4]{0:T(128)S(1)} %pad_add_fusion.ids_ref, f32[1,512]{1,0:T(1,128)S(1)} %shard_map.62.c_ref, f32[128,2048]{1,0:T(8,128)} %collective-permute-done.24.u_ref), custom_call_target="tpu_custom_call" | custom-call | tf_op jit(solution)/shard_map/pallas_call | solution.py:425
  (99 shorter events, 17.0 us)
Async XLA Ops:
  0.0 3.9 %collective-permute-start.3 = (f32[512,512]{1,0:T(8,128)}, f32[512,512]{1,0:T(8,128)S(1)}, u32[]{:S(2)}, u32[]{:S(2)}) collective-permute-start(f32[512,512]{1,0:T(8,128)} %bitcast.32), channel_id=1, source_target_pairs={{0,8},{1,9},{2,10},{3,11},{4,12},{5,13},{6,14},{7,15},{8,0},{9,1},... | collective-permute-start | bytes 3145736 | tf_op jit(solution)/shard_map/ppermute | solution.py:45
  8.8 19.7 %collective-permute-start.12 = (f32[256,512]{1,0:T(8,128)S(1)}, f32[256,512]{1,0:T(8,128)S(1)}, u32[]{:S(2)}, u32[]{:S(2)}) collective-permute-start(f32[256,512]{1,0:T(8,128)S(1)} %get-tuple-element.13.refs_0_), channel_id=1, source_target_pairs={{0,64},{1,65},{2,66},{3,67},{4,68},{5,69},{6,70},{7,71},{8,76},{9,... | collective-permute-start | bytes 1572872 | tf_op jit(solution)/shard_map/ppermute | solution.py:45
  12.7 13.9 %collective-permute-start.10 = (f32[256,512]{1,0:T(8,128)S(1)}, f32[256,512]{1,0:T(8,128)S(1)}, u32[]{:S(2)}, u32[]{:S(2)}) collective-permute-start(f32[256,512]{1,0:T(8,128)S(1)} %get-tuple-element.13.refs_0_), channel_id=1, source_target_pairs={{0,16},{1,17},{2,18},{3,19},{4,20},{5,21},{6,22},{7,23},{8,24},{9,... | collective-permute-start | bytes 1572872 | tf_op jit(solution)/shard_map/ppermute | solution.py:45
  14.0 31.0 %copy-start.1 = (f32[1,128,2048]{2,1,0:T(8,128)S(1)}, f32[1,128,2048]{2,1,0:T(8,128)}, u32[]{:S(2)}) copy-start(f32[1,128,2048]{2,1,0:T(8,128)} %param.6) | copy-start | bytes 3145732
  14.1 8.7 %collective-permute-start = (f32[16,2048]{1,0:T(8,128)S(1)}, f32[16,2048]{1,0:T(8,128)S(1)}, u32[]{:S(2)}, u32[]{:S(2)}) collective-permute-start(f32[16,2048]{1,0:T(8,128)S(1)} %pad_maximum_fusion), channel_id=1, source_target_pairs={{0,1},{1,2},{2,3},{3,4},{4,5},{5,6},{6,7},{7,0},{8,9},{9,10},{10,1... | collective-permute-start | bytes 393224 | tf_op jit(solution)/shard_map/ppermute | solution.py:54
  15.3 10.7 %collective-permute-start.1 = (f32[16,2048]{1,0:T(8,128)S(1)}, f32[16,2048]{1,0:T(8,128)S(1)}, u32[]{:S(2)}, u32[]{:S(2)}) collective-permute-start(f32[16,2048]{1,0:T(8,128)S(1)} %pad_maximum_fusion.1), channel_id=1, source_target_pairs={{0,7},{1,0},{2,1},{3,2},{4,3},{5,4},{6,5},{7,6},{8,15},{9,8},{10,9... | collective-permute-start | bytes 393224 | tf_op jit(solution)/shard_map/ppermute | solution.py:54
  19.5 3.3 %collective-permute-start.2 = (f32[1,128]{1,0:T(1,128)S(1)}, f32[1,128]{1,0:T(1,128)S(1)}, u32[]{:S(2)}, u32[]{:S(2)}) collective-permute-start(f32[1,128]{1,0:T(1,128)S(1)} %shard_map.56), channel_id=1, source_target_pairs={{0,120},{1,121},{2,122},{3,123},{4,124},{5,125},{6,126},{7,127},{8... | collective-permute-start | bytes 1544 | tf_op jit(solution)/shard_map/ppermute | solution.py:54
  22.8 5.7 %collective-permute-start.4 = (f32[64,512]{1,0:T(8,128)S(1)}, f32[64,512]{1,0:T(8,128)S(1)}, u32[]{:S(2)}, u32[]{:S(2)}) collective-permute-start(f32[64,512]{1,0:T(8,128)S(1)} %get-tuple-element.12), channel_id=1, source_target_pairs={{0,120},{1,121},{2,122},{3,123},{4,124},{5,125},{6,126},{7,127},{8... | collective-permute-start | bytes 393224 | tf_op jit(solution)/shard_map/ppermute | solution.py:54
  22.8 14.6 %collective-permute-start.6 = (f32[256,512]{1,0:T(8,128)S(1)}, f32[256,512]{1,0:T(8,128)S(1)}, u32[]{:S(2)}, u32[]{:S(2)}) collective-permute-start(f32[256,512]{1,0:T(8,128)S(1)} %get-tuple-element.13.refs_0_), channel_id=1, source_target_pairs={{0,48},{1,49},{2,50},{3,51},{4,52},{5,53},{6,54},{7,55},{8,56},{9,... | collective-permute-start | bytes 1572872 | tf_op jit(solution)/shard_map/ppermute | solution.py:45
  26.0 14.5 %collective-permute-start.5 = (f32[256,512]{1,0:T(8,128)S(1)}, f32[256,512]{1,0:T(8,128)S(1)}, u32[]{:S(2)}, u32[]{:S(2)}) collective-permute-start(f32[256,512]{1,0:T(8,128)S(1)} %get-tuple-element.13.refs_0_), channel_id=1, source_target_pairs={{0,8},{1,9},{2,10},{3,11},{4,12},{5,13},{6,14},{7,15},{8,0},{9,1},... | collective-permute-start | bytes 1572872 | tf_op jit(solution)/shard_map/ppermute | solution.py:45
  26.6 37.6 %copy-start.2 = (f32[256,512]{1,0:T(8,128)}, f32[256,512]{1,0:T(8,128)S(1)}, u32[]{:S(2)}) copy-start(f32[256,512]{1,0:T(8,128)S(1)} %collective-permute-done.10.refs_6_) | copy-start | bytes 1572868
  26.6 15.9 %collective-permute-start.18 = (f32[256,512]{1,0:T(8,128)S(1)}, f32[256,512]{1,0:T(8,128)}, u32[]{:S(2)}, u32[]{:S(2)}) collective-permute-start(f32[256,512]{1,0:T(8,128)S(1)} %collective-permute-done.10.refs_6_), channel_id=1, source_target_pairs={{0,64},{1,65},{2,66},{3,67},{4,68},{5,69},{6,70},{7,71},{8,76},{9,... | collective-permute-start | bytes 1572872 | tf_op jit(solution)/shard_map/ppermute | solution.py:45
  28.5 35.8 %collective-permute-start.11 = (f32[256,512]{1,0:T(8,128)S(1)}, f32[256,512]{1,0:T(8,128)S(1)}, u32[]{:S(2)}, u32[]{:S(2)}) collective-permute-start(f32[256,512]{1,0:T(8,128)S(1)} %collective-permute-done.10.refs_6_), channel_id=1, source_target_pairs={{0,8},{1,9},{2,10},{3,11},{4,12},{5,13},{6,14},{7,15},{8,0},{9,1},... | collective-permute-start | bytes 1572872 | tf_op jit(solution)/shard_map/ppermute | solution.py:45
  28.5 12.9 %collective-permute-start.13 = (f32[256,512]{1,0:T(8,128)S(1)}, f32[256,512]{1,0:T(8,128)S(1)}, u32[]{:S(2)}, u32[]{:S(2)}) collective-permute-start(f32[256,512]{1,0:T(8,128)S(1)} %collective-permute-done.12.refs_8_), channel_id=1, source_target_pairs={{0,8},{1,9},{2,10},{3,11},{4,12},{5,13},{6,14},{7,15},{8,0},{9,1},... | collective-permute-start | bytes 1572872 | tf_op jit(solution)/shard_map/ppermute | solution.py:45
  37.3 26.9 %copy-start.5 = (f32[256,512]{1,0:T(8,128)}, f32[256,512]{1,0:T(8,128)S(1)}, u32[]{:S(2)}) copy-start(f32[256,512]{1,0:T(8,128)S(1)} %collective-permute-done.6.refs_2_) | copy-start | bytes 1572868
  37.3 29.4 %collective-permute-start.16 = (f32[256,512]{1,0:T(8,128)S(1)}, f32[256,512]{1,0:T(8,128)}, u32[]{:S(2)}, u32[]{:S(2)}) collective-permute-start(f32[256,512]{1,0:T(8,128)S(1)} %collective-permute-done.6.refs_2_), channel_id=1, source_target_pairs={{0,112},{1,113},{2,114},{3,115},{4,116},{5,117},{6,118},{7,119},{8... | collective-permute-start | bytes 1572872 | tf_op jit(solution)/shard_map/ppermute | solution.py:45
  41.3 25.4 %collective-permute-start.14 = (f32[256,512]{1,0:T(8,128)S(1)}, f32[256,512]{1,0:T(8,128)}, u32[]{:S(2)}, u32[]{:S(2)}) collective-permute-start(f32[256,512]{1,0:T(8,128)S(1)} %collective-permute-done.6.refs_2_), channel_id=1, source_target_pairs={{0,64},{1,65},{2,66},{3,67},{4,68},{5,69},{6,70},{7,71},{8,76},{9,... | collective-permute-start | bytes 1572872 | tf_op jit(solution)/shard_map/ppermute | solution.py:45
  42.2 25.1 %collective-permute-start.8 = (f32[256,512]{1,0:T(8,128)S(1)}, f32[256,512]{1,0:T(8,128)}, u32[]{:S(2)}, u32[]{:S(2)}) collective-permute-start(f32[256,512]{1,0:T(8,128)S(1)} %collective-permute-done.6.refs_2_), channel_id=1, source_target_pairs={{0,48},{1,49},{2,50},{3,51},{4,52},{5,53},{6,54},{7,55},{8,56},{9,... | collective-permute-start | bytes 1572872 | tf_op jit(solution)/shard_map/ppermute | solution.py:45
  42.5 24.9 %collective-permute-start.7 = (f32[256,512]{1,0:T(8,128)S(1)}, f32[256,512]{1,0:T(8,128)S(1)}, u32[]{:S(2)}, u32[]{:S(2)}) collective-permute-start(f32[256,512]{1,0:T(8,128)S(1)} %collective-permute-done.6.refs_2_), channel_id=1, source_target_pairs={{0,8},{1,9},{2,10},{3,11},{4,12},{5,13},{6,14},{7,15},{8,0},{9,1},... | collective-permute-start | bytes 1572872 | tf_op jit(solution)/shard_map/ppermute | solution.py:45
  65.1 32.7 %collective-permute-start.20 = (f32[128,2048]{1,0:T(8,128)}, f32[128,2048]{1,0:T(8,128)}, u32[]{:S(2)}, u32[]{:S(2)}) collective-permute-start(f32[128,2048]{1,0:T(8,128)} %get-tuple-element.14), channel_id=1, source_target_pairs={{0,8},{1,9},{2,10},{3,11},{4,12},{5,13},{6,14},{7,15},{8,16},{9,17... | collective-permute-start | bytes 3145736 | tf_op jit(solution)/shard_map/ppermute | solution.py:54
  66.8 11.0 %collective-permute-start.19 = (f32[256,512]{1,0:T(8,128)}, f32[256,512]{1,0:T(8,128)}, u32[]{:S(2)}, u32[]{:S(2)}) collective-permute-start(f32[256,512]{1,0:T(8,128)} %collective-permute-done.18.refs_14_), channel_id=1, source_target_pairs={{0,8},{1,9},{2,10},{3,11},{4,12},{5,13},{6,14},{7,15},{8,0},{9,1},... | collective-permute-start | bytes 1572872 | tf_op jit(solution)/shard_map/ppermute | solution.py:45
  66.8 17.6 %collective-permute-start.17 = (f32[256,512]{1,0:T(8,128)}, f32[256,512]{1,0:T(8,128)}, u32[]{:S(2)}, u32[]{:S(2)}) collective-permute-start(f32[256,512]{1,0:T(8,128)} %collective-permute-done.16.refs_12_), channel_id=1, source_target_pairs={{0,8},{1,9},{2,10},{3,11},{4,12},{5,13},{6,14},{7,15},{8,0},{9,1},... | collective-permute-start | bytes 1572872 | tf_op jit(solution)/shard_map/ppermute | solution.py:45
  67.3 20.7 %collective-permute-start.15 = (f32[256,512]{1,0:T(8,128)}, f32[256,512]{1,0:T(8,128)}, u32[]{:S(2)}, u32[]{:S(2)}) collective-permute-start(f32[256,512]{1,0:T(8,128)} %collective-permute-done.14.refs_10_), channel_id=1, source_target_pairs={{0,8},{1,9},{2,10},{3,11},{4,12},{5,13},{6,14},{7,15},{8,0},{9,1},... | collective-permute-start | bytes 1572872 | tf_op jit(solution)/shard_map/ppermute | solution.py:45
  68.2 19.7 %collective-permute-start.9 = (f32[256,512]{1,0:T(8,128)}, f32[256,512]{1,0:T(8,128)}, u32[]{:S(2)}, u32[]{:S(2)}) collective-permute-start(f32[256,512]{1,0:T(8,128)} %collective-permute-done.8.refs_4_), channel_id=1, source_target_pairs={{0,8},{1,9},{2,10},{3,11},{4,12},{5,13},{6,14},{7,15},{8,0},{9,1},... | collective-permute-start | bytes 1572872 | tf_op jit(solution)/shard_map/ppermute | solution.py:45
  71.0 15.8 %all-to-all-start = ((f32[128,1,640]{2,1,0:T(1,128)}), f32[128,1,640]{2,1,0:T(1,128)}, u32[]{:S(2)}, u32[]{:S(2)}) async-start(f32[128,1,640]{2,1,0:T(1,128)} %copy.6), calls=%async_computation | async-start | bytes 655360 | tf_op jit(solution)/shard_map/all_to_all | solution.py:435
  77.7 20.1 %collective-permute-start.22 = (f32[8,2048]{1,0:T(8,128)}, f32[8,2048]{1,0:T(8,128)S(1)}, u32[]{:S(2)}, u32[]{:S(2)}) collective-permute-start(f32[8,2048]{1,0:T(8,128)} %get-tuple-element.17), channel_id=1, source_target_pairs={{0,15},{1,8},{2,9},{3,10},{4,11},{5,12},{6,13},{7,14},{8,23},{9,16... | collective-permute-start | bytes 196616 | tf_op jit(solution)/shard_map/ppermute | solution.py:54
  84.4 13.4 %collective-permute-start.21 = (f32[8,2048]{1,0:T(8,128)}, f32[8,2048]{1,0:T(8,128)S(1)}, u32[]{:S(2)}, u32[]{:S(2)}) collective-permute-start(f32[8,2048]{1,0:T(8,128)} %get-tuple-element.18), channel_id=1, source_target_pairs={{0,9},{1,10},{2,11},{3,12},{4,13},{5,14},{6,15},{7,8},{8,17},{9,18... | collective-permute-start | bytes 196616 | tf_op jit(solution)/shard_map/ppermute | solution.py:54
  117.2 31.9 %collective-permute-start.24 = (f32[128,2048]{1,0:T(8,128)}, f32[128,2048]{1,0:T(8,128)}, u32[]{:S(2)}, u32[]{:S(2)}) collective-permute-start(f32[128,2048]{1,0:T(8,128)} %get-tuple-element.16), channel_id=1, source_target_pairs={{0,8},{1,9},{2,10},{3,11},{4,12},{5,13},{6,14},{7,15},{8,16},{9,17... | collective-permute-start | bytes 3145736 | tf_op jit(solution)/shard_map/ppermute | solution.py:54
  119.2 3.0 %collective-permute-start.23 = (f32[1,128]{1,0:T(1,128)S(1)}, f32[1,128]{1,0:T(1,128)S(1)}, u32[]{:S(2)}, u32[]{:S(2)}) collective-permute-start(f32[1,128]{1,0:T(1,128)S(1)} %pad_maximum_fusion.2), channel_id=1, source_target_pairs={{0,120},{1,121},{2,122},{3,123},{4,124},{5,125},{6,126},{7,127},{8... | collective-permute-start | bytes 1544 | tf_op jit(solution)/shard_map/ppermute | solution.py:54
  122.8 19.6 %copy-start.13 = (f32[256,512]{1,0:T(8,128)S(1)}, f32[256,512]{1,0:T(8,128)}, u32[]{:S(2)}) copy-start(f32[256,512]{1,0:T(8,128)} %copy-done.11) | copy-start | bytes 1572868
  123.6 18.9 %copy-start.10 = (f32[256,512]{1,0:T(8,128)S(1)}, f32[256,512]{1,0:T(8,128)}, u32[]{:S(2)}) copy-start(f32[256,512]{1,0:T(8,128)} %copy-done.8) | copy-start | bytes 1572868
  123.9 18.5 %copy-start.4 = (f32[256,512]{1,0:T(8,128)S(1)}, f32[256,512]{1,0:T(8,128)}, u32[]{:S(2)}) copy-start(f32[256,512]{1,0:T(8,128)} %copy-done.2) | copy-start | bytes 1572868
  (21 other events, 53.8 us)

commit v2 on v1

v2 whole, which is shorter than its diff:
```python
import functools

import jax
import jax.numpy as jnp
from jax import lax
from jax.experimental import pallas as pl
from jax.experimental.pallas import tpu as pltpu
from jax.sharding import PartitionSpec as P

TILE = 128
BLK = 64
STEPS = 8
ROWS = 128
COLS = 2048
COARSE = 512
HALF = COARSE // 2
TILES = COLS // TILE
LOCAL = 64
PIECES = 5
STEP = 0.6

HIGHEST = lax.Precision.HIGHEST
HBM = pl.BlockSpec(memory_space=pltpu.HBM)
SMEM = pl.BlockSpec(memory_space=pltpu.SMEM)
VMEM = pl.BlockSpec(memory_space=pltpu.VMEM)


def place(device):
    tm, space = divmod(device, 8)
    z_lo, rest = divmod(tm, 8)
    y, core = divmod(rest, 2)
    z_hi, x = divmod(space, 4)
    return x, y, 2 * z_hi + z_lo, core


def device_at(x, y, z, core):
    x, y, z, core = x % 4, y % 4, z % 4, core % 2
    return ((z % 2) * 8 + y * 2 + core) * 8 + (z // 2) * 4 + x


def moved(value, route):
    pairs = [(i, device_at(*route(*place(i)))) for i in range(128)]
    return lax.ppermute(value, ("tm", "space"), pairs)


def shifted(value, windows, strips=0):
    pairs = [
        (tm * 8 + sp, (tm + windows) % 16 * 8 + (sp + strips) % 8)
        for tm in range(16)
        for sp in range(8)
    ]
    return lax.ppermute(value, ("tm", "space"), pairs)


def iota(shape, axis):
    return lax.broadcasted_iota(jnp.int32, shape, axis)


def packed_means(sums):
    lane = iota((32, TILE), 1)
    row = iota((32, TILE), 0)
    low = jnp.sum(jnp.where(lane < BLK, sums, 0.0), axis=1, keepdims=True)
    high = jnp.sum(jnp.where(lane < BLK, 0.0, sums), axis=1, keepdims=True)
    slot = lane & (LOCAL - 1)
    spread = jnp.where(slot == 2 * row, low, 0.0) + jnp.where(slot == 2 * row + 1, high, 0.0)
    return jnp.sum(spread, axis=0, keepdims=True) * (1.0 / (BLK * BLK))


def pair_kernel(ids_ref, own_ref, other_ref, u_ref, q_ref, half_ref, columns_ref, late, early, u, sums_ref, sems):
    strip, core = ids_ref[0], ids_ref[1]
    state = pltpu.make_async_copy(u_ref, u, sems.at[2])

    def both(first, second):
        a = pltpu.make_async_copy(first, late, sems.at[0])
        b = pltpu.make_async_copy(second, early, sems.at[1])
        a.start()
        b.start()
        state.start()
        a.wait()
        b.wait()

    @pl.when(core == 1)
    def _():
        both(own_ref, other_ref)

    @pl.when(core == 0)
    def _():
        both(other_ref, own_ref)

    def split(value):
        big = value.astype(jnp.bfloat16)
        return big, (value - big.astype(jnp.float32)).astype(jnp.bfloat16)

    def times(a, b):
        return jnp.dot(a, b, preferred_element_type=jnp.float32)

    early_big, early_small = split(early[...])
    for part in range(2):
        rows = slice(part * HALF, (part + 1) * HALF)
        big, small = split(late[rows, :])
        q_ref[rows, :] = times(big, early_big) + (times(big, early_small) + times(small, early_big))
    half_ref[...] = q_ref[pl.ds(pl.multiple_of(core * HALF, HALF), HALF), :]
    cols = pl.ds(pl.multiple_of(strip // 2 * TILE, TILE), TILE)
    wide = jnp.where(core == 1, late[:, cols], q_ref[:, cols])
    turned = jnp.transpose(wide)
    columns_ref[0:LOCAL, :] = jnp.where(lax.rem(strip, 2) == 1, turned[LOCAL:], turned[:LOCAL])
    state.wait()
    for k in range(TILES):
        cols = slice(k * TILE, (k + 1) * TILE)
        for br in range(2):
            part = u[br * BLK : (br + 1) * BLK, cols]
            sums_ref[br * TILES + k : br * TILES + k + 1, :] = jnp.sum(part, axis=0, keepdims=True)
    columns_ref[LOCAL:, :] = jnp.zeros((8, COARSE), jnp.float32)
    columns_ref[LOCAL:, 0:TILE] = jnp.broadcast_to(packed_means(sums_ref[...]), (8, TILE))


def pair_product(ids, own, other, state):
    square = pltpu.VMEM((COARSE, COARSE), jnp.float32)
    return pl.pallas_call(
        pair_kernel,
        out_shape=(
            jax.ShapeDtypeStruct((COARSE, COARSE), jnp.float32),
            jax.ShapeDtypeStruct((HALF, COARSE), jnp.float32),
            jax.ShapeDtypeStruct((LOCAL + 8, COARSE), jnp.float32),
        ),
        in_specs=[SMEM, HBM, HBM, HBM],
        out_specs=(VMEM, VMEM, VMEM),
        scratch_shapes=[
            square,
            square,
            pltpu.VMEM((ROWS, COLS), jnp.float32),
            pltpu.VMEM((32, TILE), jnp.float32),
            pltpu.SemaphoreType.DMA((3,)),
        ],
        compiler_params=pltpu.CompilerParams(vmem_limit_bytes=24 << 20),
    )(ids, own, other, state)


def fine_kernel(halo, corrected, ids_ref, class_ref, sets_ref, *refs):
    if corrected:
        c_ref, *refs = refs
        (u_ref, up_ref, f_ref, down_ref), refs = refs[:4], refs[4:]
    else:
        (up_ref, u_ref, f_ref, down_ref), refs = refs[:4], refs[4:]
    fin_ref, means_ref = refs[:2]
    u_ext, f_ext, first, second, force, coef, sums_ref, sems = refs[2:]
    ext = ROWS + 2 * halo
    lines = ext // 8
    wide = 2 * STEPS
    strip = ids_ref[0]
    if corrected:
        parts = ((u_ref, 0, ext, u_ext, 0),)
    else:
        parts = (
            (u_ref, 0, ROWS, u_ext, halo),
            (up_ref, wide - halo, halo, u_ext, 0),
            (down_ref, 0, halo, u_ext, halo + ROWS),
        )
    parts += (
        (f_ref, 0, ROWS, f_ext, halo),
        (up_ref, 2 * wide - halo, halo, f_ext, 0),
        (down_ref, wide, halo, f_ext, halo + ROWS),
    )
    copies = []
    for k in range(TILES):
        cols = pl.ds(k * TILE, TILE)
        copies.append([])
        for n, (source, at, rows, target, to) in enumerate(parts):
            copy = pltpu.make_async_copy(source.at[pl.ds(at, rows), cols], target.at[k, pl.ds(to, rows)], sems.at[n, k])
            copy.start()
            copies[k].append(copy)

    sub = iota((8, TILE), 0)
    lane = iota((8, TILE), 1)
    strips = (lax.rem(strip + 7, 8), strip, lax.rem(strip + 1, 8))

    def weights(row, k):
        label = class_ref[row, k]
        spread, along_cols, along_rows = sets_ref[0, label], sets_ref[1, label], sets_ref[2, label]
        left = STEP * (spread + jnp.maximum(along_cols, 0.0))
        right = STEP * (spread - jnp.minimum(along_cols, 0.0))
        above = STEP * (spread + jnp.maximum(along_rows, 0.0))
        below = STEP * (spread - jnp.minimum(along_rows, 0.0))
        return 1.0 - (left + right + above + below), left, right, above, below

    kinds = []
    for i in range(lines):
        kind = (i < halo, i >= lines - halo)
        if kind not in kinds:
            kinds.append(kind)
    for k in range(TILES):
        upper, inner, lower = (weights(row, k) for row in strips)
        for n, (top, bottom) in enumerate(kinds):
            for w in range(5):
                value = jnp.full((8, TILE), inner[w], jnp.float32)
                if top:
                    value = jnp.where(sub == 0, upper[w], value)
                if bottom:
                    value = jnp.where(sub == 7, lower[w], value)
                coef[k, 5 * n + w] = value

    for k in range(TILES):
        for copy in copies[k]:
            copy.wait()
        if corrected:
            added = []
            for line in range(4):
                at = lax.rem(2 * strip + 15 + line, 16) * 32 + 2 * k
                added.append(jnp.where(lane < BLK, c_ref[0, at], c_ref[0, at + 1]))
        for i in range(lines):
            value = u_ext[k, pl.ds(i, 8, stride=lines), :]
            if corrected:
                row = sub * lines + i
                addend = jnp.where(row < halo + BLK, added[1], added[2])
                if i < halo:
                    addend = jnp.where(sub == 0, added[0], addend)
                if i >= lines - halo:
                    addend = jnp.where(sub == 7, added[3], addend)
                value = value + addend
            first[k, pl.ds(i * 8, 8), :] = value
            force[k, pl.ds(i * 8, 8), :] = STEP * f_ext[k, pl.ds(i, 8, stride=lines), :]

    def tile_step(old, new, k):
        before = lax.rem(k + TILES - 1, TILES)
        after = lax.rem(k + 1, TILES)
        line = [old[k, pl.ds(i * 8, 8), :] for i in range(lines)]
        top = pltpu.roll(line[-1], 1, 0)
        bottom = pltpu.roll(line[0], 7, 0)
        for i in range(lines):
            kind = kinds.index((i < halo, i >= lines - halo))
            centre, w_left, w_right, w_above, w_below = (coef[k, 5 * kind + w] for w in range(5))
            rows = pl.ds(i * 8, 8)
            left = pltpu.roll(jnp.where(lane == TILE - 1, old[before, rows, :], line[i]), 1, 1)
            right = pltpu.roll(jnp.where(lane == 0, old[after, rows, :], line[i]), TILE - 1, 1)
            above = line[i - 1] if i else top
            below = line[i + 1] if i + 1 < lines else bottom
            new[k, rows, :] = (
                (centre * line[i] + force[k, rows, :])
                + (w_left * left + w_right * right)
                + (w_above * above + w_below * below)
            )

    def two_steps(_, carry):
        def there(k, carry):
            tile_step(first, second, k)
            return carry

        def back(k, carry):
            tile_step(second, first, k)
            return carry

        lax.fori_loop(0, TILES, there, 0, unroll=8)
        lax.fori_loop(0, TILES, back, 0, unroll=8)
        return carry

    lax.fori_loop(0, STEPS // 2, two_steps, 0)

    kept = ext - 2 * STEPS
    results = []
    for k in range(TILES):
        for i in range(lines):
            u_ext[k, pl.ds(i, 8, stride=lines), :] = first[k, pl.ds(i * 8, 8), :]
        cols = pl.ds(k * TILE, TILE)
        result = pltpu.make_async_copy(u_ext.at[k, pl.ds(STEPS, kept)], fin_ref.at[:, cols], sems.at[0, k])
        result.start()
        results.append(result)
        for br in range(2):
            part = u_ext[k, halo + br * BLK : halo + (br + 1) * BLK, :]
            sums_ref[br * TILES + k : br * TILES + k + 1, :] = jnp.sum(part, axis=0, keepdims=True)
    means_ref[...] = packed_means(sums_ref[...])
    for result in results:
        result.wait()


def fine_sweep(ids, tile_class, coeff_sets, fields, correction=None):
    corrected = correction is not None
    halo = STEPS if corrected else 2 * STEPS
    ext = ROWS + 2 * halo
    field = pltpu.VMEM((TILES, ext, TILE), jnp.float32)
    return pl.pallas_call(
        functools.partial(fine_kernel, halo, corrected),
        out_shape=(
            jax.ShapeDtypeStruct((ext - 2 * STEPS, COLS), jnp.float32),
            jax.ShapeDtypeStruct((1, TILE), jnp.float32),
        ),
        in_specs=[SMEM, SMEM, SMEM] + [SMEM] * corrected + [HBM] * 4,
        out_specs=(HBM, VMEM),
        scratch_shapes=[
            field,
            field,
            field,
            field,
            field,
            pltpu.VMEM((TILES, 15, 8, TILE), jnp.float32),
            pltpu.VMEM((32, TILE), jnp.float32),
            pltpu.SemaphoreType.DMA((6, TILES)),
        ],
        compiler_params=pltpu.CompilerParams(vmem_limit_bytes=32 << 20),
    )(ids, tile_class, coeff_sets, *([correction] * corrected), *fields)


def message_kernel(ids_ref, means_ref, base_ref, columns_ref, out_ref, block):
    defect = means_ref[...] - base_ref[...]
    lane = iota((1, TILE), 1)
    pushed = jnp.dot(
        jnp.broadcast_to(defect, (8, TILE))[:, :LOCAL],
        columns_ref[0:LOCAL, :],
        precision=HIGHEST,
        preferred_element_type=jnp.float32,
    )
    odd = lax.rem(ids_ref[0], 2)
    raw = jnp.where((lane >= LOCAL) == (odd == 1), defect, 0.0)
    pieces = [pushed[0:1, q * TILE : (q + 1) * TILE] for q in range(4)] + [raw]
    for n in range(8):
        for q in range(PIECES):
            block[n * PIECES + q : n * PIECES + q + 1, :] = pieces[q]
    for n in range(16):
        out_ref[n * 8 * PIECES : (n + 1) * 8 * PIECES, :] = block[...]


def message(ids, means, base, columns):
    return pl.pallas_call(
        message_kernel,
        out_shape=jax.ShapeDtypeStruct((128 * PIECES, TILE), jnp.float32),
        in_specs=[SMEM, VMEM, VMEM, VMEM],
        out_specs=VMEM,
        scratch_shapes=[pltpu.VMEM((8 * PIECES, TILE), jnp.float32)],
        compiler_params=pltpu.CompilerParams(vmem_limit_bytes=16 << 20),
    )(ids, means, base, columns)


def chain_kernel(last, ids_ref, got_ref, other_ref, *refs):
    whole, refs = refs[:5], refs[5:]
    halved, refs = refs[:6], refs[6:]
    if last:
        u_ref, refs = refs[0], refs[1:]
    out_ref, refs = refs[0], refs[1:]
    if not last:
        local_ref, refs = refs[0], refs[1:]
    maps, early, sems, *refs = refs
    strip, core, chip, y = ids_ref[0], ids_ref[1], ids_ref[2], ids_ref[3]

    def fetch_whole(slot, source):
        for part in range(2):
            rows = pl.ds(part * HALF, HALF)
            pltpu.make_async_copy(source.at[rows], maps.at[slot, rows], sems.at[slot, part]).start()

    def fetch_halves(slot, which):
        for part, at in ((0, core), (1, 1 - core)):
            rows = pl.ds(pl.multiple_of(at * HALF, HALF), HALF)
            pltpu.make_async_copy(halved[2 * which + part], maps.at[slot, rows], sems.at[slot, part]).start()

    def fetch_turned(slot, pair, below):
        mine, theirs = pair
        own = (core == 0) == below

        @pl.when(own)
        def _():
            fetch_whole(slot, mine)

        @pl.when(jnp.logical_not(own))
        def _():
            fetch_whole(slot, theirs)

    def fetch_near(slot, ahead):
        if ahead == 2:
            fetch_halves(slot, 0)
        else:
            fetch_turned(slot, whole[0:2], ahead == 3)

    def fetch_far(slot, ahead):
        if ahead in (0, 2):
            fetch_halves(slot, 2 if ahead else 1)
        else:
            fetch_turned(slot, whole[2:4], ahead == 3)

    def landed(slot):
        for part in range(2):
            rows = pl.ds(0, HALF)
            pltpu.make_async_copy(other_ref.at[rows], maps.at[slot, rows], sems.at[slot, part]).wait()

    for half in range(2):
        if half == 1:
            fetch_far(4, 0)
        for ahead in range(1, 4):
            wraps = y + ahead >= 4

            @pl.when(wraps == (half == 0))
            def _():
                fetch_far(4 * half + ahead, ahead)

            @pl.when(wraps != (half == 0))
            def _():
                fetch_near(4 * half + ahead, ahead)

    fetch_whole(0, whole[4])
    final = pltpu.make_async_copy(other_ref, early, sems.at[8, 0])
    final.start()
    if last:
        u, sem = refs
        state = pltpu.make_async_copy(u_ref, u, sem)
        state.start()

    diagonal = iota((TILE, TILE), 0) == iota((TILE, TILE), 1)

    def applied(matrix, vector):
        row = jnp.concatenate(vector, axis=1)
        column = jnp.sum(matrix * row, axis=1, keepdims=True)
        return [
            jnp.sum(jnp.where(diagonal, column[q * TILE : (q + 1) * TILE], 0.0), axis=0, keepdims=True)
            for q in range(4)
        ]

    def group(window):
        start = lax.rem(window + 16, 16) * (8 * PIECES)
        return [
            jnp.sum(got_ref[pl.ds(start + q, 8, stride=PIECES), :], axis=0, keepdims=True) for q in range(4)
        ]

    def add(a, b):
        return [p + q for p, q in zip(a, b, strict=True)]

    def pushed(step):
        at = 2 * lax.rem(chip + step, 8)
        return add(group(at - 1), group(at))

    value = [jnp.where(core == 1, p, q) for p, q in zip(group(2 * chip), pushed(0), strict=True)]

    def arriving(step, value):
        landed(step)
        return add(applied(maps[step], value), pushed(step))

    value = lax.fori_loop(1, 8, arriving, value)
    landed(0)

    def again(step, value):
        return add(applied(maps[step], value), pushed(step))

    value = lax.fori_loop(0, 8, again, value)
    final.wait()
    start = lax.rem(2 * chip + 15, 16) * (8 * PIECES) + 4
    raw = got_ref[pl.ds(start, 8, stride=PIECES), :]
    defect = [raw[2 * q : 2 * q + 1] + raw[2 * q + 1 : 2 * q + 2] for q in range(4)]
    value = [
        jnp.where(core == 1, p, q) for p, q in zip(applied(early[...], add(value, defect)), value, strict=True)
    ]
    if not last:
        out_ref[...] = jnp.concatenate(value, axis=1)
    lane = iota((8, TILE), 1)
    piece = value[3]
    for q in range(3):
        piece = jnp.where(strip // 2 == q, value[q], piece)
    piece = jnp.broadcast_to(piece, (8, TILE))
    odd = lax.rem(strip, 2)
    if not last:
        here = jnp.where((lane < LOCAL) == (odd == 0), piece, pltpu.roll(piece, LOCAL, 1))
        local_ref[...] = here[0:1]
        return
    state.wait()
    outs = []
    for k in range(TILES):
        cols = slice(k * TILE, (k + 1) * TILE)
        for br in range(2):
            at = odd * LOCAL + br * 32 + 2 * k
            added = jnp.take_along_axis(piece, at + jnp.where(lane < BLK, 0, 1), axis=1)
            for n in range(BLK // 8):
                rows = slice(br * BLK + n * 8, br * BLK + (n + 1) * 8)
                u[rows, cols] = u[rows, cols] + added
        if k % 4 == 3:
            cols = pl.ds((k - 3) * TILE, 4 * TILE)
            copy = pltpu.make_async_copy(u.at[:, cols], out_ref.at[:, cols], sems.at[k // 4, 0])
            copy.start()
            outs.append(copy)
    for copy in outs:
        copy.wait()


def chain(ids, got, other, whole, halved, previous=None):
    last = previous is not None
    if last:
        out_shape, out_specs = jax.ShapeDtypeStruct((ROWS, COLS), jnp.float32), HBM
    else:
        out_shape = (
            jax.ShapeDtypeStruct((1, COARSE), jnp.float32),
            jax.ShapeDtypeStruct((1, TILE), jnp.float32),
        )
        out_specs = (VMEM, VMEM)
    return pl.pallas_call(
        functools.partial(chain_kernel, last),
        out_shape=out_shape,
        in_specs=[SMEM, VMEM] + [HBM] * (12 + last),
        out_specs=out_specs,
        scratch_shapes=[
            pltpu.VMEM((8, COARSE, COARSE), jnp.float32),
            pltpu.VMEM((COARSE, COARSE), jnp.float32),
            pltpu.SemaphoreType.DMA((9, 2)),
        ]
        + [pltpu.VMEM((ROWS, COLS), jnp.float32), pltpu.SemaphoreType.DMA] * last,
        compiler_params=pltpu.CompilerParams(vmem_limit_bytes=32 << 20),
    )(ids, got, other, *whole, *halved, *([previous] * last))


def exchanged(block):
    block = block.reshape(128, 1, PIECES * TILE)
    return lax.all_to_all(block, ("tm", "space"), 0, 0, tiled=True).reshape(128 * PIECES, TILE)


def swapped(value):
    return moved(value, lambda x, y, z, core: (x, y, z, 1 - core))


def across(value):
    return moved(value, lambda x, y, z, core: (x, y, z + 1 - 2 * core, core))


def along(value, dz=0):
    return moved(value, lambda x, y, z, core: (x, y + 1 - 2 * core, z + dz * (1 - 2 * core), core))


def per_device(initial_states, sources, tile_class, coeff_sets, coarse_maps):
    state, source, own_map = initial_states[0], sources[0], coarse_maps[0]
    window = lax.axis_index("tm").astype(jnp.int32)
    strip = lax.axis_index("space").astype(jnp.int32)
    core = window % 2
    ids = jnp.stack([strip, core, window // 2, (window // 2) % 4])
    wide = 2 * STEPS

    other_map = swapped(own_map)
    upper = shifted(jnp.concatenate([state[-wide:], source[-wide:]], axis=0), 0, 1)
    lower = shifted(jnp.concatenate([state[:wide], source[:wide]], axis=0), 0, -1)

    product, half, columns = pair_product(ids, own_map, other_map, state)
    near = along(product)
    far_same = across(half)
    columns = shifted(columns, -1)

    finished, means = fine_sweep(ids, tile_class, coeff_sets, (upper, state, source, lower))
    previous = shifted(finished, 1)

    near_half = lax.dynamic_slice(near, (core * HALF, 0), (HALF, COARSE))
    far = across(near)
    near_second = along(near_half)
    far_second = along(near_half, 1)

    got = exchanged(message(ids, means, columns[LOCAL : LOCAL + 1, :TILE], columns))

    whole = [near, swapped(near), far, swapped(far), product]
    halved = []
    for part in (near_second, far_same, far_second):
        halved += [part, swapped(part)]
    correction, local = chain(ids, got, other_map, whole, halved)

    base = means + shifted(local, -1)
    finished, means = fine_sweep(ids, tile_class, coeff_sets, (previous, upper, source, lower), correction)
    previous = shifted(finished, 1)
    got = exchanged(message(ids, means, base, columns))
    return chain(ids, got, other_map, whole, halved, previous)[None]


def solution(mesh):
    placed = (P("tm", "space", None), P("tm", "space", None), P(), P(), P("tm", None, None))
    return jax.shard_map(
        per_device, mesh=mesh, in_specs=placed, out_specs=P("tm", "space", None), check_vma=False
    )
```

time: 152 us -> 146 us (0.961)
  Pallas kernels: 54.1 us -> 34.5 us
  blocking collectives: 18.5 us -> 38.1 us
  local copies, waits for them, and re-layouts: 20.3 us -> 5.46 us
  waiting for transfers between devices: 19 us -> 27.2 us
    all_to_all x1 -> x2, blocking collectives: 18.5 us -> 38.1 us  [exchanged(): lax.all_to_all(block, ('tm', 'space'), 0, 0, tiled=True)]
    pallas_call x9 -> x7, Pallas kernels: 54.1 us -> 34.5 us  [the longest x2 20.3 us: fine_sweep(): pl.pallas_call(functools.partial(fine_kernel, halo, corrected), out_shape...]
    ppermute x16 -> x11, starting transfers between devices: 18.5 us -> 30.3 us  [moved(): return lax.ppermute(value, ('tm', 'space'), pairs)]
    unnamed x56 -> x36, local copies, waits for them, and re-layouts: 15.5 us -> 5.39 us
    ppermute x16 -> x11, waiting for transfers between devices: 9.25 us -> 18.8 us  [moved(): return lax.ppermute(value, ('tm', 'space'), pairs)]
    ppermute x9 -> x6, starting transfers between devices: 15.4 us -> 9.2 us  [shifted(): return lax.ppermute(value, ('tm', 'space'), pairs)]
    all_to_all x1 -> x0, starting transfers between devices: 5.15 us -> none  [exchanged(): return lax.all_to_all(block, ('tm', 'space'), 0, 0, tiled=True)]
    slice x5 -> x3, local copies, waits for them, and re-layouts: 3.31 us -> 0.04 us  [the longest x1 0.02 us: per_device(): source[:wide]]
  transfers between devices with their start and end apart: 26 -> 17, of which waited for: 7 -> 6; matrix products, arithmetic and copies ran while one was open for 4% -> 0% of each run, Pallas kernels for 19% -> 11%
where the time goes in v2:
time: 146 us; the launch traced here: 145 us
  starting transfers between devices  39.5 us (27%)
  blocking collectives  38.1 us (26%)
  Pallas kernels  34.5 us (24%)
  waiting for transfers between devices  27.2 us (19%)
  local copies, waits for them, and re-layouts  5.46 us (4%)
    all_to_all x2, blocking collectives, exchanged(): lax.all_to_all(block, ('tm', 'space'), 0, 0, tiled=True)  38.1 us
    ppermute x11, starting transfers between devices, moved(): return lax.ppermute(value, ('tm', 'space'), pairs)  30.3 us
    pallas_call x2, Pallas kernels, fine_sweep(): pl.pallas_call(functools.partial(fine_kernel, halo, corrected), out_shape...  20.3 us
    ppermute x11, waiting for transfers between devices, moved(): return lax.ppermute(value, ('tm', 'space'), pairs)  18.8 us
    pallas_call x2, Pallas kernels, chain(): pl.pallas_call(functools.partial(chain_kernel, last), out_shape=out_shape...  9.92 us
    ppermute x6, starting transfers between devices, shifted(): return lax.ppermute(value, ('tm', 'space'), pairs)  9.2 us
    ppermute x6, waiting for transfers between devices, shifted(): return lax.ppermute(value, ('tm', 'space'), pairs)  8.43 us
    unnamed x36, local copies, waits for them, and re-layouts  5.39 us
  transfers between devices with their start and end apart: 17, of which 6 were waited for; matrix products, arithmetic and copies ran while one was open for 0% of the time, Pallas kernels for 11%

profile of v2, /device:TPU:1, one launch (start us, length us, event | category | flops | bytes accessed | tf_op | source)
XLA Modules:
  0.0 145.4 jit_solution(14167063840122472)
XLA Ops:
  0.0 1.4 collective-permute-start.2
  1.5 2.4 %collective-permute-done.2.other_ref = f32[512,512]{1,0:T(8,128)S(1)} collective-permute-done((f32[512,512]{1,0:T(8,128)}, f32[512,512]{1,0:T(8,128)S(1)}, u32[]{:S(2)}, u32[]{:S(2)}) %collective-permute-start.2) | collective-permute-done | bytes 1048608 | tf_op jit(solution)/shard_map/ppermute | solution.py:43
  3.9 1.2 copy-done
  5.1 1.2 copy-done.7
  6.4 2.8 %shard_map.56 = (f32[512,512]{1,0:T(8,128)S(1)}, f32[256,512]{1,0:T(8,128)S(1)}, f32[72,512]{1,0:T(8,128)}) custom-call(s32[4]{0:T(128)S(1)} %pad_add_fusion.ids_ref, f32[512,512]{1,0:T(8,128)S(1)} %bitcast.29, f32[512,512]{1,0:T(8,128)S(1)} %collective-permute-done.2.other_ref, f32[128,2048]{1,0:T(8,128)S(1)} %bitcast.20), custom_call_target="tpu_custom_call" | custom-call | tf_op jit(solution)/shard_map/pallas_call | solution.py:119
  9.2 2.9 %collective-permute-start.4 = (f32[512,512]{1,0:T(8,128)S(1)}, f32[512,512]{1,0:T(8,128)S(1)}, u32[]{:S(2)}, u32[]{:S(2)}) collective-permute-start(f32[512,512]{1,0:T(8,128)S(1)} %get-tuple-element.16.refs_4_), channel_id=1, source_target_pairs={{0,16},{1,17},{2,18},{3,19},{4,20},{5,21},{6,22},{7,23},{8,56},{9,... | collective-permute-start | bytes 3145736 | tf_op jit(solution)/shard_map/ppermute | solution.py:43
  12.1 1.0 copy-done.3
  13.1 3.8 %collective-permute-start.10 = (f32[256,512]{1,0:T(8,128)S(1)}, f32[256,512]{1,0:T(8,128)}, u32[]{:S(2)}, u32[]{:S(2)}) collective-permute-start(f32[256,512]{1,0:T(8,128)S(1)} %get-tuple-element.17), channel_id=1, source_target_pairs={{0,64},{1,65},{2,66},{3,67},{4,68},{5,69},{6,70},{7,71},{8,76},{9,... | collective-permute-start | bytes 1572872 | tf_op jit(solution)/shard_map/ppermute | solution.py:43
  16.9 6.9 %collective-permute-done.4.refs_0_ = f32[512,512]{1,0:T(8,128)S(1)} collective-permute-done((f32[512,512]{1,0:T(8,128)S(1)}, f32[512,512]{1,0:T(8,128)S(1)}, u32[]{:S(2)}, u32[]{:S(2)}) %collective-permute-start.4) | collective-permute-done | bytes 1048608 | tf_op jit(solution)/shard_map/ppermute | solution.py:43
  23.8 3.8 %collective-permute-start.6 = (f32[512,512]{1,0:T(8,128)S(1)}, f32[512,512]{1,0:T(8,128)}, u32[]{:S(2)}, u32[]{:S(2)}) collective-permute-start(f32[512,512]{1,0:T(8,128)S(1)} %collective-permute-done.4.refs_0_), channel_id=1, source_target_pairs={{0,64},{1,65},{2,66},{3,67},{4,68},{5,69},{6,70},{7,71},{8,76},{9,... | collective-permute-start | bytes 3145736 | tf_op jit(solution)/shard_map/ppermute | solution.py:43
  27.7 1.3 collective-permute-start
  29.3 4.2 %collective-permute-start.1 = (f32[32,2048]{1,0:T(8,128)S(1)}, f32[32,2048]{1,0:T(8,128)S(1)}, u32[]{:S(2)}, u32[]{:S(2)}) collective-permute-start(f32[32,2048]{1,0:T(8,128)S(1)} %pad_maximum_fusion.1), channel_id=1, source_target_pairs={{0,7},{1,0},{2,1},{3,2},{4,3},{5,4},{6,5},{7,6},{8,15},{9,8},{10,9... | collective-permute-start | bytes 786440 | tf_op jit(solution)/shard_map/ppermute | solution.py:52
  33.8 5.3 %collective-permute-done.refs_0_.refs_2_ = f32[32,2048]{1,0:T(8,128)S(1)} collective-permute-done((f32[32,2048]{1,0:T(8,128)S(1)}, f32[32,2048]{1,0:T(8,128)S(1)}, u32[]{:S(2)}, u32[]{:S(2)}) %collective-permute-start) | collective-permute-done | bytes 262176 | tf_op jit(solution)/shard_map/ppermute | solution.py:52
  39.3 10.6 %shard_map.55 = (f32[144,2048]{1,0:T(8,128)}, f32[1,128]{1,0:T(1,128)S(1)}) custom-call(s32[4]{0:T(128)S(1)} %pad_add_fusion.ids_ref, s32[8,16]{1,0:T(8,128)S(1)} %copy-done.11, f32[3,8]{1,0:T(4,128)S(1)} %copy-done.13, f32[32,2048]{1,0:T(8,128)S(1)} %collective-permute-done.refs_0_.refs_2_, f32[128,2048]{1,0:T(8,128)S(1)} %bitcast.21, ...), custom_call_target="tpu_custom_call" | custom-call | tf_op jit(solution)/shard_map/pallas_call | solution.py:280
  49.9 0.6 copy-done.15
  50.5 1.6 %collective-permute-start.14 = (f32[144,2048]{1,0:T(8,128)}, f32[144,2048]{1,0:T(8,128)}, u32[]{:S(2)}, u32[]{:S(2)}) collective-permute-start(f32[144,2048]{1,0:T(8,128)} %get-tuple-element.19), channel_id=1, source_target_pairs={{0,8},{1,9},{2,10},{3,11},{4,12},{5,13},{6,14},{7,15},{8,16},{9,17... | collective-permute-start | bytes 3538952 | tf_op jit(solution)/shard_map/ppermute | solution.py:52
  52.1 4.6 %collective-permute-start.12 = (f32[256,512]{1,0:T(8,128)S(1)}, f32[256,512]{1,0:T(8,128)S(1)}, u32[]{:S(2)}, u32[]{:S(2)}) collective-permute-start(f32[256,512]{1,0:T(8,128)S(1)} %constant_dynamic-slice_fusion), channel_id=1, source_target_pairs={{0,80},{1,81},{2,82},{3,83},{4,84},{5,85},{6,86},{7,87},{8,124},{9... | collective-permute-start | bytes 1572872 | tf_op jit(solution)/shard_map/ppermute | solution.py:43
  56.7 0.5 collective-permute-start.8
  57.3 9.4 %collective-permute-done.12.refs_9_ = f32[256,512]{1,0:T(8,128)S(1)} collective-permute-done((f32[256,512]{1,0:T(8,128)S(1)}, f32[256,512]{1,0:T(8,128)S(1)}, u32[]{:S(2)}, u32[]{:S(2)}) %collective-permute-start.12) | collective-permute-done | bytes 524320 | tf_op jit(solution)/shard_map/ppermute | solution.py:43
  66.7 2.9 %collective-permute-start.13 = (f32[256,512]{1,0:T(8,128)S(1)}, f32[256,512]{1,0:T(8,128)S(1)}, u32[]{:S(2)}, u32[]{:S(2)}) collective-permute-start(f32[256,512]{1,0:T(8,128)S(1)} %collective-permute-done.12.refs_9_), channel_id=1, source_target_pairs={{0,8},{1,9},{2,10},{3,11},{4,12},{5,13},{6,14},{7,15},{8,0},{9,1},... | collective-permute-start | bytes 1572872 | tf_op jit(solution)/shard_map/ppermute | solution.py:43
  69.7 10.0 %collective-permute-start.9 = (f32[256,512]{1,0:T(8,128)S(1)}, f32[256,512]{1,0:T(8,128)S(1)}, u32[]{:S(2)}, u32[]{:S(2)}) collective-permute-start(f32[256,512]{1,0:T(8,128)S(1)} %collective-permute-done.8.refs_5_), channel_id=1, source_target_pairs={{0,8},{1,9},{2,10},{3,11},{4,12},{5,13},{6,14},{7,15},{8,0},{9,1},... | collective-permute-start | bytes 1572872 | tf_op jit(solution)/shard_map/ppermute | solution.py:43
  79.7 0.7 copy-done.9
  80.3 0.7 copy-done.16
  81.0 0.7 shard_map.57
  81.7 20.2 %all_to_all.10 = f32[128,1,640]{2,1,0:T(1,128)S(1)} all-to-all(f32[128,1,640]{2,1,0:T(1,128)S(1)} %bitcast.27), channel_id=1, replica_groups=mesh['tm'=16,'space'=8] {'tm','space'}, dimensions={0} | all-to-all | bytes 655360 | tf_op jit(solution)/shard_map/all_to_all | solution.py:505
  102.1 4.5 %shard_map.58 = (f32[1,512]{1,0:T(1,128)S(1)}, f32[1,128]{1,0:T(1,128)S(1)}) custom-call(s32[4]{0:T(128)S(1)} %copy-done.10, f32[640,128]{1,0:T(8,128)S(1)} %bitcast.25, f32[512,512]{1,0:T(8,128)S(1)} %collective-permute-done.2.other_ref, f32[512,512]{1,0:T(8,128)S(1)} %collective-permute-done.4.refs_0_, f32[512,512]{1,0:T(8,128)S(1)} %collective-permute-done.5.refs_1_, ...), custom_call_target="tpu_custom_call" | custom-call | tf_op jit(solution)/shard_map/pallas_call | solution.py:488
  106.6 9.7 %shard_map.59 = (f32[128,2048]{1,0:T(8,128)S(1)}, f32[1,128]{1,0:T(1,128)S(1)}) custom-call(s32[4]{0:T(128)S(1)} %copy-done.10, s32[8,16]{1,0:T(8,128)S(1)} %copy-done.12, f32[3,8]{1,0:T(4,128)S(1)} %copy-done.14, f32[1,512]{1,0:T(1,128)S(1)} %get-tuple-element.18.refs_0_, f32[144,2048]{1,0:T(8,128)} %collective-permute-done.14.refs_1_, ...), custom_call_target="tpu_custom_call" | custom-call | tf_op jit(solution)/shard_map/pallas_call | solution.py:280
  116.3 1.8 %collective-permute-start.16 = (f32[128,2048]{1,0:T(8,128)S(1)}, f32[128,2048]{1,0:T(8,128)S(1)}, u32[]{:S(2)}, u32[]{:S(2)}) collective-permute-start(f32[128,2048]{1,0:T(8,128)S(1)} %get-tuple-element.22), channel_id=1, source_target_pairs={{0,8},{1,9},{2,10},{3,11},{4,12},{5,13},{6,14},{7,15},{8,16},{9,17... | collective-permute-start | bytes 3145736 | tf_op jit(solution)/shard_map/ppermute | solution.py:52
  118.2 3.0 %collective-permute-done.15 = f32[1,128]{1,0:T(1,128)S(1)} collective-permute-done((f32[1,128]{1,0:T(1,128)S(1)}, f32[1,128]{1,0:T(1,128)S(1)}, u32[]{:S(2)}, u32[]{:S(2)}) %collective-permute-start.15) | collective-permute-done | bytes 544 | tf_op jit(solution)/shard_map/ppermute | solution.py:52
  121.1 0.7 shard_map.60
  121.9 17.9 %all_to_all.11 = f32[128,1,640]{2,1,0:T(1,128)S(1)} all-to-all(f32[128,1,640]{2,1,0:T(1,128)S(1)} %bitcast.26), channel_id=1, replica_groups=mesh['tm'=16,'space'=8] {'tm','space'}, dimensions={0} | all-to-all | bytes 655360 | tf_op jit(solution)/shard_map/all_to_all | solution.py:505
  139.8 5.5 %shard_map.61 = f32[128,2048]{1,0:T(8,128)} custom-call(s32[4]{0:T(128)S(1)} %copy-done.10, f32[640,128]{1,0:T(8,128)S(1)} %bitcast.24, f32[512,512]{1,0:T(8,128)S(1)} %collective-permute-done.2.other_ref, f32[512,512]{1,0:T(8,128)S(1)} %collective-permute-done.4.refs_0_, f32[512,512]{1,0:T(8,128)S(1)} %collective-permute-done.5.refs_1_, ...), custom_call_target="tpu_custom_call" | custom-call | tf_op jit(solution)/shard_map/pallas_call | solution.py:488
  (55 shorter events, 1.2 us)
Async XLA Ops:
  0.0 3.9 %collective-permute-start.2 = (f32[512,512]{1,0:T(8,128)}, f32[512,512]{1,0:T(8,128)S(1)}, u32[]{:S(2)}, u32[]{:S(2)}) collective-permute-start(f32[512,512]{1,0:T(8,128)} %bitcast.28), channel_id=1, source_target_pairs={{0,8},{1,9},{2,10},{3,11},{4,12},{5,13},{6,14},{7,15},{8,0},{9,1},... | collective-permute-start | bytes 3145736 | tf_op jit(solution)/shard_map/ppermute | solution.py:43
  1.5 37.8 %copy-start.8 = (s32[4]{0:T(128)}, s32[4]{0:T(128)S(1)}, u32[]{:S(2)}) copy-start(s32[4]{0:T(128)S(1)} %pad_add_fusion.ids_ref) | copy-start | bytes 52
  3.9 1.2 copy-start
  5.1 1.2 copy-start.7
  6.4 21.2 %copy-start.2 = (f32[1,128,2048]{2,1,0:T(8,128)S(1)}, f32[1,128,2048]{2,1,0:T(8,128)}, u32[]{:S(2)}) copy-start(f32[1,128,2048]{2,1,0:T(8,128)} %param.6) | copy-start | bytes 3145732
  9.2 30.1 %copy-start.1 = (f32[1,128,2048]{2,1,0:T(8,128)S(1)}, f32[1,128,2048]{2,1,0:T(8,128)}, u32[]{:S(2)}) copy-start(f32[1,128,2048]{2,1,0:T(8,128)} %param.5) | copy-start | bytes 3145732
  9.2 30.1 %copy-start.11 = (s32[8,16]{1,0:T(8,128)S(1)}, s32[8,16]{1,0:T(8,128)}, u32[]{:S(2)}) copy-start(s32[8,16]{1,0:T(8,128)} %class_ref.3) | copy-start | bytes 1540
  9.2 30.1 %copy-start.13 = (f32[3,8]{1,0:T(4,128)S(1)}, f32[3,8]{1,0:T(4,128)}, u32[]{:S(2)}) copy-start(f32[3,8]{1,0:T(4,128)} %sets_ref.3) | copy-start | bytes 292
  9.2 14.6 %collective-permute-start.4 = (f32[512,512]{1,0:T(8,128)S(1)}, f32[512,512]{1,0:T(8,128)S(1)}, u32[]{:S(2)}, u32[]{:S(2)}) collective-permute-start(f32[512,512]{1,0:T(8,128)S(1)} %get-tuple-element.16.refs_4_), channel_id=1, source_target_pairs={{0,16},{1,17},{2,18},{3,19},{4,20},{5,21},{6,22},{7,23},{8,56},{9,... | collective-permute-start | bytes 3145736 | tf_op jit(solution)/shard_map/ppermute | solution.py:43
  12.1 1.0 copy-start.3
  13.1 15.8 %collective-permute-start.10 = (f32[256,512]{1,0:T(8,128)S(1)}, f32[256,512]{1,0:T(8,128)}, u32[]{:S(2)}, u32[]{:S(2)}) collective-permute-start(f32[256,512]{1,0:T(8,128)S(1)} %get-tuple-element.17), channel_id=1, source_target_pairs={{0,64},{1,65},{2,66},{3,67},{4,68},{5,69},{6,70},{7,71},{8,76},{9,... | collective-permute-start | bytes 1572872 | tf_op jit(solution)/shard_map/ppermute | solution.py:43
  23.8 33.4 %collective-permute-start.6 = (f32[512,512]{1,0:T(8,128)S(1)}, f32[512,512]{1,0:T(8,128)}, u32[]{:S(2)}, u32[]{:S(2)}) collective-permute-start(f32[512,512]{1,0:T(8,128)S(1)} %collective-permute-done.4.refs_0_), channel_id=1, source_target_pairs={{0,64},{1,65},{2,66},{3,67},{4,68},{5,69},{6,70},{7,71},{8,76},{9,... | collective-permute-start | bytes 3145736 | tf_op jit(solution)/shard_map/ppermute | solution.py:43
  27.7 11.4 %collective-permute-start = (f32[32,2048]{1,0:T(8,128)S(1)}, f32[32,2048]{1,0:T(8,128)S(1)}, u32[]{:S(2)}, u32[]{:S(2)}) collective-permute-start(f32[32,2048]{1,0:T(8,128)S(1)} %pad_maximum_fusion), channel_id=1, source_target_pairs={{0,1},{1,2},{2,3},{3,4},{4,5},{5,6},{6,7},{7,0},{8,9},{9,10},{10,1... | collective-permute-start | bytes 786440 | tf_op jit(solution)/shard_map/ppermute | solution.py:52
  28.9 27.8 %collective-permute-start.11 = (f32[256,512]{1,0:T(8,128)}, f32[256,512]{1,0:T(8,128)}, u32[]{:S(2)}, u32[]{:S(2)}) collective-permute-start(f32[256,512]{1,0:T(8,128)} %collective-permute-done.10.refs_7_), channel_id=1, source_target_pairs={{0,8},{1,9},{2,10},{3,11},{4,12},{5,13},{6,14},{7,15},{8,0},{9,1},... | collective-permute-start | bytes 1572872 | tf_op jit(solution)/shard_map/ppermute | solution.py:43
  29.3 9.9 %collective-permute-start.1 = (f32[32,2048]{1,0:T(8,128)S(1)}, f32[32,2048]{1,0:T(8,128)S(1)}, u32[]{:S(2)}, u32[]{:S(2)}) collective-permute-start(f32[32,2048]{1,0:T(8,128)S(1)} %pad_maximum_fusion.1), channel_id=1, source_target_pairs={{0,7},{1,0},{2,1},{3,2},{4,3},{5,4},{6,5},{7,6},{8,15},{9,8},{10,9... | collective-permute-start | bytes 786440 | tf_op jit(solution)/shard_map/ppermute | solution.py:52
  33.5 23.2 %collective-permute-start.3 = (f32[72,512]{1,0:T(8,128)}, f32[72,512]{1,0:T(8,128)S(1)}, u32[]{:S(2)}, u32[]{:S(2)}) collective-permute-start(f32[72,512]{1,0:T(8,128)} %get-tuple-element.15), channel_id=1, source_target_pairs={{0,120},{1,121},{2,122},{3,123},{4,124},{5,125},{6,126},{7,127},{8... | collective-permute-start | bytes 442376 | tf_op jit(solution)/shard_map/ppermute | solution.py:52
  39.2 10.6 %copy-start.5 = (f32[32,2048]{1,0:T(8,128)}, f32[32,2048]{1,0:T(8,128)S(1)}, u32[]{:S(2)}) copy-start(f32[32,2048]{1,0:T(8,128)S(1)} %collective-permute-done.1.refs_3_.refs_4_) | copy-start | bytes 786436
  50.5 56.1 %collective-permute-start.14 = (f32[144,2048]{1,0:T(8,128)}, f32[144,2048]{1,0:T(8,128)}, u32[]{:S(2)}, u32[]{:S(2)}) collective-permute-start(f32[144,2048]{1,0:T(8,128)} %get-tuple-element.19), channel_id=1, source_target_pairs={{0,8},{1,9},{2,10},{3,11},{4,12},{5,13},{6,14},{7,15},{8,16},{9,17... | collective-permute-start | bytes 3538952 | tf_op jit(solution)/shard_map/ppermute | solution.py:52
  52.1 49.9 %copy-start.4 = (f32[512,512]{1,0:T(8,128)S(1)}, f32[512,512]{1,0:T(8,128)}, u32[]{:S(2)}) copy-start(f32[512,512]{1,0:T(8,128)} %copy-done.3) | copy-start | bytes 3145732
  52.1 50.0 %copy-start.10 = (s32[4]{0:T(128)S(1)}, s32[4]{0:T(128)}, u32[]{:S(2)}) copy-start(s32[4]{0:T(128)} %copy-done.8) | copy-start | bytes 52
  52.1 14.6 %collective-permute-start.12 = (f32[256,512]{1,0:T(8,128)S(1)}, f32[256,512]{1,0:T(8,128)S(1)}, u32[]{:S(2)}, u32[]{:S(2)}) collective-permute-start(f32[256,512]{1,0:T(8,128)S(1)} %constant_dynamic-slice_fusion), channel_id=1, source_target_pairs={{0,80},{1,81},{2,82},{3,83},{4,84},{5,85},{6,86},{7,87},{8,124},{9... | collective-permute-start | bytes 1572872 | tf_op jit(solution)/shard_map/ppermute | solution.py:43
  56.7 45.3 %collective-permute-start.5 = (f32[512,512]{1,0:T(8,128)S(1)}, f32[512,512]{1,0:T(8,128)S(1)}, u32[]{:S(2)}, u32[]{:S(2)}) collective-permute-start(f32[512,512]{1,0:T(8,128)S(1)} %collective-permute-done.4.refs_0_), channel_id=1, source_target_pairs={{0,8},{1,9},{2,10},{3,11},{4,12},{5,13},{6,14},{7,15},{8,0},{9,1},... | collective-permute-start | bytes 3145736 | tf_op jit(solution)/shard_map/ppermute | solution.py:43
  56.7 13.0 %collective-permute-start.8 = (f32[256,512]{1,0:T(8,128)S(1)}, f32[256,512]{1,0:T(8,128)S(1)}, u32[]{:S(2)}, u32[]{:S(2)}) collective-permute-start(f32[256,512]{1,0:T(8,128)S(1)} %constant_dynamic-slice_fusion), channel_id=1, source_target_pairs={{0,16},{1,17},{2,18},{3,19},{4,20},{5,21},{6,22},{7,23},{8,56},{9,... | collective-permute-start | bytes 1572872 | tf_op jit(solution)/shard_map/ppermute | solution.py:43
  57.2 44.8 %collective-permute-start.7 = (f32[512,512]{1,0:T(8,128)}, f32[512,512]{1,0:T(8,128)S(1)}, u32[]{:S(2)}, u32[]{:S(2)}) collective-permute-start(f32[512,512]{1,0:T(8,128)} %collective-permute-done.6.refs_2_), channel_id=1, source_target_pairs={{0,8},{1,9},{2,10},{3,11},{4,12},{5,13},{6,14},{7,15},{8,0},{9,1},... | collective-permute-start | bytes 3145736 | tf_op jit(solution)/shard_map/ppermute | solution.py:43
  66.7 35.3 %collective-permute-start.13 = (f32[256,512]{1,0:T(8,128)S(1)}, f32[256,512]{1,0:T(8,128)S(1)}, u32[]{:S(2)}, u32[]{:S(2)}) collective-permute-start(f32[256,512]{1,0:T(8,128)S(1)} %collective-permute-done.12.refs_9_), channel_id=1, source_target_pairs={{0,8},{1,9},{2,10},{3,11},{4,12},{5,13},{6,14},{7,15},{8,0},{9,1},... | collective-permute-start | bytes 1572872 | tf_op jit(solution)/shard_map/ppermute | solution.py:43
  69.7 32.3 %collective-permute-start.9 = (f32[256,512]{1,0:T(8,128)S(1)}, f32[256,512]{1,0:T(8,128)S(1)}, u32[]{:S(2)}, u32[]{:S(2)}) collective-permute-start(f32[256,512]{1,0:T(8,128)S(1)} %collective-permute-done.8.refs_5_), channel_id=1, source_target_pairs={{0,8},{1,9},{2,10},{3,11},{4,12},{5,13},{6,14},{7,15},{8,0},{9,1},... | collective-permute-start | bytes 1572872 | tf_op jit(solution)/shard_map/ppermute | solution.py:43
  102.0 4.5 %copy-start.6 = (f32[32,2048]{1,0:T(8,128)S(1)}, f32[32,2048]{1,0:T(8,128)}, u32[]{:S(2)}) copy-start(f32[32,2048]{1,0:T(8,128)} %copy-done.5) | copy-start | bytes 786436
  102.0 4.5 %copy-start.12 = (s32[8,16]{1,0:T(8,128)S(1)}, s32[8,16]{1,0:T(8,128)}, u32[]{:S(2)}) copy-start(s32[8,16]{1,0:T(8,128)} %class_ref.3) | copy-start | bytes 1540
  102.1 4.5 %copy-start.14 = (f32[3,8]{1,0:T(4,128)S(1)}, f32[3,8]{1,0:T(4,128)}, u32[]{:S(2)}) copy-start(f32[3,8]{1,0:T(4,128)} %sets_ref.3) | copy-start | bytes 292
  106.6 14.5 %copy-start.17 = (f32[1,128]{1,0:T(1,128)S(1)}, f32[1,128]{1,0:T(1,128)}, u32[]{:S(2)}) copy-start(f32[1,128]{1,0:T(1,128)} %copy-done.15) | copy-start | bytes 1540
  116.3 23.4 %collective-permute-start.16 = (f32[128,2048]{1,0:T(8,128)S(1)}, f32[128,2048]{1,0:T(8,128)S(1)}, u32[]{:S(2)}, u32[]{:S(2)}) collective-permute-start(f32[128,2048]{1,0:T(8,128)S(1)} %get-tuple-element.22), channel_id=1, source_target_pairs={{0,8},{1,9},{2,10},{3,11},{4,12},{5,13},{6,14},{7,15},{8,16},{9,17... | collective-permute-start | bytes 3145736 | tf_op jit(solution)/shard_map/ppermute | solution.py:52
  118.2 3.0 %collective-permute-start.15 = (f32[1,128]{1,0:T(1,128)S(1)}, f32[1,128]{1,0:T(1,128)S(1)}, u32[]{:S(2)}, u32[]{:S(2)}) collective-permute-start(f32[1,128]{1,0:T(1,128)S(1)} %get-tuple-element.21), channel_id=1, source_target_pairs={{0,120},{1,121},{2,122},{3,123},{4,124},{5,125},{6,126},{7,127},{8... | collective-permute-start | bytes 1544 | tf_op jit(solution)/shard_map/ppermute | solution.py:52
  (3 other events, 1.9 us)

commit v3 on v2

--- a/solution.py
+++ b/solution.py
@@ -50,6 +50,14 @@
         for sp in range(8)
     ]
     return lax.ppermute(value, ("tm", "space"), pairs)
+
+
+def cost(micros):
+    return pl.CostEstimate(flops=0, transcendentals=0, bytes_accessed=int(micros * 3.6e6))
+
+
+def in_hbm(*values):
+    return [pltpu.with_memory_space_constraint(value, pltpu.HBM) for value in values]
 
 
 def iota(shape, axis):
@@ -118,6 +126,7 @@
     square = pltpu.VMEM((COARSE, COARSE), jnp.float32)
     return pl.pallas_call(
         pair_kernel,
+        cost_estimate=cost(3),
         out_shape=(
             jax.ShapeDtypeStruct((COARSE, COARSE), jnp.float32),
             jax.ShapeDtypeStruct((HALF, COARSE), jnp.float32),
@@ -133,7 +142,7 @@
             pltpu.SemaphoreType.DMA((3,)),
         ],
         compiler_params=pltpu.CompilerParams(vmem_limit_bytes=24 << 20),
-    )(ids, own, other, state)
+    )(ids, *in_hbm(own, other, state))
 
 
 def fine_kernel(halo, corrected, ids_ref, class_ref, sets_ref, *refs):
@@ -279,6 +288,7 @@
     field = pltpu.VMEM((TILES, ext, TILE), jnp.float32)
     return pl.pallas_call(
         functools.partial(fine_kernel, halo, corrected),
+        cost_estimate=cost(10),
         out_shape=(
             jax.ShapeDtypeStruct((ext - 2 * STEPS, COLS), jnp.float32),
             jax.ShapeDtypeStruct((1, TILE), jnp.float32),
@@ -296,7 +306,7 @@
             pltpu.SemaphoreType.DMA((6, TILES)),
         ],
         compiler_params=pltpu.CompilerParams(vmem_limit_bytes=32 << 20),
-    )(ids, tile_class, coeff_sets, *([correction] * corrected), *fields)
+    )(ids, tile_class, coeff_sets, *([correction] * corrected), *in_hbm(*fields))
 
 
 def message_kernel(ids_ref, means_ref, base_ref, columns_ref, out_ref, block):
@@ -321,6 +331,7 @@
 def message(ids, means, base, columns):
     return pl.pallas_call(
         message_kernel,
+        cost_estimate=cost(1),
         out_shape=jax.ShapeDtypeStruct((128 * PIECES, TILE), jnp.float32),
         in_specs=[SMEM, VMEM, VMEM, VMEM],
         out_specs=VMEM,
@@ -454,7 +465,7 @@
     odd = lax.rem(strip, 2)
     if not last:
         here = jnp.where((lane < LOCAL) == (odd == 0), piece, pltpu.roll(piece, LOCAL, 1))
-        local_ref[...] = here[0:1]
+        local_ref[...] = jnp.broadcast_to(here[0:1], (2 * TILE, TILE))
         return
     state.wait()
     outs = []
@@ -482,11 +493,12 @@
     else:
         out_shape = (
             jax.ShapeDtypeStruct((1, COARSE), jnp.float32),
-            jax.ShapeDtypeStruct((1, TILE), jnp.float32),
+            jax.ShapeDtypeStruct((2 * TILE, TILE), jnp.float32),
         )
         out_specs = (VMEM, VMEM)
     return pl.pallas_call(
         functools.partial(chain_kernel, last),
+        cost_estimate=cost(5),
         out_shape=out_shape,
         in_specs=[SMEM, VMEM] + [HBM] * (12 + last),
         out_specs=out_specs,
@@ -497,7 +509,7 @@
         ]
         + [pltpu.VMEM((ROWS, COLS), jnp.float32), pltpu.SemaphoreType.DMA] * last,
         compiler_params=pltpu.CompilerParams(vmem_limit_bytes=32 << 20),
-    )(ids, got, other, *whole, *halved, *([previous] * last))
+    )(ids, got, *in_hbm(other, *whole, *halved, *([previous] * last)))
 
 
 def exchanged(block):
@@ -530,13 +542,15 @@
     lower = shifted(jnp.concatenate([state[:wide], source[:wide]], axis=0), 0, -1)
 
     product, half, columns = pair_product(ids, own_map, other_map, state)
+    product, half, columns, upper, lower = lax.optimization_barrier((product, half, columns, upper, lower))
     near = along(product)
     far_same = across(half)
     columns = shifted(columns, -1)
 
     finished, means = fine_sweep(ids, tile_class, coeff_sets, (upper, state, source, lower))
-    previous = shifted(finished, 1)
-
+    near, far_same, columns, means, finished = lax.optimization_barrier(
+        (near, far_same, columns, means, finished)
+    )
     near_half = lax.dynamic_slice(near, (core * HALF, 0), (HALF, COARSE))
     far = across(near)
     near_second = along(near_half)
@@ -544,13 +558,17 @@
 
     got = exchanged(message(ids, means, columns[LOCAL : LOCAL + 1, :TILE], columns))
 
+    got, far, near_second, far_second, finished = lax.optimization_barrier(
+        (got, far, near_second, far_second, finished)
+    )
+    previous = shifted(finished, 1)
     whole = [near, swapped(near), far, swapped(far), product]
     halved = []
     for part in (near_second, far_same, far_second):
         halved += [part, swapped(part)]
     correction, local = chain(ids, got, other_map, whole, halved)
 
-    base = means + shifted(local, -1)
+    base = means + shifted(local, -1)[:1]
     finished, means = fine_sweep(ids, tile_class, coeff_sets, (previous, upper, source, lower), correction)
     previous = shifted(finished, 1)
     got = exchanged(message(ids, means, base, columns))

time: 146 us -> 122 us (0.84)
  waiting for transfers between devices: 27.2 us -> 10.6 us
  starting transfers between devices: 39.5 us -> 23.6 us
  blocking collectives: 38.1 us -> 42.2 us
  Pallas kernels: 34.5 us -> 37.8 us
    ppermute x11, starting transfers between devices: 30.3 us -> 13.4 us  [moved(): return lax.ppermute(value, ('tm', 'space'), pairs)]
    ppermute x11, waiting for transfers between devices: 18.8 us -> 6.2 us  [moved(): return lax.ppermute(value, ('tm', 'space'), pairs)]
    all_to_all x2, blocking collectives: 38.1 us -> 42.2 us  [exchanged(): lax.all_to_all(block, ('tm', 'space'), 0, 0, tiled=True)]
    ppermute x6, waiting for transfers between devices: 8.43 us -> 4.44 us  [shifted(): return lax.ppermute(value, ('tm', 'space'), pairs)]
    pallas_call x7, Pallas kernels: 34.5 us -> 37.8 us  [the longest x2 20.6 us: fine_sweep(): pl.pallas_call(functools.partial(fine_kernel, halo, corrected), cost_esti...]
    unnamed x36 -> x38, local copies, waits for them, and re-layouts: 5.39 us -> 5.6 us
  transfers between devices with their start and end apart: 17 -> 17, of which waited for: 6 -> 5; matrix products, arithmetic and copies ran while one was open for 0% -> 1% of each run, Pallas kernels for 11% -> 17%
where the time goes in v3:
time: 122 us
  blocking collectives  42.2 us (35%)
  Pallas kernels  37.8 us (31%)
  starting transfers between devices  23.6 us (19%)
  waiting for transfers between devices  10.6 us (9%)
  local copies, waits for them, and re-layouts  6.76 us (6%)
    all_to_all x2, blocking collectives, exchanged(): lax.all_to_all(block, ('tm', 'space'), 0, 0, tiled=True)  42.2 us
    pallas_call x2, Pallas kernels, fine_sweep(): pl.pallas_call(functools.partial(fine_kernel, halo, corrected), cost_esti...  20.6 us
    ppermute x11, starting transfers between devices, moved(): return lax.ppermute(value, ('tm', 'space'), pairs)  13.4 us
    pallas_call x2, Pallas kernels, chain(): pl.pallas_call(functools.partial(chain_kernel, last), cost_estimate=cost(...  12.2 us
    ppermute x6, starting transfers between devices, shifted(): return lax.ppermute(value, ('tm', 'space'), pairs)  10.2 us
    ppermute x11, waiting for transfers between devices, moved(): return lax.ppermute(value, ('tm', 'space'), pairs)  6.2 us
    unnamed x38, local copies, waits for them, and re-layouts  5.6 us
    ppermute x6, waiting for transfers between devices, shifted(): return lax.ppermute(value, ('tm', 'space'), pairs)  4.44 us
  transfers between devices with their start and end apart: 17, of which 5 were waited for; matrix products, arithmetic and copies ran while one was open for 1% of the time, Pallas kernels for 17%

profile of v3, /device:TPU:1, one launch (start us, length us, event | category | flops | bytes accessed | tf_op | source)
XLA Modules:
  0.0 121.6 jit_solution(10897041006015264324)
XLA Ops:
  0.0 1.4 %collective-permute-start = (f32[512,512]{1,0:T(8,128)}, f32[512,512]{1,0:T(8,128)S(1)}, u32[]{:S(2)}, u32[]{:S(2)}) collective-permute-start(f32[512,512]{1,0:T(8,128)} %bitcast.28), channel_id=1, source_target_pairs={{0,8},{1,9},{2,10},{3,11},{4,12},{5,13},{6,14},{7,15},{8,0},{9,1},... | collective-permute-start | bytes 3145736 | tf_op jit(solution)/shard_map/ppermute | solution.py:43
  1.4 1.1 slice_bitcast_fusion
  2.6 1.4 %collective-permute-start.1 = (f32[32,2048]{1,0:T(8,128)S(1)}, f32[32,2048]{1,0:T(8,128)S(1)}, u32[]{:S(2)}, u32[]{:S(2)}) collective-permute-start(f32[32,2048]{1,0:T(8,128)S(1)} %pad_maximum_fusion), channel_id=1, source_target_pairs={{0,1},{1,2},{2,3},{3,4},{4,5},{5,6},{6,7},{7,0},{8,9},{9,10},{10,1... | collective-permute-start | bytes 786440 | tf_op jit(solution)/shard_map/ppermute | solution.py:52
  4.0 4.7 %collective-permute-start.2 = (f32[32,2048]{1,0:T(8,128)S(1)}, f32[32,2048]{1,0:T(8,128)S(1)}, u32[]{:S(2)}, u32[]{:S(2)}) collective-permute-start(f32[32,2048]{1,0:T(8,128)S(1)} %pad_maximum_fusion.1), channel_id=1, source_target_pairs={{0,7},{1,0},{2,1},{3,2},{4,3},{5,4},{6,5},{7,6},{8,15},{9,8},{10,9... | collective-permute-start | bytes 786440 | tf_op jit(solution)/shard_map/ppermute | solution.py:52
  8.7 1.0 copy-done.3
  9.7 3.5 %shard_map.55 = (f32[512,512]{1,0:T(8,128)S(1)}, f32[256,512]{1,0:T(8,128)S(1)}, f32[72,512]{1,0:T(8,128)S(1)}) custom-call(s32[4]{0:T(128)S(1)} %pad_add_fusion.ids_ref, f32[512,512]{1,0:T(8,128)} %bitcast.29, f32[512,512]{1,0:T(8,128)} %copy-done.3, f32[128,2048]{1,0:T(8,128)} %bitcast.24), custom_call_target="tpu_custom_call" | custom-call | bytes 10800000 | tf_op jit(solution)/shard_map/pallas_call | solution.py:127
  13.2 2.0 %collective-permute-done.1.refs_0_.refs_2_ = f32[32,2048]{1,0:T(8,128)S(1)} collective-permute-done((f32[32,2048]{1,0:T(8,128)S(1)}, f32[32,2048]{1,0:T(8,128)S(1)}, u32[]{:S(2)}, u32[]{:S(2)}) %collective-permute-start.1) | collective-permute-done | bytes 262176 | tf_op jit(solution)/shard_map/ppermute | solution.py:52
  15.2 2.8 %collective-permute-start.3 = (f32[512,512]{1,0:T(8,128)S(1)}, f32[512,512]{1,0:T(8,128)S(1)}, u32[]{:S(2)}, u32[]{:S(2)}) collective-permute-start(f32[512,512]{1,0:T(8,128)S(1)} %get-tuple-element.32.refs_4_), channel_id=1, source_target_pairs={{0,16},{1,17},{2,18},{3,19},{4,20},{5,21},{6,22},{7,23},{8,56},{9,... | collective-permute-start | bytes 3145736 | tf_op jit(solution)/shard_map/ppermute | solution.py:43
  18.0 2.8 %collective-permute-start.4 = (f32[256,512]{1,0:T(8,128)S(1)}, f32[256,512]{1,0:T(8,128)S(1)}, u32[]{:S(2)}, u32[]{:S(2)}) collective-permute-start(f32[256,512]{1,0:T(8,128)S(1)} %get-tuple-element.33), channel_id=1, source_target_pairs={{0,64},{1,65},{2,66},{3,67},{4,68},{5,69},{6,70},{7,71},{8,76},{9,... | collective-permute-start | bytes 1572872 | tf_op jit(solution)/shard_map/ppermute | solution.py:43
  20.9 10.5 %shard_map.56 = (f32[144,2048]{1,0:T(8,128)S(1)}, f32[1,128]{1,0:T(1,128)S(1)}) custom-call(s32[4]{0:T(128)S(1)} %pad_add_fusion.ids_ref, s32[8,16]{1,0:T(8,128)S(1)} %copy-done.1, f32[3,8]{1,0:T(4,128)S(1)} %copy-done.2, f32[32,2048]{1,0:T(8,128)} %copy-done.17, f32[128,2048]{1,0:T(8,128)} %bitcast.25, f32[128,2048]{1,0:T(8,128)} %bitcast.26, ...), custom_call_target="tpu_custom_call" | custom-call | bytes 36000000 | tf_op jit(solution)/shard_map/pallas_call | solution.py:289
  31.4 0.8 copy-done.8
  32.3 1.9 %collective-permute-start.6 = (f32[512,512]{1,0:T(8,128)S(1)}, f32[512,512]{1,0:T(8,128)S(1)}, u32[]{:S(2)}, u32[]{:S(2)}) collective-permute-start(f32[512,512]{1,0:T(8,128)S(1)} %collective-permute-done.3.refs_0_), channel_id=1, source_target_pairs={{0,64},{1,65},{2,66},{3,67},{4,68},{5,69},{6,70},{7,71},{8,76},{9,... | collective-permute-start | bytes 3145736 | tf_op jit(solution)/shard_map/ppermute | solution.py:43
  34.2 3.0 %collective-permute-start.8 = (f32[256,512]{1,0:T(8,128)S(1)}, f32[256,512]{1,0:T(8,128)S(1)}, u32[]{:S(2)}, u32[]{:S(2)}) collective-permute-start(f32[256,512]{1,0:T(8,128)S(1)} %constant_dynamic-slice_fusion), channel_id=1, source_target_pairs={{0,80},{1,81},{2,82},{3,83},{4,84},{5,85},{6,86},{7,87},{8,124},{9... | collective-permute-start | bytes 1572872 | tf_op jit(solution)/shard_map/ppermute | solution.py:43
  37.5 0.7 shard_map.57
  38.2 19.8 %all_to_all.10 = f32[128,1,640]{2,1,0:T(1,128)S(1)} all-to-all(f32[128,1,640]{2,1,0:T(1,128)S(1)} %bitcast.23), channel_id=1, replica_groups=mesh['tm'=16,'space'=8] {'tm','space'}, dimensions={0} | all-to-all | bytes 655360 | tf_op jit(solution)/shard_map/all_to_all | solution.py:517
  58.1 1.3 %collective-permute-start.14 = (f32[144,2048]{1,0:T(8,128)S(1)}, f32[144,2048]{1,0:T(8,128)S(1)}, u32[]{:S(2)}, u32[]{:S(2)}) collective-permute-start(f32[144,2048]{1,0:T(8,128)S(1)} %get-tuple-element.49), channel_id=1, source_target_pairs={{0,8},{1,9},{2,10},{3,11},{4,12},{5,13},{6,14},{7,15},{8,16},{9,17... | collective-permute-start | bytes 3538952 | tf_op jit(solution)/shard_map/ppermute | solution.py:52
  59.4 0.5 collective-permute-start.12
  60.5 3.3 %collective-permute-done.12.refs_8_ = f32[256,512]{1,0:T(8,128)S(1)} collective-permute-done((f32[256,512]{1,0:T(8,128)S(1)}, f32[256,512]{1,0:T(8,128)S(1)}, u32[]{:S(2)}, u32[]{:S(2)}) %collective-permute-start.12) | collective-permute-done | bytes 524320 | tf_op jit(solution)/shard_map/ppermute | solution.py:43
  63.9 2.1 %collective-permute-done.11.refs_6_ = f32[256,512]{1,0:T(8,128)S(1)} collective-permute-done((f32[256,512]{1,0:T(8,128)S(1)}, f32[256,512]{1,0:T(8,128)S(1)}, u32[]{:S(2)}, u32[]{:S(2)}) %collective-permute-start.11) | collective-permute-done | bytes 524320 | tf_op jit(solution)/shard_map/ppermute | solution.py:43
  66.0 0.7 collective-permute-done.13.refs_10_
  66.9 0.7 copy-done.14
  67.6 1.0 copy-done.7
  68.6 5.6 %shard_map.58 = (f32[1,512]{1,0:T(1,128)S(1)}, f32[256,128]{1,0:T(8,128)S(1)}) custom-call(s32[4]{0:T(128)S(1)} %pad_add_fusion.ids_ref, f32[640,128]{1,0:T(8,128)S(1)} %bitcast.20, f32[512,512]{1,0:T(8,128)} %copy-done.3, f32[512,512]{1,0:T(8,128)} %copy-done.4, f32[512,512]{1,0:T(8,128)} %copy-done.6, f32[512,512]{1,0:T(8,128)} %copy-done.5, ...), custom_call_target="tpu_custom_call" | custom-call | bytes 18000000 | tf_op jit(solution)/shard_map/pallas_call | solution.py:499
  74.2 1.0 copy-done.15
  75.2 10.1 %shard_map.59 = (f32[128,2048]{1,0:T(8,128)S(1)}, f32[1,128]{1,0:T(1,128)S(1)}) custom-call(s32[4]{0:T(128)S(1)} %pad_add_fusion.ids_ref, s32[8,16]{1,0:T(8,128)S(1)} %copy-done.1, f32[3,8]{1,0:T(4,128)S(1)} %copy-done.2, f32[1,512]{1,0:T(1,128)S(1)} %get-tuple-element.48.refs_0_, f32[144,2048]{1,0:T(8,128)} %copy-done.15, f32[32,2048]{1,0:T(8,128)} %copy-done.17, ...), custom_call_target="tpu_custom_call" | custom-call | bytes 36000000 | tf_op jit(solution)/shard_map/pallas_call | solution.py:289
  85.4 0.9 collective-permute-start.16
  86.3 2.0 %collective-permute-start.15 = (f32[256,128]{1,0:T(8,128)S(1)}, f32[256,128]{1,0:T(8,128)S(1)}, u32[]{:S(2)}, u32[]{:S(2)}) collective-permute-start(f32[256,128]{1,0:T(8,128)S(1)} %get-tuple-element.51), channel_id=1, source_target_pairs={{0,120},{1,121},{2,122},{3,123},{4,124},{5,125},{6,126},{7,127},{8... | collective-permute-start | bytes 393224 | tf_op jit(solution)/shard_map/ppermute | solution.py:52
  88.2 2.4 %collective-permute-done.15 = f32[256,128]{1,0:T(8,128)S(1)} collective-permute-done((f32[256,128]{1,0:T(8,128)S(1)}, f32[256,128]{1,0:T(8,128)S(1)}, u32[]{:S(2)}, u32[]{:S(2)}) %collective-permute-start.15) | collective-permute-done | bytes 131104 | tf_op jit(solution)/shard_map/ppermute | solution.py:52
  90.7 0.7 shard_map.60
  91.4 22.4 %all_to_all.11 = f32[128,1,640]{2,1,0:T(1,128)S(1)} all-to-all(f32[128,1,640]{2,1,0:T(1,128)S(1)} %bitcast.22), channel_id=1, replica_groups=mesh['tm'=16,'space'=8] {'tm','space'}, dimensions={0} | all-to-all | bytes 655360 | tf_op jit(solution)/shard_map/all_to_all | solution.py:517
  113.8 1.0 copy-done.16
  114.8 6.6 %shard_map.61 = f32[128,2048]{1,0:T(8,128)} custom-call(s32[4]{0:T(128)S(1)} %pad_add_fusion.ids_ref, f32[640,128]{1,0:T(8,128)S(1)} %bitcast.21, f32[512,512]{1,0:T(8,128)} %copy-done.3, f32[512,512]{1,0:T(8,128)} %copy-done.4, f32[512,512]{1,0:T(8,128)} %copy-done.6, f32[512,512]{1,0:T(8,128)} %copy-done.5, f32[512,512]{1,0:T(8,128)} %copy-done.7, ...), custom_call_target="tpu_custom_call" | custom-call | bytes 18000000 | tf_op jit(solution)/shard_map/pallas_call | solution.py:499
  (56 shorter events, 1.2 us)
Async XLA Ops:
  0.0 8.7 %collective-permute-start = (f32[512,512]{1,0:T(8,128)}, f32[512,512]{1,0:T(8,128)S(1)}, u32[]{:S(2)}, u32[]{:S(2)}) collective-permute-start(f32[512,512]{1,0:T(8,128)} %bitcast.28), channel_id=1, source_target_pairs={{0,8},{1,9},{2,10},{3,11},{4,12},{5,13},{6,14},{7,15},{8,0},{9,1},... | collective-permute-start | bytes 3145736 | tf_op jit(solution)/shard_map/ppermute | solution.py:43
  2.6 12.6 %collective-permute-start.1 = (f32[32,2048]{1,0:T(8,128)S(1)}, f32[32,2048]{1,0:T(8,128)S(1)}, u32[]{:S(2)}, u32[]{:S(2)}) collective-permute-start(f32[32,2048]{1,0:T(8,128)S(1)} %pad_maximum_fusion), channel_id=1, source_target_pairs={{0,1},{1,2},{2,3},{3,4},{4,5},{5,6},{6,7},{7,0},{8,9},{9,10},{10,1... | collective-permute-start | bytes 786440 | tf_op jit(solution)/shard_map/ppermute | solution.py:52
  4.0 11.2 %collective-permute-start.2 = (f32[32,2048]{1,0:T(8,128)S(1)}, f32[32,2048]{1,0:T(8,128)S(1)}, u32[]{:S(2)}, u32[]{:S(2)}) collective-permute-start(f32[32,2048]{1,0:T(8,128)S(1)} %pad_maximum_fusion.1), channel_id=1, source_target_pairs={{0,7},{1,0},{2,1},{3,2},{4,3},{5,4},{6,5},{7,6},{8,15},{9,8},{10,9... | collective-permute-start | bytes 786440 | tf_op jit(solution)/shard_map/ppermute | solution.py:52
  8.7 1.0 copy-start.3
  9.7 11.1 %copy-start.1 = (s32[8,16]{1,0:T(8,128)S(1)}, s32[8,16]{1,0:T(8,128)}, u32[]{:S(2)}) copy-start(s32[8,16]{1,0:T(8,128)} %class_ref.3) | copy-start | bytes 1540
  9.7 11.1 %copy-start.2 = (f32[3,8]{1,0:T(4,128)S(1)}, f32[3,8]{1,0:T(4,128)}, u32[]{:S(2)}) copy-start(f32[3,8]{1,0:T(4,128)} %sets_ref.3) | copy-start | bytes 292
  13.2 18.2 %copy-start = (f32[512,512]{1,0:T(8,128)}, f32[512,512]{1,0:T(8,128)S(1)}, u32[]{:S(2)}) copy-start(f32[512,512]{1,0:T(8,128)S(1)} %get-tuple-element.32.refs_4_) | copy-start | bytes 3145732
  15.2 5.6 %copy-start.17 = (f32[32,2048]{1,0:T(8,128)}, f32[32,2048]{1,0:T(8,128)S(1)}, u32[]{:S(2)}) copy-start(f32[32,2048]{1,0:T(8,128)S(1)} %collective-permute-done.1.refs_0_.refs_2_) | copy-start | bytes 786436
  15.2 5.6 %copy-start.18 = (f32[32,2048]{1,0:T(8,128)}, f32[32,2048]{1,0:T(8,128)S(1)}, u32[]{:S(2)}) copy-start(f32[32,2048]{1,0:T(8,128)S(1)} %collective-permute-done.2.refs_3_.refs_4_) | copy-start | bytes 786436
  15.2 16.2 %collective-permute-start.3 = (f32[512,512]{1,0:T(8,128)S(1)}, f32[512,512]{1,0:T(8,128)S(1)}, u32[]{:S(2)}, u32[]{:S(2)}) collective-permute-start(f32[512,512]{1,0:T(8,128)S(1)} %get-tuple-element.32.refs_4_), channel_id=1, source_target_pairs={{0,16},{1,17},{2,18},{3,19},{4,20},{5,21},{6,22},{7,23},{8,56},{9,... | collective-permute-start | bytes 3145736 | tf_op jit(solution)/shard_map/ppermute | solution.py:43
  18.0 13.4 %collective-permute-start.4 = (f32[256,512]{1,0:T(8,128)S(1)}, f32[256,512]{1,0:T(8,128)S(1)}, u32[]{:S(2)}, u32[]{:S(2)}) collective-permute-start(f32[256,512]{1,0:T(8,128)S(1)} %get-tuple-element.33), channel_id=1, source_target_pairs={{0,64},{1,65},{2,66},{3,67},{4,68},{5,69},{6,70},{7,71},{8,76},{9,... | collective-permute-start | bytes 1572872 | tf_op jit(solution)/shard_map/ppermute | solution.py:43
  20.9 10.5 %collective-permute-start.5 = (f32[72,512]{1,0:T(8,128)S(1)}, f32[72,512]{1,0:T(8,128)S(1)}, u32[]{:S(2)}, u32[]{:S(2)}) collective-permute-start(f32[72,512]{1,0:T(8,128)S(1)} %get-tuple-element.34), channel_id=1, source_target_pairs={{0,120},{1,121},{2,122},{3,123},{4,124},{5,125},{6,126},{7,127},{8... | collective-permute-start | bytes 442376 | tf_op jit(solution)/shard_map/ppermute | solution.py:52
  31.4 35.4 %copy-start.4 = (f32[512,512]{1,0:T(8,128)}, f32[512,512]{1,0:T(8,128)S(1)}, u32[]{:S(2)}) copy-start(f32[512,512]{1,0:T(8,128)S(1)} %collective-permute-done.3.refs_0_) | copy-start | bytes 3145732
  32.3 25.8 %collective-permute-start.6 = (f32[512,512]{1,0:T(8,128)S(1)}, f32[512,512]{1,0:T(8,128)S(1)}, u32[]{:S(2)}, u32[]{:S(2)}) collective-permute-start(f32[512,512]{1,0:T(8,128)S(1)} %collective-permute-done.3.refs_0_), channel_id=1, source_target_pairs={{0,64},{1,65},{2,66},{3,67},{4,68},{5,69},{6,70},{7,71},{8,76},{9,... | collective-permute-start | bytes 3145736 | tf_op jit(solution)/shard_map/ppermute | solution.py:43
  34.2 25.3 %copy-start.9 = (f32[256,512]{1,0:T(8,128)S(1)}, f32[256,512]{1,0:T(8,128)}, u32[]{:S(2)}) copy-start(f32[256,512]{1,0:T(8,128)} %copy-done.8) | copy-start | bytes 1572868
  34.2 23.8 %collective-permute-start.8 = (f32[256,512]{1,0:T(8,128)S(1)}, f32[256,512]{1,0:T(8,128)S(1)}, u32[]{:S(2)}, u32[]{:S(2)}) collective-permute-start(f32[256,512]{1,0:T(8,128)S(1)} %constant_dynamic-slice_fusion), channel_id=1, source_target_pairs={{0,80},{1,81},{2,82},{3,83},{4,84},{5,85},{6,86},{7,87},{8,124},{9... | collective-permute-start | bytes 1572872 | tf_op jit(solution)/shard_map/ppermute | solution.py:43
  37.2 20.8 %collective-permute-start.7 = (f32[256,512]{1,0:T(8,128)S(1)}, f32[256,512]{1,0:T(8,128)S(1)}, u32[]{:S(2)}, u32[]{:S(2)}) collective-permute-start(f32[256,512]{1,0:T(8,128)S(1)} %constant_dynamic-slice_fusion), channel_id=1, source_target_pairs={{0,16},{1,17},{2,18},{3,19},{4,20},{5,21},{6,22},{7,23},{8,56},{9,... | collective-permute-start | bytes 1572872 | tf_op jit(solution)/shard_map/ppermute | solution.py:43
  58.1 8.7 %copy-start.10 = (f32[256,512]{1,0:T(8,128)}, f32[256,512]{1,0:T(8,128)S(1)}, u32[]{:S(2)}) copy-start(f32[256,512]{1,0:T(8,128)S(1)} %collective-permute-done.8.refs_9_) | copy-start | bytes 1572868
  58.1 8.7 %copy-start.11 = (f32[256,512]{1,0:T(8,128)}, f32[256,512]{1,0:T(8,128)S(1)}, u32[]{:S(2)}) copy-start(f32[256,512]{1,0:T(8,128)S(1)} %collective-permute-done.7.refs_5_) | copy-start | bytes 1572868
  58.1 8.7 %copy-start.5 = (f32[512,512]{1,0:T(8,128)}, f32[512,512]{1,0:T(8,128)S(1)}, u32[]{:S(2)}) copy-start(f32[512,512]{1,0:T(8,128)S(1)} %collective-permute-done.6.refs_2_) | copy-start | bytes 3145732
  58.1 16.1 %collective-permute-start.14 = (f32[144,2048]{1,0:T(8,128)S(1)}, f32[144,2048]{1,0:T(8,128)S(1)}, u32[]{:S(2)}, u32[]{:S(2)}) collective-permute-start(f32[144,2048]{1,0:T(8,128)S(1)} %get-tuple-element.49), channel_id=1, source_target_pairs={{0,8},{1,9},{2,10},{3,11},{4,12},{5,13},{6,14},{7,15},{8,16},{9,17... | collective-permute-start | bytes 3538952 | tf_op jit(solution)/shard_map/ppermute | solution.py:52
  59.4 4.5 %collective-permute-start.9 = (f32[512,512]{1,0:T(8,128)S(1)}, f32[512,512]{1,0:T(8,128)S(1)}, u32[]{:S(2)}, u32[]{:S(2)}) collective-permute-start(f32[512,512]{1,0:T(8,128)S(1)} %collective-permute-done.3.refs_0_), channel_id=1, source_target_pairs={{0,8},{1,9},{2,10},{3,11},{4,12},{5,13},{6,14},{7,15},{8,0},{9,1},... | collective-permute-start | bytes 3145736 | tf_op jit(solution)/shard_map/ppermute | solution.py:43
  59.4 4.4 %collective-permute-start.12 = (f32[256,512]{1,0:T(8,128)S(1)}, f32[256,512]{1,0:T(8,128)S(1)}, u32[]{:S(2)}, u32[]{:S(2)}) collective-permute-start(f32[256,512]{1,0:T(8,128)S(1)} %copy-done.9), channel_id=1, source_target_pairs={{0,8},{1,9},{2,10},{3,11},{4,12},{5,13},{6,14},{7,15},{8,0},{9,1},... | collective-permute-start | bytes 1572872 | tf_op jit(solution)/shard_map/ppermute | solution.py:43
  59.9 6.8 %collective-permute-start.10 = (f32[512,512]{1,0:T(8,128)S(1)}, f32[512,512]{1,0:T(8,128)S(1)}, u32[]{:S(2)}, u32[]{:S(2)}) collective-permute-start(f32[512,512]{1,0:T(8,128)S(1)} %collective-permute-done.6.refs_2_), channel_id=1, source_target_pairs={{0,8},{1,9},{2,10},{3,11},{4,12},{5,13},{6,14},{7,15},{8,0},{9,1},... | collective-permute-start | bytes 3145736 | tf_op jit(solution)/shard_map/ppermute | solution.py:43
  59.9 6.1 %collective-permute-start.11 = (f32[256,512]{1,0:T(8,128)S(1)}, f32[256,512]{1,0:T(8,128)S(1)}, u32[]{:S(2)}, u32[]{:S(2)}) collective-permute-start(f32[256,512]{1,0:T(8,128)S(1)} %collective-permute-done.7.refs_5_), channel_id=1, source_target_pairs={{0,8},{1,9},{2,10},{3,11},{4,12},{5,13},{6,14},{7,15},{8,0},{9,1},... | collective-permute-start | bytes 1572872 | tf_op jit(solution)/shard_map/ppermute | solution.py:43
  63.8 3.0 %copy-start.12 = (f32[256,512]{1,0:T(8,128)}, f32[256,512]{1,0:T(8,128)S(1)}, u32[]{:S(2)}) copy-start(f32[256,512]{1,0:T(8,128)S(1)} %collective-permute-done.12.refs_8_) | copy-start | bytes 1572868
  63.8 3.0 %collective-permute-start.13 = (f32[256,512]{1,0:T(8,128)S(1)}, f32[256,512]{1,0:T(8,128)S(1)}, u32[]{:S(2)}, u32[]{:S(2)}) collective-permute-start(f32[256,512]{1,0:T(8,128)S(1)} %collective-permute-done.8.refs_9_), channel_id=1, source_target_pairs={{0,8},{1,9},{2,10},{3,11},{4,12},{5,13},{6,14},{7,15},{8,0},{9,1},... | collective-permute-start | bytes 1572872 | tf_op jit(solution)/shard_map/ppermute | solution.py:43
  63.9 2.9 %copy-start.6 = (f32[512,512]{1,0:T(8,128)}, f32[512,512]{1,0:T(8,128)S(1)}, u32[]{:S(2)}) copy-start(f32[512,512]{1,0:T(8,128)S(1)} %collective-permute-done.9.refs_1_) | copy-start | bytes 3145732
  74.2 1.0 copy-start.15
  85.4 28.5 %collective-permute-start.16 = (f32[128,2048]{1,0:T(8,128)S(1)}, f32[128,2048]{1,0:T(8,128)S(1)}, u32[]{:S(2)}, u32[]{:S(2)}) collective-permute-start(f32[128,2048]{1,0:T(8,128)S(1)} %get-tuple-element.52), channel_id=1, source_target_pairs={{0,8},{1,9},{2,10},{3,11},{4,12},{5,13},{6,14},{7,15},{8,16},{9,17... | collective-permute-start | bytes 3145736 | tf_op jit(solution)/shard_map/ppermute | solution.py:52
  86.3 4.4 %collective-permute-start.15 = (f32[256,128]{1,0:T(8,128)S(1)}, f32[256,128]{1,0:T(8,128)S(1)}, u32[]{:S(2)}, u32[]{:S(2)}) collective-permute-start(f32[256,128]{1,0:T(8,128)S(1)} %get-tuple-element.51), channel_id=1, source_target_pairs={{0,120},{1,121},{2,122},{3,123},{4,124},{5,125},{6,126},{7,127},{8... | collective-permute-start | bytes 393224 | tf_op jit(solution)/shard_map/ppermute | solution.py:52
  113.8 1.0 copy-start.16
  (4 other events, 3.4 us)

commit v4 on v3

v4 whole, which is shorter than its diff:
```python
import functools

import jax
import jax.numpy as jnp
from jax import lax
from jax.experimental import pallas as pl
from jax.experimental.pallas import tpu as pltpu
from jax.sharding import PartitionSpec as P

TILE = 128
BLK = 64
STEPS = 8
ROWS = 128
COLS = 2048
COARSE = 512
HALF = COARSE // 2
TILES = COLS // TILE
LOCAL = 64
PIECES = 5
STEP = 0.6

HIGHEST = lax.Precision.HIGHEST
HBM = pl.BlockSpec(memory_space=pltpu.HBM)
ANY = pl.BlockSpec(memory_space=pl.ANY)
SMEM = pl.BlockSpec(memory_space=pltpu.SMEM)
VMEM = pl.BlockSpec(memory_space=pltpu.VMEM)


def place(device):
    tm, space = divmod(device, 8)
    z_lo, rest = divmod(tm, 8)
    y, core = divmod(rest, 2)
    z_hi, x = divmod(space, 4)
    return x, y, 2 * z_hi + z_lo, core


def device_at(x, y, z, core):
    x, y, z, core = x % 4, y % 4, z % 4, core % 2
    return ((z % 2) * 8 + y * 2 + core) * 8 + (z // 2) * 4 + x


def moved(value, route):
    pairs = [(i, device_at(*route(*place(i)))) for i in range(128)]
    return lax.ppermute(value, ("tm", "space"), pairs)


def shifted(value, windows, strips=0):
    pairs = [
        (tm * 8 + sp, (tm + windows) % 16 * 8 + (sp + strips) % 8)
        for tm in range(16)
        for sp in range(8)
    ]
    return lax.ppermute(value, ("tm", "space"), pairs)


def cost(micros):
    return pl.CostEstimate(flops=0, transcendentals=0, bytes_accessed=int(micros * 3.6e6))


def in_hbm(*values):
    return [pltpu.with_memory_space_constraint(value, pltpu.HBM) for value in values]


def position():
    window = lax.axis_index("tm")
    pair = window // 2
    return lax.axis_index("space"), lax.rem(window, 2), pair, lax.rem(pair, 4)


def iota(shape, axis):
    return lax.broadcasted_iota(jnp.int32, shape, axis)


def packed_means(sums):
    lane = iota((32, TILE), 1)
    row = iota((32, TILE), 0)
    low = jnp.sum(jnp.where(lane < BLK, sums, 0.0), axis=1, keepdims=True)
    high = jnp.sum(jnp.where(lane < BLK, 0.0, sums), axis=1, keepdims=True)
    slot = lane & (LOCAL - 1)
    spread = jnp.where(slot == 2 * row, low, 0.0) + jnp.where(slot == 2 * row + 1, high, 0.0)
    return jnp.sum(spread, axis=0, keepdims=True) * (1.0 / (BLK * BLK))


def fill_weights(strip, class_ref, sets_ref, coef_ref):
    sub = iota((8, TILE), 0)
    strips = (lax.rem(strip + 7, 8), strip, lax.rem(strip + 1, 8))

    def weights(row, k):
        label = class_ref[row, k]
        spread, along_cols, along_rows = sets_ref[0, label], sets_ref[1, label], sets_ref[2, label]
        left = STEP * (spread + jnp.maximum(along_cols, 0.0))
        right = STEP * (spread - jnp.minimum(along_cols, 0.0))
        above = STEP * (spread + jnp.maximum(along_rows, 0.0))
        below = STEP * (spread - jnp.minimum(along_rows, 0.0))
        return 1.0 - (left + right + above + below), left, right, above, below

    for k in range(TILES):
        upper, inner, lower = (weights(row, k) for row in strips)
        for w in range(5):
            value = jnp.full((8, TILE), inner[w], jnp.float32)
            with_upper = jnp.where(sub == 0, upper[w], value)
            coef_ref[k, w] = value
            coef_ref[k, 5 + w] = with_upper
            coef_ref[k, 10 + w] = jnp.where(sub == 7, lower[w], value)
            coef_ref[k, 15 + w] = jnp.where(sub == 7, lower[w], with_upper)


def pair_kernel(class_ref, sets_ref, own_ref, other_ref, u_ref, q_ref, half_ref, columns_ref, coef_ref, *scratch):
    late, early, u, sums_ref, columns, sems = scratch
    strip, core, _, _ = position()
    state = pltpu.make_async_copy(u_ref, u, sems.at[2])

    def both(first, second):
        a = pltpu.make_async_copy(first, late, sems.at[0])
        b = pltpu.make_async_copy(second, early, sems.at[1])
        a.start()
        b.start()
        state.start()
        a.wait()
        b.wait()

    @pl.when(core == 1)
    def _():
        both(own_ref, other_ref)

    @pl.when(core == 0)
    def _():
        both(other_ref, own_ref)

    fill_weights(strip, class_ref, sets_ref, coef_ref)

    def split(value):
        big = value.astype(jnp.bfloat16)
        return big, (value - big.astype(jnp.float32)).astype(jnp.bfloat16)

    def times(a, b):
        return jnp.dot(a, b, preferred_element_type=jnp.float32)

    early_big, early_small = split(early[...])
    for part in range(2):
        rows = slice(part * HALF, (part + 1) * HALF)
        big, small = split(late[rows, :])
        q_ref[rows, :] = times(big, early_big) + (times(big, early_small) + times(small, early_big))
    half_ref[...] = q_ref[pl.ds(pl.multiple_of(core * HALF, HALF), HALF), :]
    cols = pl.ds(pl.multiple_of(strip // 2 * TILE, TILE), TILE)
    wide = jnp.where(core == 1, late[:, cols], q_ref[:, cols])
    turned = jnp.transpose(wide)
    columns[0:LOCAL, :] = jnp.where(lax.rem(strip, 2) == 1, turned[LOCAL:], turned[:LOCAL])
    state.wait()
    for k in range(TILES):
        cols = slice(k * TILE, (k + 1) * TILE)
        for br in range(2):
            part = u[br * BLK : (br + 1) * BLK, cols]
            sums_ref[br * TILES + k : br * TILES + k + 1, :] = jnp.sum(part, axis=0, keepdims=True)
    columns[LOCAL:, :] = jnp.zeros((8, COARSE), jnp.float32)
    columns[LOCAL:, 0:TILE] = jnp.broadcast_to(packed_means(sums_ref[...]), (8, TILE))
    done = pltpu.make_async_copy(columns, columns_ref, sems.at[0])
    done.start()
    done.wait()


def pair_product(tile_class, coeff_sets, own, other, state):
    square = pltpu.VMEM((COARSE, COARSE), jnp.float32)
    return pl.pallas_call(
        pair_kernel,
        cost_estimate=cost(3),
        out_shape=(
            jax.ShapeDtypeStruct((COARSE, COARSE), jnp.float32),
            jax.ShapeDtypeStruct((HALF, COARSE), jnp.float32),
            pltpu.HBM((LOCAL + 8, COARSE), jnp.float32),
            jax.ShapeDtypeStruct((TILES, 20, 8, TILE), jnp.float32),
        ),
        in_specs=[SMEM, SMEM, HBM, ANY, HBM],
        out_specs=(VMEM, VMEM, HBM, VMEM),
        scratch_shapes=[
            square,
            square,
            pltpu.VMEM((ROWS, COLS), jnp.float32),
            pltpu.VMEM((32, TILE), jnp.float32),
            pltpu.VMEM((LOCAL + 8, COARSE), jnp.float32),
            pltpu.SemaphoreType.DMA((3,)),
        ],
        compiler_params=pltpu.CompilerParams(vmem_limit_bytes=24 << 20),
    )(tile_class, coeff_sets, *in_hbm(own), other, *in_hbm(state))


def fine_kernel(halo, corrected, coef, *refs):
    if corrected:
        c_ref, means_ref, own_ref, other_ref, own_columns_ref, columns_ref, u_ref, f_ref, fin_ref, out_ref, *refs = refs
        block, means_scratch, columns_scratch, extra, *refs = refs
    else:
        up_ref, u_ref, f_ref, down_ref, fin_ref, out_ref, means_ref, force_ref, *refs = refs
        means_scratch, extra, *refs = refs
    u_ext, f_ext, first, second, force, sums_ref, sems = refs
    ext = ROWS + 2 * halo
    lines = ext // 8
    wide = 2 * STEPS
    strip, core, _, _ = position()
    if corrected:
        parts = ((u_ref, 0, ext, u_ext, 0), (f_ref, 0, ext, f_ext, 0))
    else:
        parts = (
            (u_ref, 0, ROWS, u_ext, halo),
            (up_ref, wide - halo, halo, u_ext, 0),
            (down_ref, 0, halo, u_ext, halo + ROWS),
            (f_ref, 0, ROWS, f_ext, halo),
            (up_ref, 2 * wide - halo, halo, f_ext, 0),
            (down_ref, wide, halo, f_ext, halo + ROWS),
        )
    copies = []
    for k in range(TILES):
        cols = pl.ds(k * TILE, TILE)
        copies.append([])
        for n, (source, at, rows, target, to) in enumerate(parts):
            copy = pltpu.make_async_copy(source.at[pl.ds(at, rows), cols], target.at[k, pl.ds(to, rows)], sems.at[n, k])
            copy.start()
            copies[k].append(copy)

    if corrected:
        needed = [
            pltpu.make_async_copy(means_ref, means_scratch, extra.at[0]),
            pltpu.make_async_copy(own_columns_ref, columns_scratch, extra.at[1]),
        ]
        for copy in needed:
            copy.start()
    sub = iota((8, TILE), 0)
    lane = iota((8, TILE), 1)

    results = []
    for k in range(TILES):
        for copy in copies[k]:
            copy.wait()
        if not corrected:
            cols = pl.ds(k * TILE, TILE)
            result = pltpu.make_async_copy(f_ext.at[k, pl.ds(STEPS, ext - 2 * STEPS)], force_ref.at[:, cols], extra.at[1, k])
            result.start()
            results.append(result)
        if corrected:
            added = []
            for line in range(4):
                at = lax.rem(2 * strip + 15 + line, 16) * 32 + 2 * k
                added.append(jnp.where(lane < BLK, c_ref[0, at], c_ref[0, at + 1]))
        for i in range(lines):
            value = u_ext[k, pl.ds(i, 8, stride=lines), :]
            if corrected:
                row = sub * lines + i
                addend = jnp.where(row < halo + BLK, added[1], added[2])
                if i < halo:
                    addend = jnp.where(sub == 0, added[0], addend)
                if i >= lines - halo:
                    addend = jnp.where(sub == 7, added[3], addend)
                value = value + addend
            first[k, pl.ds(i * 8, 8), :] = value
            force[k, pl.ds(i * 8, 8), :] = STEP * f_ext[k, pl.ds(i, 8, stride=lines), :]

    def tile_step(old, new, k):
        before = lax.rem(k + TILES - 1, TILES)
        after = lax.rem(k + 1, TILES)
        line = [old[k, pl.ds(i * 8, 8), :] for i in range(lines)]
        top = pltpu.roll(line[-1], 1, 0)
        bottom = pltpu.roll(line[0], 7, 0)
        for i in range(lines):
            kind = (i < halo) + 2 * (i >= lines - halo)
            centre, w_left, w_right, w_above, w_below = (coef[k, 5 * kind + w] for w in range(5))
            rows = pl.ds(i * 8, 8)
            left = pltpu.roll(jnp.where(lane == TILE - 1, old[before, rows, :], line[i]), 1, 1)
            right = pltpu.roll(jnp.where(lane == 0, old[after, rows, :], line[i]), TILE - 1, 1)
            above = line[i - 1] if i else top
            below = line[i + 1] if i + 1 < lines else bottom
            new[k, rows, :] = (
                (centre * line[i] + force[k, rows, :])
                + (w_left * left + w_right * right)
                + (w_above * above + w_below * below)
            )

    def two_steps(_, carry):
        def there(k, carry):
            tile_step(first, second, k)
            return carry

        def back(k, carry):
            tile_step(second, first, k)
            return carry

        lax.fori_loop(0, TILES, there, 0, unroll=8)
        lax.fori_loop(0, TILES, back, 0, unroll=8)
        return carry

    lax.fori_loop(0, STEPS // 2, two_steps, 0)

    kept = ext - 2 * STEPS
    for k in range(TILES):
        for i in range(lines):
            u_ext[k, pl.ds(i, 8, stride=lines), :] = first[k, pl.ds(i * 8, 8), :]
        cols = pl.ds(k * TILE, TILE)
        result = pltpu.make_async_copy(u_ext.at[k, pl.ds(STEPS, kept)], fin_ref.at[:, cols], sems.at[0, k])
        result.start()
        results.append(result)
        for br in range(2):
            part = u_ext[k, halo + br * BLK : halo + (br + 1) * BLK, :]
            sums_ref[br * TILES + k : br * TILES + k + 1, :] = jnp.sum(part, axis=0, keepdims=True)
    means = packed_means(sums_ref[...])
    if corrected:
        for copy in needed:
            copy.wait()
        grown = means - means_scratch[...]
        even = core == 0
        pushed = rows_times(grown - jnp.where(even, other_ref[...], 0.0), columns_ref[0:LOCAL, :])
        pushed = pushed - rows_times(jnp.where(even, own_ref[...], 0.0), columns_scratch[0:LOCAL, :])
        write_message(strip, pushed, grown, block, out_ref)
    else:
        out_ref[...] = means
        means_scratch[...] = means
        result = pltpu.make_async_copy(means_scratch, means_ref, extra.at[0, 0])
        result.start()
        results.append(result)
    for result in results:
        result.wait()


def fine_call(halo, corrected, in_specs, more_out, more_specs, scratch, args):
    ext = ROWS + 2 * halo
    field = pltpu.VMEM((TILES, ext, TILE), jnp.float32)
    return pl.pallas_call(
        functools.partial(fine_kernel, halo, corrected),
        cost_estimate=cost(10),
        out_shape=(pltpu.HBM((ext - 2 * STEPS, COLS), jnp.float32), *more_out),
        in_specs=in_specs,
        out_specs=(HBM, *more_specs),
        scratch_shapes=[
            *scratch,
            field,
            field,
            field,
            field,
            field,
            pltpu.VMEM((32, TILE), jnp.float32),
            pltpu.SemaphoreType.DMA((6, TILES)),
        ],
        compiler_params=pltpu.CompilerParams(vmem_limit_bytes=16 << 20),
    )(*args)


def first_sweep(coef, upper, state, source, lower):
    state, source = in_hbm(state, source)
    return fine_call(
        2 * STEPS,
        False,
        [VMEM] + [ANY] * 4,
        (
            jax.ShapeDtypeStruct((1, TILE), jnp.float32),
            pltpu.HBM((1, TILE), jnp.float32),
            pltpu.HBM((ROWS + 2 * STEPS, COLS), jnp.float32),
        ),
        (VMEM, HBM, HBM),
        [pltpu.VMEM((1, TILE), jnp.float32), pltpu.SemaphoreType.DMA((2, TILES))],
        (coef, upper, state, source, lower),
    )


def second_sweep(coef, correction, means, own_part, other_part, columns, next_columns, state, sources):
    means, columns, sources = in_hbm(means, columns, sources)
    return fine_call(
        STEPS,
        True,
        [VMEM, SMEM, HBM, VMEM, VMEM, HBM, VMEM, ANY, HBM],
        (jax.ShapeDtypeStruct((128 * PIECES, TILE), jnp.float32),),
        (VMEM,),
        [
            pltpu.VMEM((8 * PIECES, TILE), jnp.float32),
            pltpu.VMEM((1, TILE), jnp.float32),
            pltpu.VMEM((LOCAL + 8, COARSE), jnp.float32),
            pltpu.SemaphoreType.DMA((2,)),
        ],
        (coef, correction, means, own_part, other_part, columns, next_columns, state, sources),
    )


def rows_times(row, matrix):
    row = jnp.broadcast_to(row, (8, TILE))[:, :LOCAL]
    return jnp.dot(row, matrix, precision=HIGHEST, preferred_element_type=jnp.float32)


def write_message(strip, pushed, raw, block, out_ref):
    lane = iota((1, TILE), 1)
    raw = jnp.where((lane >= LOCAL) == (lax.rem(strip, 2) == 1), raw, 0.0)
    pieces = [pushed[0:1, q * TILE : (q + 1) * TILE] for q in range(4)] + [raw]
    for n in range(8):
        for q in range(PIECES):
            block[n * PIECES + q : n * PIECES + q + 1, :] = pieces[q]
    for n in range(16):
        out_ref[n * 8 * PIECES : (n + 1) * 8 * PIECES, :] = block[...]


def message_kernel(means_ref, base_ref, columns_ref, out_ref, block):
    defect = means_ref[...] - base_ref[...]
    strip, _, _, _ = position()
    write_message(strip, rows_times(defect, columns_ref[0:LOCAL, :]), defect, block, out_ref)


def message(means, base, columns):
    return pl.pallas_call(
        message_kernel,
        cost_estimate=cost(1),
        out_shape=jax.ShapeDtypeStruct((128 * PIECES, TILE), jnp.float32),
        in_specs=[VMEM, VMEM, VMEM],
        out_specs=VMEM,
        scratch_shapes=[pltpu.VMEM((8 * PIECES, TILE), jnp.float32)],
        compiler_params=pltpu.CompilerParams(vmem_limit_bytes=16 << 20),
    )(means, base, columns)


def add(a, b):
    return [p + q for p, q in zip(a, b, strict=True)]


def minus(a, b):
    return [p - q for p, q in zip(a, b, strict=True)]


def select(condition, a, b):
    return [jnp.where(condition, p, q) for p, q in zip(a, b, strict=True)]


def quarters(row):
    return [row[:, q * TILE : (q + 1) * TILE] for q in range(4)]


def applied(matrix, vector):
    diagonal = iota((TILE, TILE), 0) == iota((TILE, TILE), 1)
    column = jnp.sum(matrix * jnp.concatenate(vector, axis=1), axis=1, keepdims=True)
    return [
        jnp.sum(jnp.where(diagonal, column[q * TILE : (q + 1) * TILE], 0.0), axis=0, keepdims=True) for q in range(4)
    ]


def pushes(got_ref, window):
    start = lax.rem(window + 16, 16) * (8 * PIECES)
    return [jnp.sum(got_ref[pl.ds(start + q, 8, stride=PIECES), :], axis=0, keepdims=True) for q in range(4)]


def gathered(got_ref, window):
    start = lax.rem(window + 16, 16) * (8 * PIECES) + 4
    raw = got_ref[pl.ds(start, 8, stride=PIECES), :]
    return [raw[2 * q : 2 * q + 1] + raw[2 * q + 1 : 2 * q + 2] for q in range(4)]


def pair_pushes(got_ref, pair):
    at = 2 * lax.rem(pair, 8)
    return add(pushes(got_ref, at - 1), pushes(got_ref, at))


def strip_piece(strip, value):
    piece = value[3]
    for q in range(3):
        piece = jnp.where(strip // 2 == q, value[q], piece)
    return jnp.broadcast_to(piece, (8, TILE))


def first_chain_kernel(got_ref, other_ref, *refs):
    whole, halved = refs[:5], refs[5:11]
    out_ref, maps_ref, maps, sems, out_sems = refs[11:]
    strip, core, chip, y = position()

    def fetch(slot, source):
        for part in range(2):
            rows = pl.ds(part * HALF, HALF)
            pltpu.make_async_copy(source.at[rows], maps.at[slot, rows], sems.at[slot, part]).start()

    def fetch_halves(slot, which):
        for part, at in ((0, core), (1, 1 - core)):
            rows = pl.ds(pl.multiple_of(at * HALF, HALF), HALF)
            pltpu.make_async_copy(halved[2 * which + part], maps.at[slot, rows], sems.at[slot, part]).start()

    def fetch_turned(slot, pair, below):
        own = (core == 0) == below

        @pl.when(own)
        def _():
            fetch(slot, pair[0])

        @pl.when(jnp.logical_not(own))
        def _():
            fetch(slot, pair[1])

    def fetch_near(slot, ahead):
        if ahead == 2:
            fetch_halves(slot, 0)
        else:
            fetch_turned(slot, whole[0:2], ahead == 3)

    def fetch_far(slot, ahead):
        if ahead in (0, 2):
            fetch_halves(slot, 2 if ahead else 1)
        else:
            fetch_turned(slot, whole[2:4], ahead == 3)

    def landed(slot):
        for part in range(2):
            rows = pl.ds(0, HALF)
            pltpu.make_async_copy(whole[4].at[rows], maps.at[slot, rows], sems.at[slot, part]).wait()
        kept(slot).start()

    def kept(slot):
        return pltpu.make_async_copy(maps.at[slot], maps_ref.at[slot], out_sems.at[slot])

    for half in range(2):
        if half == 1:
            fetch_far(4, 0)
        for ahead in range(1, 4):
            wraps = y + ahead >= 4

            @pl.when(wraps == (half == 0))
            def _():
                fetch_far(4 * half + ahead, ahead)

            @pl.when(wraps != (half == 0))
            def _():
                fetch_near(4 * half + ahead, ahead)

    fetch(0, whole[4])
    fetch(8, other_ref)
    value = select(core == 1, pushes(got_ref, 2 * chip), pair_pushes(got_ref, chip))

    def arriving(step, value):
        landed(step)
        return add(applied(maps[step], value), pair_pushes(got_ref, chip + step))

    value = lax.fori_loop(1, 8, arriving, value)
    landed(0)
    landed(8)

    def again(step, value):
        return add(applied(maps[step], value), pair_pushes(got_ref, chip + step))

    value = lax.fori_loop(0, 8, again, value)
    value = select(core == 1, applied(maps[8], add(value, gathered(got_ref, 2 * chip + 15))), value)
    piece = strip_piece(strip, value)
    lane = iota((8, TILE), 1)
    here = jnp.where((lane < LOCAL) == (lax.rem(strip, 2) == 0), piece, pltpu.roll(piece, LOCAL, 1))
    out_ref[...] = jnp.concatenate(value + [here[0:1]], axis=1)
    for slot in range(9):
        kept(slot).wait()


def first_chain(got, other, whole, halved):
    return pl.pallas_call(
        first_chain_kernel,
        cost_estimate=cost(5),
        out_shape=(
            jax.ShapeDtypeStruct((1, COARSE + TILE), jnp.float32),
            pltpu.HBM((9, COARSE, COARSE), jnp.float32),
        ),
        in_specs=[VMEM] + [ANY] * 12,
        out_specs=(VMEM, HBM),
        scratch_shapes=[
            pltpu.VMEM((9, COARSE, COARSE), jnp.float32),
            pltpu.SemaphoreType.DMA((9, 2)),
            pltpu.SemaphoreType.DMA((9,)),
        ],
        compiler_params=pltpu.CompilerParams(vmem_limit_bytes=16 << 20),
    )(got, other, *whole, *halved)


def last_chain_kernel(got_ref, own_ref, partner_ref, late_ref, maps_ref, u_ref, out_ref, late, maps, sems, u, sem, out_sems):
    strip, core, chip, _ = position()

    def fetched(slot):
        return pltpu.make_async_copy(maps_ref.at[slot], maps.at[slot], sems.at[slot])

    first = pltpu.make_async_copy(late_ref, late, sems.at[9])
    first.start()
    for slot in (1, 2, 3, 4, 5, 6, 7, 0, 8):
        fetched(slot).start()
    state = pltpu.make_async_copy(u_ref, u, sem)
    state.start()
    own, partner = quarters(own_ref[...]), quarters(partner_ref[...])
    even_start = pair_pushes(got_ref, chip)
    odd_start = minus(gathered(got_ref, 2 * chip), own)
    first.wait()
    value = select(core == 1, applied(late[...], odd_start), even_start)

    def arriving(step, value):
        fetched(step).wait()
        return add(applied(maps[step], value), pair_pushes(got_ref, chip + step))

    value = lax.fori_loop(1, 8, arriving, value)
    fetched(0).wait()

    def again(step, value):
        return add(applied(maps[step], value), pair_pushes(got_ref, chip + step))

    value = lax.fori_loop(0, 8, again, value)
    fetched(8).wait()
    final = applied(maps[8], add(value, minus(gathered(got_ref, 2 * chip + 15), partner)))
    piece = strip_piece(strip, select(core == 1, final, value))
    state.wait()
    lane = iota((8, TILE), 1)
    outs = []
    for k in range(TILES):
        cols = slice(k * TILE, (k + 1) * TILE)
        for br in range(2):
            at = lax.rem(strip, 2) * LOCAL + br * 32 + 2 * k
            added = jnp.take_along_axis(piece, at + jnp.where(lane < BLK, 0, 1), axis=1)
            for n in range(BLK // 8):
                rows = slice(br * BLK + n * 8, br * BLK + (n + 1) * 8)
                u[rows, cols] = u[rows, cols] + added
        if k % 4 == 3:
            cols = pl.ds((k - 3) * TILE, 4 * TILE)
            copy = pltpu.make_async_copy(u.at[:, cols], out_ref.at[:, cols], out_sems.at[k // 4])
            copy.start()
            outs.append(copy)
    for copy in outs:
        copy.wait()


def last_chain(got, own, partner, late, maps, previous):
    square = (COARSE, COARSE)
    return pl.pallas_call(
        last_chain_kernel,
        cost_estimate=cost(6),
        out_shape=jax.ShapeDtypeStruct((ROWS, COLS), jnp.float32),
        in_specs=[VMEM, VMEM, VMEM, HBM, HBM, ANY],
        out_specs=HBM,
        scratch_shapes=[
            pltpu.VMEM(square, jnp.float32),
            pltpu.VMEM((9, *square), jnp.float32),
            pltpu.SemaphoreType.DMA((10,)),
            pltpu.VMEM((ROWS, COLS), jnp.float32),
            pltpu.SemaphoreType.DMA,
            pltpu.SemaphoreType.DMA((4,)),
        ],
        compiler_params=pltpu.CompilerParams(vmem_limit_bytes=16 << 20),
    )(got, own, partner, *in_hbm(late, maps), previous)


def exchanged(block):
    block = block.reshape(128, 1, PIECES * TILE)
    return lax.all_to_all(block, ("tm", "space"), 0, 0, tiled=True).reshape(128 * PIECES, TILE)


def swapped(value):
    return moved(value, lambda x, y, z, core: (x, y, z, 1 - core))


def across(value):
    return moved(value, lambda x, y, z, core: (x, y, z + 1 - 2 * core, core))


def along(value, dz=0):
    return moved(value, lambda x, y, z, core: (x, y + 1 - 2 * core, z + dz * (1 - 2 * core), core))


def per_device(initial_states, sources, tile_class, coeff_sets, coarse_maps):
    state, source, own_map = initial_states[0], sources[0], coarse_maps[0]
    core = lax.axis_index("tm") % 2
    wide = 2 * STEPS

    other_map = swapped(own_map)
    upper = shifted(jnp.concatenate([state[-wide:], source[-wide:]], axis=0), 0, 1)
    lower = shifted(jnp.concatenate([state[:wide], source[:wide]], axis=0), 0, -1)

    product, half, columns, coef = pair_product(tile_class, coeff_sets, own_map, other_map, state)
    product, half, columns, upper, lower = lax.optimization_barrier((product, half, columns, upper, lower))
    near = along(product)
    far_same = across(half)
    next_columns = shifted(columns, -1)

    finished, means, kept_means, kept_sources = first_sweep(coef, upper, state, source, lower)
    near, far_same, next_columns, means, finished = lax.optimization_barrier(
        (near, far_same, next_columns, means, finished)
    )
    near_half = lax.dynamic_slice(near, (core * HALF, 0), (HALF, COARSE))
    far = across(near)
    near_second = along(near_half)
    far_second = along(near_half, 1)

    got = exchanged(message(means, next_columns[LOCAL : LOCAL + 1, :TILE], next_columns))

    got, far, near_second, far_second, finished = lax.optimization_barrier(
        (got, far, near_second, far_second, finished)
    )
    previous = shifted(finished, 1)
    whole = [near, swapped(near), far, swapped(far), product]
    halved = []
    for part in (near_second, far_same, far_second):
        halved += [part, swapped(part)]
    correction, maps = first_chain(got, other_map, whole, halved)
    partner = swapped(correction)
    here, there = correction[:, :COARSE], partner[:, :COARSE]
    own_part, other_part = correction[:, COARSE:], partner[:, COARSE:]

    finished, block = second_sweep(
        coef, here, kept_means, own_part, other_part, columns, next_columns, previous, kept_sources
    )
    previous = shifted(finished, 1)
    got = exchanged(block)
    return last_chain(got, here, there, own_map, maps, previous)[None]


def solution(mesh):
    placed = (P("tm", "space", None), P("tm", "space", None), P(), P(), P("tm", None, None))
    return jax.shard_map(
        per_device, mesh=mesh, in_specs=placed, out_specs=P("tm", "space", None), check_vma=False
    )
```

time: 122 us -> 115 us (0.943)
  blocking collectives: 42.2 us -> 19.6 us
  waiting for transfers between devices: 10.6 us -> 22.2 us
  starting transfers between devices: 23.6 us -> 33 us
  local copies, waits for them, and re-layouts: 6.76 us -> 2.66 us
    all_to_all x2 -> x1, blocking collectives: 42.2 us -> 19.6 us  [exchanged(): lax.all_to_all(block, ('tm', 'space'), 0, 0, tiled=True)]
    all_to_all x0 -> x1, waiting for transfers between devices: none -> 12 us  [exchanged(): lax.all_to_all(block, ('tm', 'space'), 0, 0, tiled=True)]
    all_to_all x0 -> x1, starting transfers between devices: none -> 9.45 us  [exchanged(): lax.all_to_all(block, ('tm', 'space'), 0, 0, tiled=True)]
    unnamed x38 -> x16, local copies, waits for them, and re-layouts: 5.6 us -> 1.49 us
    ppermute x6 -> x5, waiting for transfers between devices: 4.44 us -> 2.58 us  [shifted(): return lax.ppermute(value, ('tm', 'space'), pairs)]
    ppermute x11 -> x12, waiting for transfers between devices: 6.2 us -> 7.64 us  [moved(): return lax.ppermute(value, ('tm', 'space'), pairs)]
    pallas_call x2 -> x1, Pallas kernels: 1.49 us -> 0.21 us  [message(): pl.pallas_call(message_kernel, cost_estimate=cost(1), out_shape=jax.Shape...]
    ppermute x6 -> x5, starting transfers between devices: 10.2 us -> 9.94 us  [shifted(): return lax.ppermute(value, ('tm', 'space'), pairs)]
  transfers between devices with their start and end apart: 17 -> 18, of which waited for: 5 -> 6; matrix products, arithmetic and copies ran while one was open for 1% -> 1% of each run, Pallas kernels for 17% -> 17%
where the time goes in v4:
time: 115 us
  Pallas kernels  36.7 us (32%)
  starting transfers between devices  33 us (29%)
  waiting for transfers between devices  22.2 us (19%)
  blocking collectives  19.6 us (17%)
  local copies, waits for them, and re-layouts  2.66 us (2%)
    pallas_call x2, Pallas kernels, fine_call(): pl.pallas_call(functools.partial(fine_kernel, halo, corrected), cost_esti...  21.8 us
    all_to_all x1, blocking collectives, exchanged(): lax.all_to_all(block, ('tm', 'space'), 0, 0, tiled=True)  19.6 us
    ppermute x12, starting transfers between devices, moved(): return lax.ppermute(value, ('tm', 'space'), pairs)  13.6 us
    all_to_all x1, waiting for transfers between devices, exchanged(): lax.all_to_all(block, ('tm', 'space'), 0, 0, tiled=True)  12 us
    ppermute x5, starting transfers between devices, shifted(): return lax.ppermute(value, ('tm', 'space'), pairs)  9.94 us
    all_to_all x1, starting transfers between devices, exchanged(): lax.all_to_all(block, ('tm', 'space'), 0, 0, tiled=True)  9.45 us
    ppermute x12, waiting for transfers between devices, moved(): return lax.ppermute(value, ('tm', 'space'), pairs)  7.64 us
    pallas_call x1, Pallas kernels, last_chain(): pl.pallas_call(last_chain_kernel, cost_estimate=cost(6), out_shape=jax.Sh...  6.32 us
  transfers between devices with their start and end apart: 18, of which 6 were waited for; matrix products, arithmetic and copies ran while one was open for 1% of the time, Pallas kernels for 17%

profile of v4, /device:TPU:1, one launch (start us, length us, event | category | flops | bytes accessed | tf_op | source)
XLA Modules:
  0.0 114.5 jit_solution(1570491604534560061)
XLA Ops:
  0.0 1.4 %collective-permute-start = (f32[512,512]{1,0:T(8,128)}, f32[512,512]{1,0:T(8,128)S(1)}, u32[]{:S(2)}, u32[]{:S(2)}) collective-permute-start(f32[512,512]{1,0:T(8,128)} %bitcast.21), channel_id=1, source_target_pairs={{0,8},{1,9},{2,10},{3,11},{4,12},{5,13},{6,14},{7,15},{8,0},{9,1},... | collective-permute-start | bytes 3145736 | tf_op jit(solution)/shard_map/ppermute | solution.py:44
  1.4 1.1 slice_bitcast_fusion
  2.6 1.4 %collective-permute-start.1 = (f32[32,2048]{1,0:T(8,128)S(1)}, f32[32,2048]{1,0:T(8,128)S(1)}, u32[]{:S(2)}, u32[]{:S(2)}) collective-permute-start(f32[32,2048]{1,0:T(8,128)S(1)} %pad_maximum_fusion), channel_id=1, source_target_pairs={{0,1},{1,2},{2,3},{3,4},{4,5},{5,6},{6,7},{7,0},{8,9},{9,10},{10,1... | collective-permute-start | bytes 786440 | tf_op jit(solution)/shard_map/ppermute | solution.py:53
  4.0 4.7 %collective-permute-start.2 = (f32[32,2048]{1,0:T(8,128)S(1)}, f32[32,2048]{1,0:T(8,128)S(1)}, u32[]{:S(2)}, u32[]{:S(2)}) collective-permute-start(f32[32,2048]{1,0:T(8,128)S(1)} %pad_maximum_fusion.1), channel_id=1, source_target_pairs={{0,7},{1,0},{2,1},{3,2},{4,3},{5,4},{6,5},{7,6},{8,15},{9,8},{10,9... | collective-permute-start | bytes 786440 | tf_op jit(solution)/shard_map/ppermute | solution.py:53
  8.7 3.9 %shard_map.55 = (f32[512,512]{1,0:T(8,128)S(1)}, f32[256,512]{1,0:T(8,128)S(1)}, f32[72,512]{1,0:T(8,128)}, f32[16,20,8,128]{3,2,1,0:T(8,128)S(1)}) custom-call(s32[8,16]{1,0:T(8,128)S(1)} %copy-done.4, f32[3,8]{1,0:T(4,128)S(1)} %copy-done.5, f32[512,512]{1,0:T(8,128)} %bitcast.22, f32[512,512]{1,0:T(8,128)S(1)} %collective-permute-done.other_ref, ...), custom_call_target="tpu_custom_call" | custom-call | bytes 10800000 | tf_op jit(solution)/shard_map/pallas_call | solution.py:164
  12.6 0.0 copy-start
  12.6 2.6 %collective-permute-done.1.refs_0_ = f32[32,2048]{1,0:T(8,128)S(1)} collective-permute-done((f32[32,2048]{1,0:T(8,128)S(1)}, f32[32,2048]{1,0:T(8,128)S(1)}, u32[]{:S(2)}, u32[]{:S(2)}) %collective-permute-start.1) | collective-permute-done | bytes 262176 | tf_op jit(solution)/shard_map/ppermute | solution.py:53
  15.2 2.7 %collective-permute-start.3 = (f32[512,512]{1,0:T(8,128)S(1)}, f32[512,512]{1,0:T(8,128)S(1)}, u32[]{:S(2)}, u32[]{:S(2)}) collective-permute-start(f32[512,512]{1,0:T(8,128)S(1)} %get-tuple-element.36.refs_4_), channel_id=1, source_target_pairs={{0,16},{1,17},{2,18},{3,19},{4,20},{5,21},{6,22},{7,23},{8,56},{9,... | collective-permute-start | bytes 3145736 | tf_op jit(solution)/shard_map/ppermute | solution.py:44
  17.9 2.8 %collective-permute-start.4 = (f32[256,512]{1,0:T(8,128)S(1)}, f32[256,512]{1,0:T(8,128)S(1)}, u32[]{:S(2)}, u32[]{:S(2)}) collective-permute-start(f32[256,512]{1,0:T(8,128)S(1)} %get-tuple-element.37), channel_id=1, source_target_pairs={{0,64},{1,65},{2,66},{3,67},{4,68},{5,69},{6,70},{7,71},{8,76},{9,... | collective-permute-start | bytes 1572872 | tf_op jit(solution)/shard_map/ppermute | solution.py:44
  20.8 10.7 %shard_map.56 = (f32[144,2048]{1,0:T(8,128)}, f32[1,128]{1,0:T(1,128)S(1)}, f32[1,128]{1,0:T(1,128)}, f32[144,2048]{1,0:T(8,128)}) custom-call(f32[16,20,8,128]{3,2,1,0:T(8,128)S(1)} %get-tuple-element.32.coef, f32[32,2048]{1,0:T(8,128)S(1)} %collective-permute-done.1.refs_0_, f32[128,2048]{1,0:T(8,128)} %bitcast.20, f32[128,2048]{1,0:T(8,128)} %bitcast.24, ...), custom_call_target="tpu_custom_call" | custom-call | bytes 36000000 | tf_op jit(solution)/shard_map/pallas_call | solution.py:324
  31.5 0.8 copy-done.2
  32.3 1.8 %collective-permute-start.6 = (f32[512,512]{1,0:T(8,128)S(1)}, f32[512,512]{1,0:T(8,128)}, u32[]{:S(2)}, u32[]{:S(2)}) collective-permute-start(f32[512,512]{1,0:T(8,128)S(1)} %collective-permute-done.3.refs_0_), channel_id=1, source_target_pairs={{0,64},{1,65},{2,66},{3,67},{4,68},{5,69},{6,70},{7,71},{8,76},{9,... | collective-permute-start | bytes 3145736 | tf_op jit(solution)/shard_map/ppermute | solution.py:44
  34.1 3.0 %collective-permute-start.8 = (f32[256,512]{1,0:T(8,128)S(1)}, f32[256,512]{1,0:T(8,128)S(1)}, u32[]{:S(2)}, u32[]{:S(2)}) collective-permute-start(f32[256,512]{1,0:T(8,128)S(1)} %constant_dynamic-slice_fusion), channel_id=1, source_target_pairs={{0,80},{1,81},{2,82},{3,83},{4,84},{5,85},{6,86},{7,87},{8,124},{9... | collective-permute-start | bytes 1572872 | tf_op jit(solution)/shard_map/ppermute | solution.py:44
  37.2 0.2 collective-permute-start.7
  37.4 0.7 copy-done.7
  38.1 0.2 shard_map.57
  38.3 19.6 %all_to_all.10 = f32[128,1,640]{2,1,0:T(1,128)S(1)} all-to-all(f32[128,1,640]{2,1,0:T(1,128)S(1)} %bitcast.18), channel_id=1, replica_groups=mesh['tm'=16,'space'=8] {'tm','space'}, dimensions={0} | all-to-all | bytes 655360 | tf_op jit(solution)/shard_map/all_to_all | solution.py:639
  57.9 1.7 %collective-permute-start.15 = (f32[144,2048]{1,0:T(8,128)}, f32[144,2048]{1,0:T(8,128)S(1)}, u32[]{:S(2)}, u32[]{:S(2)}) collective-permute-start(f32[144,2048]{1,0:T(8,128)} %get-tuple-element.54), channel_id=1, source_target_pairs={{0,8},{1,9},{2,10},{3,11},{4,12},{5,13},{6,14},{7,15},{8,16},{9,17... | collective-permute-start | bytes 3538952 | tf_op jit(solution)/shard_map/ppermute | solution.py:53
  59.5 0.5 collective-permute-start.12
  60.1 0.5 collective-permute-start.11
  60.6 4.8 %collective-permute-done.12.refs_8_ = f32[256,512]{1,0:T(8,128)S(1)} collective-permute-done((f32[256,512]{1,0:T(8,128)S(1)}, f32[256,512]{1,0:T(8,128)S(1)}, u32[]{:S(2)}, u32[]{:S(2)}) %collective-permute-start.12) | collective-permute-done | bytes 524320 | tf_op jit(solution)/shard_map/ppermute | solution.py:44
  65.4 0.1 collective-permute-start.13
  65.5 0.6 collective-permute-done.11.refs_6_
  66.1 1.2 %collective-permute-done.13.refs_10_ = f32[256,512]{1,0:T(8,128)S(1)} collective-permute-done((f32[256,512]{1,0:T(8,128)S(1)}, f32[256,512]{1,0:T(8,128)S(1)}, u32[]{:S(2)}, u32[]{:S(2)}) %collective-permute-start.13) | collective-permute-done | bytes 524320 | tf_op jit(solution)/shard_map/ppermute | solution.py:44
  67.3 4.5 %shard_map.58 = (f32[1,640]{1,0:T(1,128)S(1)}, f32[9,512,512]{2,1,0:T(8,128)}) custom-call(f32[640,128]{1,0:T(8,128)S(1)} %bitcast.16, f32[512,512]{1,0:T(8,128)S(1)} %collective-permute-done.other_ref, f32[512,512]{1,0:T(8,128)S(1)} %collective-permute-done.3.refs_0_, f32[512,512]{1,0:T(8,128)S(1)} %collective-permute-done.9.refs_1_, ...), custom_call_target="tpu_custom_call" | custom-call | bytes 18000000 | tf_op jit(solution)/shard_map/pallas_call | solution.py:547
  71.8 0.4 collective-permute-start.14
  72.2 1.0 collective-permute-done.14
  73.2 11.1 %shard_map.59 = (f32[128,2048]{1,0:T(8,128)}, f32[640,128]{1,0:T(8,128)}) custom-call(f32[16,20,8,128]{3,2,1,0:T(8,128)S(1)} %get-tuple-element.32.coef, f32[1,512]{1,0:T(1,128)S(1)} %slice.48.refs_0_.own_ref, f32[1,128]{1,0:T(1,128)} %get-tuple-element.53.refs_1_, f32[1,128]{1,0:T(1,128)S(1)} %slice.49.refs_2_, f32[1,128]{1,0:T(1,128)S(1)} %slice.52.refs_3_, ...), custom_call_target="tpu_custom_call" | custom-call | bytes 36000000 | tf_op jit(solution)/shard_map/pallas_call | solution.py:324
  84.3 2.2 %collective-permute-start.16 = (f32[128,2048]{1,0:T(8,128)}, f32[128,2048]{1,0:T(8,128)S(1)}, u32[]{:S(2)}, u32[]{:S(2)}) collective-permute-start(f32[128,2048]{1,0:T(8,128)} %get-tuple-element.58), channel_id=1, source_target_pairs={{0,8},{1,9},{2,10},{3,11},{4,12},{5,13},{6,14},{7,15},{8,16},{9,17... | collective-permute-start | bytes 3145736 | tf_op jit(solution)/shard_map/ppermute | solution.py:53
  86.6 9.4 %all-to-all-start.1 = ((f32[128,1,640]{2,1,0:T(1,128)}), f32[128,1,640]{2,1,0:T(1,128)S(1)}, u32[]{:S(2)}, u32[]{:S(2)}) async-start(f32[128,1,640]{2,1,0:T(1,128)} %bitcast.9), calls=%async_computation.1 | async-start | bytes 655360 | tf_op jit(solution)/shard_map/all_to_all | solution.py:639
  96.0 12.0 %all-to-all-done.1 = f32[128,1,640]{2,1,0:T(1,128)S(1)} async-done(((f32[128,1,640]{2,1,0:T(1,128)}), f32[128,1,640]{2,1,0:T(1,128)S(1)}, u32[]{:S(2)}, u32[]{:S(2)}) %all-to-all-start.1) | async-done | bytes 327712 | tf_op jit(solution)/shard_map/all_to_all | solution.py:639
  108.0 6.3 %shard_map.60 = f32[128,2048]{1,0:T(8,128)} custom-call(f32[640,128]{1,0:T(8,128)S(1)} %bitcast.17, f32[1,512]{1,0:T(1,128)S(1)} %slice.48.refs_0_.own_ref, f32[1,512]{1,0:T(1,128)S(1)} %slice.53.partner_ref, f32[512,512]{1,0:T(8,128)} %bitcast.23, f32[9,512,512]{2,1,0:T(8,128)} %get-tuple-element.57.maps_ref, f32[128,2048]{1,0:T(8,128)S(1)} %collective-permute-done.16.u_ref), custom_call_target="tpu_custom_call" | custom-call | bytes 21600000 | tf_op jit(solution)/shard_map/pallas_call | solution.py:619
  (36 shorter events, 0.1 us)
Async XLA Ops:
  0.0 8.6 %copy-start.5 = (f32[3,8]{1,0:T(4,128)S(1)}, f32[3,8]{1,0:T(4,128)}, u32[]{:S(2)}) copy-start(f32[3,8]{1,0:T(4,128)} %sets_ref.1) | copy-start | bytes 292
  0.0 8.6 %copy-start.4 = (s32[8,16]{1,0:T(8,128)S(1)}, s32[8,16]{1,0:T(8,128)}, u32[]{:S(2)}) copy-start(s32[8,16]{1,0:T(8,128)} %class_ref.1) | copy-start | bytes 1540
  0.0 8.6 %collective-permute-start = (f32[512,512]{1,0:T(8,128)}, f32[512,512]{1,0:T(8,128)S(1)}, u32[]{:S(2)}, u32[]{:S(2)}) collective-permute-start(f32[512,512]{1,0:T(8,128)} %bitcast.21), channel_id=1, source_target_pairs={{0,8},{1,9},{2,10},{3,11},{4,12},{5,13},{6,14},{7,15},{8,0},{9,1},... | collective-permute-start | bytes 3145736 | tf_op jit(solution)/shard_map/ppermute | solution.py:44
  2.6 12.6 %collective-permute-start.1 = (f32[32,2048]{1,0:T(8,128)S(1)}, f32[32,2048]{1,0:T(8,128)S(1)}, u32[]{:S(2)}, u32[]{:S(2)}) collective-permute-start(f32[32,2048]{1,0:T(8,128)S(1)} %pad_maximum_fusion), channel_id=1, source_target_pairs={{0,1},{1,2},{2,3},{3,4},{4,5},{5,6},{6,7},{7,0},{8,9},{9,10},{10,1... | collective-permute-start | bytes 786440 | tf_op jit(solution)/shard_map/ppermute | solution.py:53
  4.0 11.2 %collective-permute-start.2 = (f32[32,2048]{1,0:T(8,128)S(1)}, f32[32,2048]{1,0:T(8,128)S(1)}, u32[]{:S(2)}, u32[]{:S(2)}) collective-permute-start(f32[32,2048]{1,0:T(8,128)S(1)} %pad_maximum_fusion.1), channel_id=1, source_target_pairs={{0,7},{1,0},{2,1},{3,2},{4,3},{5,4},{6,5},{7,6},{8,15},{9,8},{10,9... | collective-permute-start | bytes 786440 | tf_op jit(solution)/shard_map/ppermute | solution.py:53
  12.6 18.8 %copy-start = (f32[512,512]{1,0:T(8,128)}, f32[512,512]{1,0:T(8,128)S(1)}, u32[]{:S(2)}) copy-start(f32[512,512]{1,0:T(8,128)S(1)} %get-tuple-element.36.refs_4_) | copy-start | bytes 3145732
  15.2 16.3 %collective-permute-start.3 = (f32[512,512]{1,0:T(8,128)S(1)}, f32[512,512]{1,0:T(8,128)S(1)}, u32[]{:S(2)}, u32[]{:S(2)}) collective-permute-start(f32[512,512]{1,0:T(8,128)S(1)} %get-tuple-element.36.refs_4_), channel_id=1, source_target_pairs={{0,16},{1,17},{2,18},{3,19},{4,20},{5,21},{6,22},{7,23},{8,56},{9,... | collective-permute-start | bytes 3145736 | tf_op jit(solution)/shard_map/ppermute | solution.py:44
  17.9 13.5 %collective-permute-start.4 = (f32[256,512]{1,0:T(8,128)S(1)}, f32[256,512]{1,0:T(8,128)S(1)}, u32[]{:S(2)}, u32[]{:S(2)}) collective-permute-start(f32[256,512]{1,0:T(8,128)S(1)} %get-tuple-element.37), channel_id=1, source_target_pairs={{0,64},{1,65},{2,66},{3,67},{4,68},{5,69},{6,70},{7,71},{8,76},{9,... | collective-permute-start | bytes 1572872 | tf_op jit(solution)/shard_map/ppermute | solution.py:44
  20.8 10.7 %collective-permute-start.5 = (f32[72,512]{1,0:T(8,128)}, f32[72,512]{1,0:T(8,128)S(1)}, u32[]{:S(2)}, u32[]{:S(2)}) collective-permute-start(f32[72,512]{1,0:T(8,128)} %get-tuple-element.38.refs_4_), channel_id=1, source_target_pairs={{0,120},{1,121},{2,122},{3,123},{4,124},{5,125},{6,126},{7,127},{8... | collective-permute-start | bytes 442376 | tf_op jit(solution)/shard_map/ppermute | solution.py:53
  31.4 0.8 copy-start.6
  31.5 0.8 copy-start.2
  32.3 25.6 %collective-permute-start.6 = (f32[512,512]{1,0:T(8,128)S(1)}, f32[512,512]{1,0:T(8,128)}, u32[]{:S(2)}, u32[]{:S(2)}) collective-permute-start(f32[512,512]{1,0:T(8,128)S(1)} %collective-permute-done.3.refs_0_), channel_id=1, source_target_pairs={{0,64},{1,65},{2,66},{3,67},{4,68},{5,69},{6,70},{7,71},{8,76},{9,... | collective-permute-start | bytes 3145736 | tf_op jit(solution)/shard_map/ppermute | solution.py:44
  34.1 25.4 %copy-start.3 = (f32[256,512]{1,0:T(8,128)S(1)}, f32[256,512]{1,0:T(8,128)}, u32[]{:S(2)}) copy-start(f32[256,512]{1,0:T(8,128)} %copy-done.2) | copy-start | bytes 1572868
  34.1 33.2 %copy-start.1 = (f32[512,512]{1,0:T(8,128)S(1)}, f32[512,512]{1,0:T(8,128)}, u32[]{:S(2)}) copy-start(f32[512,512]{1,0:T(8,128)} %copy-done) | copy-start | bytes 3145732
  34.1 23.7 %collective-permute-start.8 = (f32[256,512]{1,0:T(8,128)S(1)}, f32[256,512]{1,0:T(8,128)S(1)}, u32[]{:S(2)}, u32[]{:S(2)}) collective-permute-start(f32[256,512]{1,0:T(8,128)S(1)} %constant_dynamic-slice_fusion), channel_id=1, source_target_pairs={{0,80},{1,81},{2,82},{3,83},{4,84},{5,85},{6,86},{7,87},{8,124},{9... | collective-permute-start | bytes 1572872 | tf_op jit(solution)/shard_map/ppermute | solution.py:44
  37.2 20.7 %collective-permute-start.7 = (f32[256,512]{1,0:T(8,128)S(1)}, f32[256,512]{1,0:T(8,128)S(1)}, u32[]{:S(2)}, u32[]{:S(2)}) collective-permute-start(f32[256,512]{1,0:T(8,128)S(1)} %constant_dynamic-slice_fusion), channel_id=1, source_target_pairs={{0,16},{1,17},{2,18},{3,19},{4,20},{5,21},{6,22},{7,23},{8,56},{9,... | collective-permute-start | bytes 1572872 | tf_op jit(solution)/shard_map/ppermute | solution.py:44
  37.4 0.7 copy-start.7
  57.9 15.3 %collective-permute-start.15 = (f32[144,2048]{1,0:T(8,128)}, f32[144,2048]{1,0:T(8,128)S(1)}, u32[]{:S(2)}, u32[]{:S(2)}) collective-permute-start(f32[144,2048]{1,0:T(8,128)} %get-tuple-element.54), channel_id=1, source_target_pairs={{0,8},{1,9},{2,10},{3,11},{4,12},{5,13},{6,14},{7,15},{8,16},{9,17... | collective-permute-start | bytes 3538952 | tf_op jit(solution)/shard_map/ppermute | solution.py:53
  59.5 6.0 %collective-permute-start.9 = (f32[512,512]{1,0:T(8,128)S(1)}, f32[512,512]{1,0:T(8,128)S(1)}, u32[]{:S(2)}, u32[]{:S(2)}) collective-permute-start(f32[512,512]{1,0:T(8,128)S(1)} %collective-permute-done.3.refs_0_), channel_id=1, source_target_pairs={{0,8},{1,9},{2,10},{3,11},{4,12},{5,13},{6,14},{7,15},{8,0},{9,1},... | collective-permute-start | bytes 3145736 | tf_op jit(solution)/shard_map/ppermute | solution.py:44
  59.5 5.8 %collective-permute-start.12 = (f32[256,512]{1,0:T(8,128)S(1)}, f32[256,512]{1,0:T(8,128)S(1)}, u32[]{:S(2)}, u32[]{:S(2)}) collective-permute-start(f32[256,512]{1,0:T(8,128)S(1)} %copy-done.3), channel_id=1, source_target_pairs={{0,8},{1,9},{2,10},{3,11},{4,12},{5,13},{6,14},{7,15},{8,0},{9,1},... | collective-permute-start | bytes 1572872 | tf_op jit(solution)/shard_map/ppermute | solution.py:44
  60.1 7.3 %collective-permute-start.10 = (f32[512,512]{1,0:T(8,128)}, f32[512,512]{1,0:T(8,128)S(1)}, u32[]{:S(2)}, u32[]{:S(2)}) collective-permute-start(f32[512,512]{1,0:T(8,128)} %collective-permute-done.6.refs_2_), channel_id=1, source_target_pairs={{0,8},{1,9},{2,10},{3,11},{4,12},{5,13},{6,14},{7,15},{8,0},{9,1},... | collective-permute-start | bytes 3145736 | tf_op jit(solution)/shard_map/ppermute | solution.py:44
  60.1 6.1 %collective-permute-start.11 = (f32[256,512]{1,0:T(8,128)S(1)}, f32[256,512]{1,0:T(8,128)S(1)}, u32[]{:S(2)}, u32[]{:S(2)}) collective-permute-start(f32[256,512]{1,0:T(8,128)S(1)} %collective-permute-done.7.refs_5_), channel_id=1, source_target_pairs={{0,8},{1,9},{2,10},{3,11},{4,12},{5,13},{6,14},{7,15},{8,0},{9,1},... | collective-permute-start | bytes 1572872 | tf_op jit(solution)/shard_map/ppermute | solution.py:44
  65.4 1.9 %collective-permute-start.13 = (f32[256,512]{1,0:T(8,128)S(1)}, f32[256,512]{1,0:T(8,128)S(1)}, u32[]{:S(2)}, u32[]{:S(2)}) collective-permute-start(f32[256,512]{1,0:T(8,128)S(1)} %collective-permute-done.8.refs_9_), channel_id=1, source_target_pairs={{0,8},{1,9},{2,10},{3,11},{4,12},{5,13},{6,14},{7,15},{8,0},{9,1},... | collective-permute-start | bytes 1572872 | tf_op jit(solution)/shard_map/ppermute | solution.py:44
  71.8 1.4 %collective-permute-start.14 = (f32[1,640]{1,0:T(1,128)S(1)}, f32[1,640]{1,0:T(1,128)S(1)}, u32[]{:S(2)}, u32[]{:S(2)}) collective-permute-start(f32[1,640]{1,0:T(1,128)S(1)} %get-tuple-element.52), channel_id=1, source_target_pairs={{0,8},{1,9},{2,10},{3,11},{4,12},{5,13},{6,14},{7,15},{8,0},{9,1},... | collective-permute-start | bytes 7688 | tf_op jit(solution)/shard_map/ppermute | solution.py:44
  84.3 23.7 %collective-permute-start.16 = (f32[128,2048]{1,0:T(8,128)}, f32[128,2048]{1,0:T(8,128)S(1)}, u32[]{:S(2)}, u32[]{:S(2)}) collective-permute-start(f32[128,2048]{1,0:T(8,128)} %get-tuple-element.58), channel_id=1, source_target_pairs={{0,8},{1,9},{2,10},{3,11},{4,12},{5,13},{6,14},{7,15},{8,16},{9,17... | collective-permute-start | bytes 3145736 | tf_op jit(solution)/shard_map/ppermute | solution.py:53
  86.6 21.4 %all-to-all-start.1 = ((f32[128,1,640]{2,1,0:T(1,128)}), f32[128,1,640]{2,1,0:T(1,128)S(1)}, u32[]{:S(2)}, u32[]{:S(2)}) async-start(f32[128,1,640]{2,1,0:T(1,128)} %bitcast.9), calls=%async_computation.1 | async-start | bytes 655360 | tf_op jit(solution)/shard_map/all_to_all | solution.py:639

commit v5 on v4

--- a/solution.py
+++ b/solution.py
@@ -15,6 +15,8 @@
 COARSE = 512
 HALF = COARSE // 2
 TILES = COLS // TILE
+EXT = ROWS + 2 * STEPS
+LINES = EXT // 8
 LOCAL = 64
 PIECES = 5
 STEP = 0.6
@@ -98,11 +100,9 @@
         upper, inner, lower = (weights(row, k) for row in strips)
         for w in range(5):
             value = jnp.full((8, TILE), inner[w], jnp.float32)
-            with_upper = jnp.where(sub == 0, upper[w], value)
             coef_ref[k, w] = value
-            coef_ref[k, 5 + w] = with_upper
+            coef_ref[k, 5 + w] = jnp.where(sub == 0, upper[w], value)
             coef_ref[k, 10 + w] = jnp.where(sub == 7, lower[w], value)
-            coef_ref[k, 15 + w] = jnp.where(sub == 7, lower[w], with_upper)
 
 
 def pair_kernel(class_ref, sets_ref, own_ref, other_ref, u_ref, q_ref, half_ref, columns_ref, coef_ref, *scratch):
@@ -168,7 +168,7 @@
             jax.ShapeDtypeStruct((COARSE, COARSE), jnp.float32),
             jax.ShapeDtypeStruct((HALF, COARSE), jnp.float32),
             pltpu.HBM((LOCAL + 8, COARSE), jnp.float32),
-            jax.ShapeDtypeStruct((TILES, 20, 8, TILE), jnp.float32),
+            jax.ShapeDtypeStruct((TILES, 15, 8, TILE), jnp.float32),
         ),
         in_specs=[SMEM, SMEM, HBM, ANY, HBM],
         out_specs=(VMEM, VMEM, HBM, VMEM),
@@ -181,124 +181,134 @@
             pltpu.SemaphoreType.DMA((3,)),
         ],
         compiler_params=pltpu.CompilerParams(vmem_limit_bytes=24 << 20),
-    )(tile_class, coeff_sets, *in_hbm(own), other, *in_hbm(state))
-
-
-def fine_kernel(halo, corrected, coef, *refs):
+    )(*in_hbm(tile_class, coeff_sets, own), other, *in_hbm(state))
+
+
+def fine_kernel(corrected, coef, *refs):
     if corrected:
-        c_ref, means_ref, own_ref, other_ref, own_columns_ref, columns_ref, u_ref, f_ref, fin_ref, out_ref, *refs = refs
-        block, means_scratch, columns_scratch, extra, *refs = refs
+        c_ref, means_ref, own_ref, other_ref, own_columns_ref, columns_ref, *refs = refs
+        up_ref, u_ref, down_ref, f_ref, fin_ref, out_ref, *refs = refs
+        block, means_scratch, columns_scratch, extra, u_ext, first, second, force, sums_ref, sems = refs
+        fields = [
+            pltpu.make_async_copy(u_ref, u_ext.at[:, pl.ds(STEPS, ROWS)], extra.at[0]),
+            pltpu.make_async_copy(f_ref, force, extra.at[1]),
+        ]
+        needed = [
+            pltpu.make_async_copy(means_ref, means_scratch, extra.at[2]),
+            pltpu.make_async_copy(own_columns_ref, columns_scratch, extra.at[3]),
+        ]
+        for copy in fields + needed:
+            copy.start()
     else:
-        up_ref, u_ref, f_ref, down_ref, fin_ref, out_ref, means_ref, force_ref, *refs = refs
-        means_scratch, extra, *refs = refs
-    u_ext, f_ext, first, second, force, sums_ref, sems = refs
-    ext = ROWS + 2 * halo
-    lines = ext // 8
-    wide = 2 * STEPS
+        up_ref, u_ref, f_ref, down_ref, fin_ref, out_ref, top_ref, bottom_ref, means_ref, force_ref, *refs = refs
+        means_scratch, f_ext, f_sems, u_ext, first, second, force, sums_ref, sems = refs
+        copies = []
+        for k in range(TILES):
+            cols = pl.ds(k * TILE, TILE)
+            inner = pl.ds(STEPS, ROWS)
+            copies.append(
+                (
+                    pltpu.make_async_copy(u_ref.at[:, cols], u_ext.at[k, inner], sems.at[k]),
+                    pltpu.make_async_copy(f_ref.at[:, cols], f_ext.at[k, inner], f_sems.at[k]),
+                )
+            )
+            for copy in copies[k]:
+                copy.start()
     strip, core, _, _ = position()
-    if corrected:
-        parts = ((u_ref, 0, ext, u_ext, 0), (f_ref, 0, ext, f_ext, 0))
-    else:
-        parts = (
-            (u_ref, 0, ROWS, u_ext, halo),
-            (up_ref, wide - halo, halo, u_ext, 0),
-            (down_ref, 0, halo, u_ext, halo + ROWS),
-            (f_ref, 0, ROWS, f_ext, halo),
-            (up_ref, 2 * wide - halo, halo, f_ext, 0),
-            (down_ref, wide, halo, f_ext, halo + ROWS),
-        )
-    copies = []
-    for k in range(TILES):
-        cols = pl.ds(k * TILE, TILE)
-        copies.append([])
-        for n, (source, at, rows, target, to) in enumerate(parts):
-            copy = pltpu.make_async_copy(source.at[pl.ds(at, rows), cols], target.at[k, pl.ds(to, rows)], sems.at[n, k])
-            copy.start()
-            copies[k].append(copy)
-
-    if corrected:
-        needed = [
-            pltpu.make_async_copy(means_ref, means_scratch, extra.at[0]),
-            pltpu.make_async_copy(own_columns_ref, columns_scratch, extra.at[1]),
-        ]
-        for copy in needed:
-            copy.start()
     sub = iota((8, TILE), 0)
     lane = iota((8, TILE), 1)
-
-    results = []
     for k in range(TILES):
-        for copy in copies[k]:
+        cols = slice(k * TILE, (k + 1) * TILE)
+        u_ext[k, 0:STEPS, :] = up_ref[0:STEPS, cols]
+        u_ext[k, STEPS + ROWS : EXT, :] = down_ref[0:STEPS, cols]
+        if not corrected:
+            f_ext[k, 0:STEPS, :] = up_ref[STEPS : 2 * STEPS, cols]
+            f_ext[k, STEPS + ROWS : EXT, :] = down_ref[STEPS : 2 * STEPS, cols]
+    if corrected:
+        for copy in fields:
             copy.wait()
-        if not corrected:
-            cols = pl.ds(k * TILE, TILE)
-            result = pltpu.make_async_copy(f_ext.at[k, pl.ds(STEPS, ext - 2 * STEPS)], force_ref.at[:, cols], extra.at[1, k])
-            result.start()
-            results.append(result)
+    for k in range(TILES):
         if corrected:
             added = []
             for line in range(4):
                 at = lax.rem(2 * strip + 15 + line, 16) * 32 + 2 * k
                 added.append(jnp.where(lane < BLK, c_ref[0, at], c_ref[0, at + 1]))
-        for i in range(lines):
-            value = u_ext[k, pl.ds(i, 8, stride=lines), :]
+        else:
+            for copy in copies[k]:
+                copy.wait()
+        for i in range(LINES):
+            rows = pl.ds(i * 8, 8)
+            value = u_ext[k, pl.ds(i, 8, stride=LINES), :]
             if corrected:
-                row = sub * lines + i
-                addend = jnp.where(row < halo + BLK, added[1], added[2])
-                if i < halo:
+                row = sub * LINES + i
+                addend = jnp.where(row < STEPS + BLK, added[1], added[2])
+                if i < STEPS:
                     addend = jnp.where(sub == 0, added[0], addend)
-                if i >= lines - halo:
+                if i >= LINES - STEPS:
                     addend = jnp.where(sub == 7, added[3], addend)
                 value = value + addend
-            first[k, pl.ds(i * 8, 8), :] = value
-            force[k, pl.ds(i * 8, 8), :] = STEP * f_ext[k, pl.ds(i, 8, stride=lines), :]
-
-    def tile_step(old, new, k):
+            else:
+                force[k, rows, :] = STEP * f_ext[k, pl.ds(i, 8, stride=LINES), :]
+            first[k, rows, :] = value
+    results = []
+    if not corrected:
+        results.append(pltpu.make_async_copy(force, force_ref, f_sems.at[0]))
+        results[0].start()
+
+    def tile_step(old, new, k, last=False):
         before = lax.rem(k + TILES - 1, TILES)
         after = lax.rem(k + 1, TILES)
-        line = [old[k, pl.ds(i * 8, 8), :] for i in range(lines)]
+        line = [old[k, pl.ds(i * 8, 8), :] for i in range(LINES)]
         top = pltpu.roll(line[-1], 1, 0)
         bottom = pltpu.roll(line[0], 7, 0)
-        for i in range(lines):
-            kind = (i < halo) + 2 * (i >= lines - halo)
+        for i in range(LINES):
+            kind = (i < STEPS) + 2 * (i >= LINES - STEPS)
             centre, w_left, w_right, w_above, w_below = (coef[k, 5 * kind + w] for w in range(5))
             rows = pl.ds(i * 8, 8)
             left = pltpu.roll(jnp.where(lane == TILE - 1, old[before, rows, :], line[i]), 1, 1)
             right = pltpu.roll(jnp.where(lane == 0, old[after, rows, :], line[i]), TILE - 1, 1)
             above = line[i - 1] if i else top
-            below = line[i + 1] if i + 1 < lines else bottom
-            new[k, rows, :] = (
+            below = line[i + 1] if i + 1 < LINES else bottom
+            new[k, pl.ds(i, 8, stride=LINES) if last else rows, :] = (
                 (centre * line[i] + force[k, rows, :])
                 + (w_left * left + w_right * right)
                 + (w_above * above + w_below * below)
             )
 
+    def sweep(old, new):
+        def one_tile(k, carry):
+            tile_step(old, new, k)
+            return carry
+
+        lax.fori_loop(0, TILES, one_tile, 0, unroll=16)
+
     def two_steps(_, carry):
-        def there(k, carry):
-            tile_step(first, second, k)
-            return carry
-
-        def back(k, carry):
-            tile_step(second, first, k)
-            return carry
-
-        lax.fori_loop(0, TILES, there, 0, unroll=8)
-        lax.fori_loop(0, TILES, back, 0, unroll=8)
+        sweep(first, second)
+        sweep(second, first)
         return carry
 
-    lax.fori_loop(0, STEPS // 2, two_steps, 0)
-
-    kept = ext - 2 * STEPS
-    for k in range(TILES):
-        for i in range(lines):
-            u_ext[k, pl.ds(i, 8, stride=lines), :] = first[k, pl.ds(i * 8, 8), :]
-        cols = pl.ds(k * TILE, TILE)
-        result = pltpu.make_async_copy(u_ext.at[k, pl.ds(STEPS, kept)], fin_ref.at[:, cols], sems.at[0, k])
-        result.start()
-        results.append(result)
+    lax.fori_loop(0, STEPS // 2 - 1, two_steps, 0)
+    sweep(first, second)
+
+    def last_tile(k, carry):
+        tile_step(second, u_ext, k, last=True)
         for br in range(2):
-            part = u_ext[k, halo + br * BLK : halo + (br + 1) * BLK, :]
-            sums_ref[br * TILES + k : br * TILES + k + 1, :] = jnp.sum(part, axis=0, keepdims=True)
+            part = u_ext[k, STEPS + br * BLK : STEPS + (br + 1) * BLK, :]
+            sums_ref[pl.ds(br * TILES + k, 1), :] = jnp.sum(part, axis=0, keepdims=True)
+        return carry
+
+    for part in range(2):
+        half = TILES // 2
+        tiles = pl.ds(part * half, half)
+        lax.fori_loop(part * half, (part + 1) * half, last_tile, 0, unroll=8)
+        copy = pltpu.make_async_copy(u_ext.at[tiles, pl.ds(STEPS, ROWS)], fin_ref.at[tiles], sems.at[part])
+        copy.start()
+        results.append(copy)
+    if not corrected:
+        for k in range(TILES):
+            cols = slice(k * TILE, (k + 1) * TILE)
+            top_ref[:, cols] = u_ext[k, STEPS : 2 * STEPS, :]
+            bottom_ref[:, cols] = u_ext[k, ROWS : STEPS + ROWS, :]
     means = packed_means(sums_ref[...])
     if corrected:
         for copy in needed:
@@ -311,31 +321,32 @@
     else:
         out_ref[...] = means
         means_scratch[...] = means
-        result = pltpu.make_async_copy(means_scratch, means_ref, extra.at[0, 0])
-        result.start()
-        results.append(result)
-    for result in results:
-        result.wait()
-
-
-def fine_call(halo, corrected, in_specs, more_out, more_specs, scratch, args):
-    ext = ROWS + 2 * halo
-    field = pltpu.VMEM((TILES, ext, TILE), jnp.float32)
+        copy = pltpu.make_async_copy(means_scratch, means_ref, f_sems.at[1])
+        copy.start()
+        results.append(copy)
+    for copy in results:
+        copy.wait()
+
+
+FIELD = pltpu.VMEM((TILES, EXT, TILE), jnp.float32)
+EDGE = jax.ShapeDtypeStruct((STEPS, COLS), jnp.float32)
+
+
+def fine_call(corrected, in_specs, more_out, more_specs, scratch, args):
     return pl.pallas_call(
-        functools.partial(fine_kernel, halo, corrected),
+        functools.partial(fine_kernel, corrected),
         cost_estimate=cost(10),
-        out_shape=(pltpu.HBM((ext - 2 * STEPS, COLS), jnp.float32), *more_out),
+        out_shape=(pltpu.HBM((TILES, ROWS, TILE), jnp.float32), *more_out),
         in_specs=in_specs,
         out_specs=(HBM, *more_specs),
         scratch_shapes=[
             *scratch,
-            field,
-            field,
-            field,
-            field,
-            field,
+            FIELD,
+            FIELD,
+            FIELD,
+            FIELD,
             pltpu.VMEM((32, TILE), jnp.float32),
-            pltpu.SemaphoreType.DMA((6, TILES)),
+            pltpu.SemaphoreType.DMA((TILES,)),
         ],
         compiler_params=pltpu.CompilerParams(vmem_limit_bytes=16 << 20),
     )(*args)
@@ -344,35 +355,35 @@
 def first_sweep(coef, upper, state, source, lower):
     state, source = in_hbm(state, source)
     return fine_call(
-        2 * STEPS,
         False,
-        [VMEM] + [ANY] * 4,
+        [VMEM, VMEM, HBM, HBM, VMEM],
         (
             jax.ShapeDtypeStruct((1, TILE), jnp.float32),
+            EDGE,
+            EDGE,
             pltpu.HBM((1, TILE), jnp.float32),
-            pltpu.HBM((ROWS + 2 * STEPS, COLS), jnp.float32),
+            pltpu.HBM((TILES, EXT, TILE), jnp.float32),
         ),
-        (VMEM, HBM, HBM),
-        [pltpu.VMEM((1, TILE), jnp.float32), pltpu.SemaphoreType.DMA((2, TILES))],
+        (VMEM, VMEM, VMEM, HBM, HBM),
+        [pltpu.VMEM((1, TILE), jnp.float32), FIELD, pltpu.SemaphoreType.DMA((TILES,))],
         (coef, upper, state, source, lower),
     )
 
 
-def second_sweep(coef, correction, means, own_part, other_part, columns, next_columns, state, sources):
-    means, columns, sources = in_hbm(means, columns, sources)
+def second_sweep(coef, correction, means, own_part, other_part, columns, next_columns, state, forcing):
+    means, columns, forcing = in_hbm(means, columns, forcing)
     return fine_call(
-        STEPS,
         True,
-        [VMEM, SMEM, HBM, VMEM, VMEM, HBM, VMEM, ANY, HBM],
+        [VMEM, SMEM, HBM, VMEM, VMEM, HBM, VMEM, VMEM, ANY, VMEM, HBM],
         (jax.ShapeDtypeStruct((128 * PIECES, TILE), jnp.float32),),
         (VMEM,),
         [
             pltpu.VMEM((8 * PIECES, TILE), jnp.float32),
             pltpu.VMEM((1, TILE), jnp.float32),
             pltpu.VMEM((LOCAL + 8, COARSE), jnp.float32),
-            pltpu.SemaphoreType.DMA((2,)),
+            pltpu.SemaphoreType.DMA((4,)),
         ],
-        (coef, correction, means, own_part, other_part, columns, next_columns, state, sources),
+        (coef, correction, means, own_part, other_part, columns, next_columns, *state, forcing),
     )
 
 
@@ -544,6 +555,7 @@
 
 
 def first_chain(got, other, whole, halved):
+    whole[4], halved[2] = in_hbm(whole[4], halved[2])
     return pl.pallas_call(
         first_chain_kernel,
         cost_estimate=cost(5),
@@ -562,7 +574,7 @@
     )(got, other, *whole, *halved)
 
 
-def last_chain_kernel(got_ref, own_ref, partner_ref, late_ref, maps_ref, u_ref, out_ref, late, maps, sems, u, sem, out_sems):
+def last_chain_kernel(got_ref, own_ref, partner_ref, late_ref, maps_ref, u_ref, out_ref, late, maps, sems, u, whole, sem, out_sems):
     strip, core, chip, _ = position()
 
     def fetched(slot):
@@ -604,10 +616,10 @@
             added = jnp.take_along_axis(piece, at + jnp.where(lane < BLK, 0, 1), axis=1)
             for n in range(BLK // 8):
                 rows = slice(br * BLK + n * 8, br * BLK + (n + 1) * 8)
-                u[rows, cols] = u[rows, cols] + added
+                whole[rows, cols] = u[k, rows, :] + added
         if k % 4 == 3:
             cols = pl.ds((k - 3) * TILE, 4 * TILE)
-            copy = pltpu.make_async_copy(u.at[:, cols], out_ref.at[:, cols], out_sems.at[k // 4])
+            copy = pltpu.make_async_copy(whole.at[:, cols], out_ref.at[:, cols], out_sems.at[k // 4])
             copy.start()
             outs.append(copy)
     for copy in outs:
@@ -626,6 +638,7 @@
             pltpu.VMEM(square, jnp.float32),
             pltpu.VMEM((9, *square), jnp.float32),
             pltpu.SemaphoreType.DMA((10,)),
+            pltpu.VMEM((TILES, ROWS, TILE), jnp.float32),
             pltpu.VMEM((ROWS, COLS), jnp.float32),
             pltpu.SemaphoreType.DMA,
             pltpu.SemaphoreType.DMA((4,)),
@@ -654,11 +667,9 @@
 def per_device(initial_states, sources, tile_class, coeff_sets, coarse_maps):
     state, source, own_map = initial_states[0], sources[0], coarse_maps[0]
     core = lax.axis_index("tm") % 2
-    wide = 2 * STEPS
-
     other_map = swapped(own_map)
-    upper = shifted(jnp.concatenate([state[-wide:], source[-wide:]], axis=0), 0, 1)
-    lower = shifted(jnp.concatenate([state[:wide], source[:wide]], axis=0), 0, -1)
+    upper = shifted(jnp.concatenate([state[-STEPS:], source[-STEPS:]], axis=0), 0, 1)
+    lower = shifted(jnp.concatenate([state[:STEPS], source[:STEPS]], axis=0), 0, -1)
 
     product, half, columns, coef = pair_product(tile_class, coeff_sets, own_map, other_map, state)
     product, half, columns, upper, lower = lax.optimization_barrier((product, half, columns, upper, lower))
@@ -666,7 +677,7 @@
     far_same = across(half)
     next_columns = shifted(columns, -1)
 
-    finished, means, kept_means, kept_sources = first_sweep(coef, upper, state, source, lower)
+    finished, means, top, bottom, kept_means, forcing = first_sweep(coef, upper, state, source, lower)
     near, far_same, next_columns, means, finished = lax.optimization_barrier(
         (near, far_same, next_columns, means, finished)
     )
@@ -677,10 +688,10 @@
 
     got = exchanged(message(means, next_columns[LOCAL : LOCAL + 1, :TILE], next_columns))
 
-    got, far, near_second, far_second, finished = lax.optimization_barrier(
-        (got, far, near_second, far_second, finished)
+    got, far, near_second, far_second, finished, top, bottom = lax.optimization_barrier(
+        (got, far, near_second, far_second, finished, top, bottom)
     )
-    previous = shifted(finished, 1)
+    previous = shifted(bottom, 1, 1), shifted(finished, 1), shifted(top, 1, -1)
     whole = [near, swapped(near), far, swapped(far), product]
     halved = []
     for part in (near_second, far_same, far_second):
@@ -691,7 +702,7 @@
     own_part, other_part = correction[:, COARSE:], partner[:, COARSE:]
 
     finished, block = second_sweep(
-        coef, here, kept_means, own_part, other_part, columns, next_columns, previous, kept_sources
+        coef, here, kept_means, own_part, other_part, columns, next_columns, previous, forcing
     )
     previous = shifted(finished, 1)
     got = exchanged(block)

time: 115 us -> 111 us (0.965)
  blocking collectives: 19.6 us -> 0 us
  starting transfers between devices: 33 us -> 44.8 us
  waiting for transfers between devices: 22.2 us -> 28 us
  Pallas kernels: 36.7 us -> 33.6 us
    all_to_all x1 -> x0, blocking collectives: 19.6 us -> none  [exchanged(): lax.all_to_all(block, ('tm', 'space'), 0, 0, tiled=True)]
    all_to_all x1 -> x2, waiting for transfers between devices: 12 us -> 22.6 us  [exchanged(): lax.all_to_all(block, ('tm', 'space'), 0, 0, tiled=True)]
    all_to_all x1 -> x2, starting transfers between devices: 9.45 us -> 16.3 us  [exchanged(): lax.all_to_all(block, ('tm', 'space'), 0, 0, tiled=True)]
    pallas_call x2, Pallas kernels: 21.8 us -> 17.1 us  [fine_call(): pl.pallas_call(functools.partial(fine_kernel, corrected), cost_estimate=c...]
    ppermute x12, starting transfers between devices: 13.6 us -> 16.8 us  [moved(): return lax.ppermute(value, ('tm', 'space'), pairs)]
    ppermute x5 -> x7, waiting for transfers between devices: 2.58 us -> 0.02 us  [shifted(): return lax.ppermute(value, ('tm', 'space'), pairs)]
    ppermute x12, waiting for transfers between devices: 7.64 us -> 5.37 us  [moved(): return lax.ppermute(value, ('tm', 'space'), pairs)]
    ppermute x5 -> x7, starting transfers between devices: 9.94 us -> 11.7 us  [shifted(): return lax.ppermute(value, ('tm', 'space'), pairs)]
  transfers between devices with their start and end apart: 18 -> 21, of which waited for: 6 -> 5; matrix products, arithmetic and copies ran while one was open for 1% -> 2% of each run, Pallas kernels for 17% -> 16%
where the time goes in v5:
time: 111 us
  starting transfers between devices  44.8 us (40%)
  Pallas kernels  33.6 us (30%)
  waiting for transfers between devices  28 us (25%)
  local copies, waits for them, and re-layouts  3.76 us (3%)
    all_to_all x2, waiting for transfers between devices, exchanged(): lax.all_to_all(block, ('tm', 'space'), 0, 0, tiled=True)  22.6 us
    pallas_call x2, Pallas kernels, fine_call(): pl.pallas_call(functools.partial(fine_kernel, corrected), cost_estimate=c...  17.1 us
    ppermute x12, starting transfers between devices, moved(): return lax.ppermute(value, ('tm', 'space'), pairs)  16.8 us
    all_to_all x2, starting transfers between devices, exchanged(): lax.all_to_all(block, ('tm', 'space'), 0, 0, tiled=True)  16.3 us
    ppermute x7, starting transfers between devices, shifted(): return lax.ppermute(value, ('tm', 'space'), pairs)  11.7 us
    pallas_call x1, Pallas kernels, last_chain(): pl.pallas_call(last_chain_kernel, cost_estimate=cost(6), out_shape=jax.Sh...  6.32 us
    pallas_call x1, Pallas kernels, first_chain(): pl.pallas_call(first_chain_kernel, cost_estimate=cost(5), out_shape=(jax....  5.9 us
    ppermute x12, waiting for transfers between devices, moved(): return lax.ppermute(value, ('tm', 'space'), pairs)  5.37 us
  transfers between devices with their start and end apart: 21, of which 5 were waited for; matrix products, arithmetic and copies ran while one was open for 2% of the time, Pallas kernels for 16%

profile of v5, /device:TPU:1, one launch (start us, length us, event | category | flops | bytes accessed | tf_op | source)
XLA Modules:
  0.0 110.5 jit_solution(8148329487652823787)
XLA Ops:
  0.0 1.4 %collective-permute-start = (f32[512,512]{1,0:T(8,128)}, f32[512,512]{1,0:T(8,128)S(1)}, u32[]{:S(2)}, u32[]{:S(2)}) collective-permute-start(f32[512,512]{1,0:T(8,128)} %bitcast.21), channel_id=1, source_target_pairs={{0,8},{1,9},{2,10},{3,11},{4,12},{5,13},{6,14},{7,15},{8,0},{9,1},... | collective-permute-start | bytes 3145736 | tf_op jit(solution)/shard_map/ppermute | solution.py:46
  1.4 1.0 slice_bitcast_fusion
  2.4 1.4 %collective-permute-start.1 = (f32[16,2048]{1,0:T(8,128)S(1)}, f32[16,2048]{1,0:T(8,128)S(1)}, u32[]{:S(2)}, u32[]{:S(2)}) collective-permute-start(f32[16,2048]{1,0:T(8,128)S(1)} %pad_maximum_fusion), channel_id=1, source_target_pairs={{0,1},{1,2},{2,3},{3,4},{4,5},{5,6},{6,7},{7,0},{8,9},{9,10},{10,1... | collective-permute-start | bytes 393224 | tf_op jit(solution)/shard_map/ppermute | solution.py:55
  3.8 4.7 %collective-permute-start.2 = (f32[16,2048]{1,0:T(8,128)S(1)}, f32[16,2048]{1,0:T(8,128)S(1)}, u32[]{:S(2)}, u32[]{:S(2)}) collective-permute-start(f32[16,2048]{1,0:T(8,128)S(1)} %pad_maximum_fusion.1), channel_id=1, source_target_pairs={{0,7},{1,0},{2,1},{3,2},{4,3},{5,4},{6,5},{7,6},{8,15},{9,8},{10,9... | collective-permute-start | bytes 393224 | tf_op jit(solution)/shard_map/ppermute | solution.py:55
  8.4 4.1 %shard_map.55 = (f32[512,512]{1,0:T(8,128)S(1)}, f32[256,512]{1,0:T(8,128)S(1)}, f32[72,512]{1,0:T(8,128)}, f32[16,15,8,128]{3,2,1,0:T(8,128)S(1)}) custom-call(s32[8,16]{1,0:T(8,128)} %class_ref.1, f32[3,8]{1,0:T(4,128)} %sets_ref.1, f32[512,512]{1,0:T(8,128)} %bitcast.22, f32[512,512]{1,0:T(8,128)S(1)} %collective-permute-done.other_ref, f32[128,2048]{1,0:T(8,128)} %bitcast.19), custom_call_target="tpu_custom_call" | custom-call | bytes 10800000 | tf_op jit(solution)/shard_map/pallas_call | solution.py:164
  12.5 2.8 %collective-permute-start.3 = (f32[512,512]{1,0:T(8,128)S(1)}, f32[512,512]{1,0:T(8,128)S(1)}, u32[]{:S(2)}, u32[]{:S(2)}) collective-permute-start(f32[512,512]{1,0:T(8,128)S(1)} %get-tuple-element.40.refs_4_), channel_id=1, source_target_pairs={{0,16},{1,17},{2,18},{3,19},{4,20},{5,21},{6,22},{7,23},{8,56},{9,... | collective-permute-start | bytes 3145736 | tf_op jit(solution)/shard_map/ppermute | solution.py:46
  15.3 3.0 %collective-permute-start.4 = (f32[256,512]{1,0:T(8,128)S(1)}, f32[256,512]{1,0:T(8,128)S(1)}, u32[]{:S(2)}, u32[]{:S(2)}) collective-permute-start(f32[256,512]{1,0:T(8,128)S(1)} %get-tuple-element.41), channel_id=1, source_target_pairs={{0,64},{1,65},{2,66},{3,67},{4,68},{5,69},{6,70},{7,71},{8,76},{9,... | collective-permute-start | bytes 1572872 | tf_op jit(solution)/shard_map/ppermute | solution.py:46
  18.4 8.0 %shard_map.56 = (f32[16,128,128]{2,1,0:T(8,128)}, f32[1,128]{1,0:T(1,128)S(1)}, f32[8,2048]{1,0:T(8,128)S(1)}, f32[8,2048]{1,0:T(8,128)S(1)}, f32[1,128]{1,0:T(1,128)}, /*index=5*/f32[16,144,128]{2,1,0:T(8,128)}) custom-call(f32[16,15,8,128]{3,2,1,0:T(8,128)S(1)} %get-tuple-element.36.coef, f32[16,2048]{1,0:T(8,128)S(1)} %collective-permute-done.1.refs_0_, ...), custom_call_target="tpu_custom_call" | custom-call | bytes 36000000 | tf_op jit(solution)/shard_map/pallas_call | solution.py:336
  26.4 0.6 copy-done.2
  27.0 0.6 copy-done.3
  27.6 1.0 collective-permute-done.3.refs_0_
  28.7 3.0 %collective-permute-start.6 = (f32[512,512]{1,0:T(8,128)S(1)}, f32[512,512]{1,0:T(8,128)}, u32[]{:S(2)}, u32[]{:S(2)}) collective-permute-start(f32[512,512]{1,0:T(8,128)S(1)} %collective-permute-done.3.refs_0_), channel_id=1, source_target_pairs={{0,64},{1,65},{2,66},{3,67},{4,68},{5,69},{6,70},{7,71},{8,76},{9,... | collective-permute-start | bytes 3145736 | tf_op jit(solution)/shard_map/ppermute | solution.py:46
  31.7 0.8 constant_dynamic-slice_fusion
  32.5 3.0 %collective-permute-start.8 = (f32[256,512]{1,0:T(8,128)}, f32[256,512]{1,0:T(8,128)}, u32[]{:S(2)}, u32[]{:S(2)}) collective-permute-start(f32[256,512]{1,0:T(8,128)} %constant_dynamic-slice_fusion), channel_id=1, source_target_pairs={{0,80},{1,81},{2,82},{3,83},{4,84},{5,85},{6,86},{7,87},{8,124},{9... | collective-permute-start | bytes 1572872 | tf_op jit(solution)/shard_map/ppermute | solution.py:46
  35.7 0.2 shard_map.57
  35.9 0.7 copy-done
  36.6 8.2 %all-to-all-start = ((f32[128,1,640]{2,1,0:T(1,128)}), f32[128,1,640]{2,1,0:T(1,128)S(1)}, u32[]{:S(2)}, u32[]{:S(2)}) async-start(f32[128,1,640]{2,1,0:T(1,128)} %bitcast.18), calls=%async_computation | async-start | bytes 655360 | tf_op jit(solution)/shard_map/all_to_all | solution.py:652
  44.8 1.1 %collective-permute-start.9 = (f32[512,512]{1,0:T(8,128)S(1)}, f32[512,512]{1,0:T(8,128)}, u32[]{:S(2)}, u32[]{:S(2)}) collective-permute-start(f32[512,512]{1,0:T(8,128)S(1)} %collective-permute-done.3.refs_0_), channel_id=1, source_target_pairs={{0,8},{1,9},{2,10},{3,11},{4,12},{5,13},{6,14},{7,15},{8,0},{9,1},... | collective-permute-start | bytes 3145736 | tf_op jit(solution)/shard_map/ppermute | solution.py:46
  46.1 9.7 %all-to-all-done = f32[128,1,640]{2,1,0:T(1,128)S(1)} async-done(((f32[128,1,640]{2,1,0:T(1,128)}), f32[128,1,640]{2,1,0:T(1,128)S(1)}, u32[]{:S(2)}, u32[]{:S(2)}) %all-to-all-start) | async-done | bytes 327712 | tf_op jit(solution)/shard_map/all_to_all | solution.py:652
  55.8 1.5 %collective-permute-start.10 = (f32[512,512]{1,0:T(8,128)}, f32[512,512]{1,0:T(8,128)S(1)}, u32[]{:S(2)}, u32[]{:S(2)}) collective-permute-start(f32[512,512]{1,0:T(8,128)} %collective-permute-done.6.refs_2_), channel_id=1, source_target_pairs={{0,8},{1,9},{2,10},{3,11},{4,12},{5,13},{6,14},{7,15},{8,0},{9,1},... | collective-permute-start | bytes 3145736 | tf_op jit(solution)/shard_map/ppermute | solution.py:46
  57.3 0.3 collective-permute-start.16
  57.8 0.3 collective-permute-start.13
  58.1 0.6 collective-permute-start.15
  58.7 3.2 %collective-permute-done.11.refs_6_ = f32[256,512]{1,0:T(8,128)S(1)} collective-permute-done((f32[256,512]{1,0:T(8,128)}, f32[256,512]{1,0:T(8,128)S(1)}, u32[]{:S(2)}, u32[]{:S(2)}) %collective-permute-start.11) | collective-permute-done | bytes 524320 | tf_op jit(solution)/shard_map/ppermute | solution.py:46
  61.9 2.7 %collective-permute-start.17 = (f32[8,2048]{1,0:T(8,128)}, f32[8,2048]{1,0:T(8,128)S(1)}, u32[]{:S(2)}, u32[]{:S(2)}) collective-permute-start(f32[8,2048]{1,0:T(8,128)} %copy-done.2), channel_id=1, source_target_pairs={{0,15},{1,8},{2,9},{3,10},{4,11},{5,12},{6,13},{7,14},{8,23},{9,16... | collective-permute-start | bytes 196616 | tf_op jit(solution)/shard_map/ppermute | solution.py:55
  64.6 5.9 %shard_map.58 = (f32[1,640]{1,0:T(1,128)S(1)}, f32[9,512,512]{2,1,0:T(8,128)}) custom-call(f32[640,128]{1,0:T(8,128)S(1)} %bitcast.16, f32[512,512]{1,0:T(8,128)S(1)} %collective-permute-done.other_ref, f32[512,512]{1,0:T(8,128)S(1)} %collective-permute-done.3.refs_0_, f32[512,512]{1,0:T(8,128)} %collective-permute-done.9.refs_1_, ...), custom_call_target="tpu_custom_call" | custom-call | bytes 18000000 | tf_op jit(solution)/shard_map/pallas_call | solution.py:559
  70.6 1.1 %collective-permute-done.14 = f32[1,640]{1,0:T(1,128)S(1)} collective-permute-done((f32[1,640]{1,0:T(1,128)S(1)}, f32[1,640]{1,0:T(1,128)S(1)}, u32[]{:S(2)}, u32[]{:S(2)}) %collective-permute-start.14) | collective-permute-done | bytes 2592 | tf_op jit(solution)/shard_map/ppermute | solution.py:46
  71.8 9.1 %shard_map.59 = (f32[16,128,128]{2,1,0:T(8,128)}, f32[640,128]{1,0:T(8,128)}) custom-call(f32[16,15,8,128]{3,2,1,0:T(8,128)S(1)} %get-tuple-element.36.coef, f32[1,512]{1,0:T(1,128)S(1)} %slice.48.refs_0_.own_ref, f32[1,128]{1,0:T(1,128)} %get-tuple-element.59.refs_1_, f32[1,128]{1,0:T(1,128)S(1)} %slice.49.refs_2_, f32[1,128]{1,0:T(1,128)S(1)} %slice.52.refs_3_, ...), custom_call_target="tpu_custom_call" | custom-call | bytes 36000000 | tf_op jit(solution)/shard_map/pallas_call | solution.py:336
  80.8 2.1 %collective-permute-start.18 = (f32[16,128,128]{2,1,0:T(8,128)}, f32[16,128,128]{2,1,0:T(8,128)S(1)}, u32[]{:S(2)}, u32[]{:S(2)}) collective-permute-start(f32[16,128,128]{2,1,0:T(8,128)} %get-tuple-element.66), channel_id=1, source_target_pairs={{0,8},{1,9},{2,10},{3,11},{4,12},{5,13},{6,14},{7,15},{8,16},{9,17... | collective-permute-start | bytes 3145736 | tf_op jit(solution)/shard_map/ppermute | solution.py:55
  82.9 8.1 %all-to-all-start.1 = ((f32[128,1,640]{2,1,0:T(1,128)}), f32[128,1,640]{2,1,0:T(1,128)S(1)}, u32[]{:S(2)}, u32[]{:S(2)}) async-start(f32[128,1,640]{2,1,0:T(1,128)} %bitcast.9), calls=%async_computation.1 | async-start | bytes 655360 | tf_op jit(solution)/shard_map/all_to_all | solution.py:652
  91.1 12.9 %all-to-all-done.1 = f32[128,1,640]{2,1,0:T(1,128)S(1)} async-done(((f32[128,1,640]{2,1,0:T(1,128)}), f32[128,1,640]{2,1,0:T(1,128)S(1)}, u32[]{:S(2)}, u32[]{:S(2)}) %all-to-all-start.1) | async-done | bytes 327712 | tf_op jit(solution)/shard_map/all_to_all | solution.py:652
  104.0 6.3 %shard_map.60 = f32[128,2048]{1,0:T(8,128)} custom-call(f32[640,128]{1,0:T(8,128)S(1)} %bitcast.17, f32[1,512]{1,0:T(1,128)S(1)} %slice.48.refs_0_.own_ref, f32[1,512]{1,0:T(1,128)S(1)} %slice.53.partner_ref, f32[512,512]{1,0:T(8,128)} %bitcast.23, f32[9,512,512]{2,1,0:T(8,128)} %get-tuple-element.65.maps_ref, f32[16,128,128]{2,1,0:T(8,128)S(1)} %collective-permute-done.18.u_ref), custom_call_target="tpu_custom_call" | custom-call | bytes 21600000 | tf_op jit(solution)/shard_map/pallas_call | solution.py:631
  (35 shorter events, 0.6 us)
Async XLA Ops:
  0.0 8.4 %collective-permute-start = (f32[512,512]{1,0:T(8,128)}, f32[512,512]{1,0:T(8,128)S(1)}, u32[]{:S(2)}, u32[]{:S(2)}) collective-permute-start(f32[512,512]{1,0:T(8,128)} %bitcast.21), channel_id=1, source_target_pairs={{0,8},{1,9},{2,10},{3,11},{4,12},{5,13},{6,14},{7,15},{8,0},{9,1},... | collective-permute-start | bytes 3145736 | tf_op jit(solution)/shard_map/ppermute | solution.py:46
  2.4 10.1 %collective-permute-start.1 = (f32[16,2048]{1,0:T(8,128)S(1)}, f32[16,2048]{1,0:T(8,128)S(1)}, u32[]{:S(2)}, u32[]{:S(2)}) collective-permute-start(f32[16,2048]{1,0:T(8,128)S(1)} %pad_maximum_fusion), channel_id=1, source_target_pairs={{0,1},{1,2},{2,3},{3,4},{4,5},{5,6},{6,7},{7,0},{8,9},{9,10},{10,1... | collective-permute-start | bytes 393224 | tf_op jit(solution)/shard_map/ppermute | solution.py:55
  3.8 8.8 %collective-permute-start.2 = (f32[16,2048]{1,0:T(8,128)S(1)}, f32[16,2048]{1,0:T(8,128)S(1)}, u32[]{:S(2)}, u32[]{:S(2)}) collective-permute-start(f32[16,2048]{1,0:T(8,128)S(1)} %pad_maximum_fusion.1), channel_id=1, source_target_pairs={{0,7},{1,0},{2,1},{3,2},{4,3},{5,4},{6,5},{7,6},{8,15},{9,8},{10,9... | collective-permute-start | bytes 393224 | tf_op jit(solution)/shard_map/ppermute | solution.py:55
  12.5 16.2 %copy-start.1 = (f32[512,512]{1,0:T(8,128)}, f32[512,512]{1,0:T(8,128)S(1)}, u32[]{:S(2)}) copy-start(f32[512,512]{1,0:T(8,128)S(1)} %get-tuple-element.40.refs_4_) | copy-start | bytes 3145732
  12.5 16.1 %collective-permute-start.3 = (f32[512,512]{1,0:T(8,128)S(1)}, f32[512,512]{1,0:T(8,128)S(1)}, u32[]{:S(2)}, u32[]{:S(2)}) collective-permute-start(f32[512,512]{1,0:T(8,128)S(1)} %get-tuple-element.40.refs_4_), channel_id=1, source_target_pairs={{0,16},{1,17},{2,18},{3,19},{4,20},{5,21},{6,22},{7,23},{8,56},{9,... | collective-permute-start | bytes 3145736 | tf_op jit(solution)/shard_map/ppermute | solution.py:46
  15.3 12.3 %collective-permute-start.4 = (f32[256,512]{1,0:T(8,128)S(1)}, f32[256,512]{1,0:T(8,128)S(1)}, u32[]{:S(2)}, u32[]{:S(2)}) collective-permute-start(f32[256,512]{1,0:T(8,128)S(1)} %get-tuple-element.41), channel_id=1, source_target_pairs={{0,64},{1,65},{2,66},{3,67},{4,68},{5,69},{6,70},{7,71},{8,76},{9,... | collective-permute-start | bytes 1572872 | tf_op jit(solution)/shard_map/ppermute | solution.py:46
  18.4 9.3 %collective-permute-start.5 = (f32[72,512]{1,0:T(8,128)}, f32[72,512]{1,0:T(8,128)S(1)}, u32[]{:S(2)}, u32[]{:S(2)}) collective-permute-start(f32[72,512]{1,0:T(8,128)} %get-tuple-element.42.refs_4_), channel_id=1, source_target_pairs={{0,120},{1,121},{2,122},{3,123},{4,124},{5,125},{6,126},{7,127},{8... | collective-permute-start | bytes 442376 | tf_op jit(solution)/shard_map/ppermute | solution.py:55
  26.4 0.6 copy-start.2
  27.0 0.6 copy-start.3
  27.6 1.0 copy-start.4
  28.7 27.1 %collective-permute-start.6 = (f32[512,512]{1,0:T(8,128)S(1)}, f32[512,512]{1,0:T(8,128)}, u32[]{:S(2)}, u32[]{:S(2)}) collective-permute-start(f32[512,512]{1,0:T(8,128)S(1)} %collective-permute-done.3.refs_0_), channel_id=1, source_target_pairs={{0,64},{1,65},{2,66},{3,67},{4,68},{5,69},{6,70},{7,71},{8,76},{9,... | collective-permute-start | bytes 3145736 | tf_op jit(solution)/shard_map/ppermute | solution.py:46
  32.5 23.2 %collective-permute-start.8 = (f32[256,512]{1,0:T(8,128)}, f32[256,512]{1,0:T(8,128)}, u32[]{:S(2)}, u32[]{:S(2)}) collective-permute-start(f32[256,512]{1,0:T(8,128)} %constant_dynamic-slice_fusion), channel_id=1, source_target_pairs={{0,80},{1,81},{2,82},{3,83},{4,84},{5,85},{6,86},{7,87},{8,124},{9... | collective-permute-start | bytes 1572872 | tf_op jit(solution)/shard_map/ppermute | solution.py:46
  35.5 20.2 %collective-permute-start.7 = (f32[256,512]{1,0:T(8,128)}, f32[256,512]{1,0:T(8,128)}, u32[]{:S(2)}, u32[]{:S(2)}) collective-permute-start(f32[256,512]{1,0:T(8,128)} %constant_dynamic-slice_fusion), channel_id=1, source_target_pairs={{0,16},{1,17},{2,18},{3,19},{4,20},{5,21},{6,22},{7,23},{8,56},{9,... | collective-permute-start | bytes 1572872 | tf_op jit(solution)/shard_map/ppermute | solution.py:46
  35.9 0.7 copy-start
  36.6 19.1 %all-to-all-start = ((f32[128,1,640]{2,1,0:T(1,128)}), f32[128,1,640]{2,1,0:T(1,128)S(1)}, u32[]{:S(2)}, u32[]{:S(2)}) async-start(f32[128,1,640]{2,1,0:T(1,128)} %bitcast.18), calls=%async_computation | async-start | bytes 655360 | tf_op jit(solution)/shard_map/all_to_all | solution.py:652
  44.8 13.3 %collective-permute-start.9 = (f32[512,512]{1,0:T(8,128)S(1)}, f32[512,512]{1,0:T(8,128)}, u32[]{:S(2)}, u32[]{:S(2)}) collective-permute-start(f32[512,512]{1,0:T(8,128)S(1)} %collective-permute-done.3.refs_0_), channel_id=1, source_target_pairs={{0,8},{1,9},{2,10},{3,11},{4,12},{5,13},{6,14},{7,15},{8,0},{9,1},... | collective-permute-start | bytes 3145736 | tf_op jit(solution)/shard_map/ppermute | solution.py:46
  46.0 11.8 %collective-permute-start.12 = (f32[256,512]{1,0:T(8,128)}, f32[256,512]{1,0:T(8,128)}, u32[]{:S(2)}, u32[]{:S(2)}) collective-permute-start(f32[256,512]{1,0:T(8,128)} %copy-done.4), channel_id=1, source_target_pairs={{0,8},{1,9},{2,10},{3,11},{4,12},{5,13},{6,14},{7,15},{8,0},{9,1},... | collective-permute-start | bytes 1572872 | tf_op jit(solution)/shard_map/ppermute | solution.py:46
  55.8 8.8 %collective-permute-start.10 = (f32[512,512]{1,0:T(8,128)}, f32[512,512]{1,0:T(8,128)S(1)}, u32[]{:S(2)}, u32[]{:S(2)}) collective-permute-start(f32[512,512]{1,0:T(8,128)} %collective-permute-done.6.refs_2_), channel_id=1, source_target_pairs={{0,8},{1,9},{2,10},{3,11},{4,12},{5,13},{6,14},{7,15},{8,0},{9,1},... | collective-permute-start | bytes 3145736 | tf_op jit(solution)/shard_map/ppermute | solution.py:46
  57.3 14.5 %collective-permute-start.16 = (f32[16,128,128]{2,1,0:T(8,128)}, f32[16,128,128]{2,1,0:T(8,128)S(1)}, u32[]{:S(2)}, u32[]{:S(2)}) collective-permute-start(f32[16,128,128]{2,1,0:T(8,128)} %get-tuple-element.61), channel_id=1, source_target_pairs={{0,8},{1,9},{2,10},{3,11},{4,12},{5,13},{6,14},{7,15},{8,16},{9,17... | collective-permute-start | bytes 3145736 | tf_op jit(solution)/shard_map/ppermute | solution.py:55
  57.6 4.3 %collective-permute-start.11 = (f32[256,512]{1,0:T(8,128)}, f32[256,512]{1,0:T(8,128)S(1)}, u32[]{:S(2)}, u32[]{:S(2)}) collective-permute-start(f32[256,512]{1,0:T(8,128)} %collective-permute-done.7.refs_5_), channel_id=1, source_target_pairs={{0,8},{1,9},{2,10},{3,11},{4,12},{5,13},{6,14},{7,15},{8,0},{9,1},... | collective-permute-start | bytes 1572872 | tf_op jit(solution)/shard_map/ppermute | solution.py:46
  57.8 6.8 %collective-permute-start.13 = (f32[256,512]{1,0:T(8,128)}, f32[256,512]{1,0:T(8,128)S(1)}, u32[]{:S(2)}, u32[]{:S(2)}) collective-permute-start(f32[256,512]{1,0:T(8,128)} %collective-permute-done.8.refs_9_), channel_id=1, source_target_pairs={{0,8},{1,9},{2,10},{3,11},{4,12},{5,13},{6,14},{7,15},{8,0},{9,1},... | collective-permute-start | bytes 1572872 | tf_op jit(solution)/shard_map/ppermute | solution.py:46
  58.1 13.6 %collective-permute-start.15 = (f32[8,2048]{1,0:T(8,128)}, f32[8,2048]{1,0:T(8,128)S(1)}, u32[]{:S(2)}, u32[]{:S(2)}) collective-permute-start(f32[8,2048]{1,0:T(8,128)} %copy-done.3), channel_id=1, source_target_pairs={{0,9},{1,10},{2,11},{3,12},{4,13},{5,14},{6,15},{7,8},{8,17},{9,18... | collective-permute-start | bytes 196616 | tf_op jit(solution)/shard_map/ppermute | solution.py:55
  61.9 9.8 %collective-permute-start.17 = (f32[8,2048]{1,0:T(8,128)}, f32[8,2048]{1,0:T(8,128)S(1)}, u32[]{:S(2)}, u32[]{:S(2)}) collective-permute-start(f32[8,2048]{1,0:T(8,128)} %copy-done.2), channel_id=1, source_target_pairs={{0,15},{1,8},{2,9},{3,10},{4,11},{5,12},{6,13},{7,14},{8,23},{9,16... | collective-permute-start | bytes 196616 | tf_op jit(solution)/shard_map/ppermute | solution.py:55
  70.5 1.2 %collective-permute-start.14 = (f32[1,640]{1,0:T(1,128)S(1)}, f32[1,640]{1,0:T(1,128)S(1)}, u32[]{:S(2)}, u32[]{:S(2)}) collective-permute-start(f32[1,640]{1,0:T(1,128)S(1)} %get-tuple-element.58), channel_id=1, source_target_pairs={{0,8},{1,9},{2,10},{3,11},{4,12},{5,13},{6,14},{7,15},{8,0},{9,1},... | collective-permute-start | bytes 7688 | tf_op jit(solution)/shard_map/ppermute | solution.py:46
  80.8 23.2 %collective-permute-start.18 = (f32[16,128,128]{2,1,0:T(8,128)}, f32[16,128,128]{2,1,0:T(8,128)S(1)}, u32[]{:S(2)}, u32[]{:S(2)}) collective-permute-start(f32[16,128,128]{2,1,0:T(8,128)} %get-tuple-element.66), channel_id=1, source_target_pairs={{0,8},{1,9},{2,10},{3,11},{4,12},{5,13},{6,14},{7,15},{8,16},{9,17... | collective-permute-start | bytes 3145736 | tf_op jit(solution)/shard_map/ppermute | solution.py:55
  82.9 21.1 %all-to-all-start.1 = ((f32[128,1,640]{2,1,0:T(1,128)}), f32[128,1,640]{2,1,0:T(1,128)S(1)}, u32[]{:S(2)}, u32[]{:S(2)}) async-start(f32[128,1,640]{2,1,0:T(1,128)} %bitcast.9), calls=%async_computation.1 | async-start | bytes 655360 | tf_op jit(solution)/shard_map/all_to_all | solution.py:652

commit v6 on v5

--- a/solution.py
+++ b/solution.py
@@ -17,6 +17,7 @@
 TILES = COLS // TILE
 EXT = ROWS + 2 * STEPS
 LINES = EXT // 8
+PARTS = 4
 LOCAL = 64
 PIECES = 5
 STEP = 0.6
@@ -189,15 +190,16 @@
         c_ref, means_ref, own_ref, other_ref, own_columns_ref, columns_ref, *refs = refs
         up_ref, u_ref, down_ref, f_ref, fin_ref, out_ref, *refs = refs
         block, means_scratch, columns_scratch, extra, u_ext, first, second, force, sums_ref, sems = refs
-        fields = [
-            pltpu.make_async_copy(u_ref, u_ext.at[:, pl.ds(STEPS, ROWS)], extra.at[0]),
-            pltpu.make_async_copy(f_ref, force, extra.at[1]),
+        states, forces = [], []
+        for n in range(PARTS):
+            tiles = pl.ds(n * TILES // PARTS, TILES // PARTS)
+            states.append(pltpu.make_async_copy(u_ref.at[tiles], u_ext.at[tiles, pl.ds(STEPS, ROWS)], sems.at[n]))
+            forces.append(pltpu.make_async_copy(f_ref.at[tiles], force.at[tiles], sems.at[PARTS + n]))
+        needed = [
+            pltpu.make_async_copy(means_ref, means_scratch, extra.at[0]),
+            pltpu.make_async_copy(own_columns_ref, columns_scratch, extra.at[1]),
         ]
-        needed = [
-            pltpu.make_async_copy(means_ref, means_scratch, extra.at[2]),
-            pltpu.make_async_copy(own_columns_ref, columns_scratch, extra.at[3]),
-        ]
-        for copy in fields + needed:
+        for copy in states + forces + needed:
             copy.start()
     else:
         up_ref, u_ref, f_ref, down_ref, fin_ref, out_ref, top_ref, bottom_ref, means_ref, force_ref, *refs = refs
@@ -224,15 +226,21 @@
         if not corrected:
             f_ext[k, 0:STEPS, :] = up_ref[STEPS : 2 * STEPS, cols]
             f_ext[k, STEPS + ROWS : EXT, :] = down_ref[STEPS : 2 * STEPS, cols]
+    quarter, places = [], []
     if corrected:
-        for copy in fields:
-            copy.wait()
+        for line in range(4):
+            block_row = lax.rem(2 * strip + 15 + line, 16)
+            cols = pl.ds(pl.multiple_of(block_row // 4 * TILE, TILE), TILE)
+            quarter.append(jnp.broadcast_to(c_ref[:, cols], (8, TILE)))
+            places.append(lax.rem(block_row, 4) * 32)
     for k in range(TILES):
         if corrected:
+            if k % (TILES // PARTS) == 0:
+                states[k * PARTS // TILES].wait()
             added = []
             for line in range(4):
-                at = lax.rem(2 * strip + 15 + line, 16) * 32 + 2 * k
-                added.append(jnp.where(lane < BLK, c_ref[0, at], c_ref[0, at + 1]))
+                at = jnp.where(lane < BLK, 2 * k, 2 * k + 1) + places[line]
+                added.append(jnp.take_along_axis(quarter[line], at, axis=1))
         else:
             for copy in copies[k]:
                 copy.wait()
@@ -251,7 +259,10 @@
                 force[k, rows, :] = STEP * f_ext[k, pl.ds(i, 8, stride=LINES), :]
             first[k, rows, :] = value
     results = []
-    if not corrected:
+    if corrected:
+        for copy in forces:
+            copy.wait()
+    else:
         results.append(pltpu.make_async_copy(force, force_ref, f_sems.at[0]))
         results[0].start()
 
@@ -297,10 +308,10 @@
             sums_ref[pl.ds(br * TILES + k, 1), :] = jnp.sum(part, axis=0, keepdims=True)
         return carry
 
-    for part in range(2):
-        half = TILES // 2
+    for part in range(4):
+        half = TILES // 4
         tiles = pl.ds(part * half, half)
-        lax.fori_loop(part * half, (part + 1) * half, last_tile, 0, unroll=8)
+        lax.fori_loop(part * half, (part + 1) * half, last_tile, 0, unroll=4)
         copy = pltpu.make_async_copy(u_ext.at[tiles, pl.ds(STEPS, ROWS)], fin_ref.at[tiles], sems.at[part])
         copy.start()
         results.append(copy)
@@ -374,14 +385,14 @@
     means, columns, forcing = in_hbm(means, columns, forcing)
     return fine_call(
         True,
-        [VMEM, SMEM, HBM, VMEM, VMEM, HBM, VMEM, VMEM, ANY, VMEM, HBM],
+        [VMEM, VMEM, HBM, VMEM, VMEM, HBM, VMEM, VMEM, ANY, VMEM, HBM],
         (jax.ShapeDtypeStruct((128 * PIECES, TILE), jnp.float32),),
         (VMEM,),
         [
             pltpu.VMEM((8 * PIECES, TILE), jnp.float32),
             pltpu.VMEM((1, TILE), jnp.float32),
             pltpu.VMEM((LOCAL + 8, COARSE), jnp.float32),
-            pltpu.SemaphoreType.DMA((4,)),
+            pltpu.SemaphoreType.DMA((2,)),
         ],
         (coef, correction, means, own_part, other_part, columns, next_columns, *state, forcing),
     )
@@ -403,20 +414,27 @@
         out_ref[n * 8 * PIECES : (n + 1) * 8 * PIECES, :] = block[...]
 
 
-def message_kernel(means_ref, base_ref, columns_ref, out_ref, block):
+def message_kernel(means_ref, base_ref, columns_ref, out_ref, block, out, sem):
     defect = means_ref[...] - base_ref[...]
     strip, _, _, _ = position()
-    write_message(strip, rows_times(defect, columns_ref[0:LOCAL, :]), defect, block, out_ref)
+    write_message(strip, rows_times(defect, columns_ref[0:LOCAL, :]), defect, block, out)
+    sent = pltpu.make_async_copy(out, out_ref, sem)
+    sent.start()
+    sent.wait()
 
 
 def message(means, base, columns):
     return pl.pallas_call(
         message_kernel,
         cost_estimate=cost(1),
-        out_shape=jax.ShapeDtypeStruct((128 * PIECES, TILE), jnp.float32),
+        out_shape=pltpu.HBM((128 * PIECES, TILE), jnp.float32),
         in_specs=[VMEM, VMEM, VMEM],
-        out_specs=VMEM,
-        scratch_shapes=[pltpu.VMEM((8 * PIECES, TILE), jnp.float32)],
+        out_specs=HBM,
+        scratch_shapes=[
+            pltpu.VMEM((8 * PIECES, TILE), jnp.float32),
+            pltpu.VMEM((128 * PIECES, TILE), jnp.float32),
+            pltpu.SemaphoreType.DMA,
+        ],
         compiler_params=pltpu.CompilerParams(vmem_limit_bytes=16 << 20),
     )(means, base, columns)
 
@@ -678,15 +696,16 @@
     next_columns = shifted(columns, -1)
 
     finished, means, top, bottom, kept_means, forcing = first_sweep(coef, upper, state, source, lower)
-    near, far_same, next_columns, means, finished = lax.optimization_barrier(
-        (near, far_same, next_columns, means, finished)
+    block = message(means, next_columns[LOCAL : LOCAL + 1, :TILE], next_columns)
+    near, far_same, next_columns, block, finished = lax.optimization_barrier(
+        (near, far_same, next_columns, block, finished)
     )
     near_half = lax.dynamic_slice(near, (core * HALF, 0), (HALF, COARSE))
     far = across(near)
     near_second = along(near_half)
     far_second = along(near_half, 1)
 
-    got = exchanged(message(means, next_columns[LOCAL : LOCAL + 1, :TILE], next_columns))
+    got = exchanged(block)
 
     got, far, near_second, far_second, finished, top, bottom = lax.optimization_barrier(
         (got, far, near_second, far_second, finished, top, bottom)

time: 111 us -> 109 us (0.982)
  local copies, waits for them, and re-layouts: 3.76 us -> 1.83 us
    unnamed x10 -> x8, local copies, waits for them, and re-layouts: 1.96 us -> 0.02 us
  transfers between devices with their start and end apart: 21 -> 21, of which waited for: 5 -> 5; matrix products, arithmetic and copies ran while one was open for 2% -> 2% of each run, Pallas kernels for 16% -> 17%
where the time goes in v6:
time: 109 us
  starting transfers between devices  45.2 us (41%)
  Pallas kernels  33.3 us (31%)
  waiting for transfers between devices  28.2 us (26%)
  local copies, waits for them, and re-layouts  1.83 us (2%)
    all_to_all x2, waiting for transfers between devices, exchanged(): lax.all_to_all(block, ('tm', 'space'), 0, 0, tiled=True)  22.5 us
    all_to_all x2, starting transfers between devices, exchanged(): lax.all_to_all(block, ('tm', 'space'), 0, 0, tiled=True)  16.4 us
    ppermute x12, starting transfers between devices, moved(): return lax.ppermute(value, ('tm', 'space'), pairs)  16.2 us
    pallas_call x2, Pallas kernels, fine_call(): pl.pallas_call(functools.partial(fine_kernel, corrected), cost_estimate=c...  16.1 us
    ppermute x7, starting transfers between devices, shifted(): return lax.ppermute(value, ('tm', 'space'), pairs)  12.7 us
    pallas_call x1, Pallas kernels, last_chain(): pl.pallas_call(last_chain_kernel, cost_estimate=cost(6), out_shape=jax.Sh...  6.32 us
    pallas_call x1, Pallas kernels, first_chain(): pl.pallas_call(first_chain_kernel, cost_estimate=cost(5), out_shape=(jax....  5.9 us
    ppermute x12, waiting for transfers between devices, moved(): return lax.ppermute(value, ('tm', 'space'), pairs)  5.68 us
  transfers between devices with their start and end apart: 21, of which 5 were waited for; matrix products, arithmetic and copies ran while one was open for 2% of the time, Pallas kernels for 17%

profile of v6, /device:TPU:1, one launch (start us, length us, event | category | flops | bytes accessed | tf_op | source)
XLA Modules:
  0.0 108.9 jit_solution(3681692402273410915)
XLA Ops:
  0.0 1.4 %collective-permute-start = (f32[512,512]{1,0:T(8,128)}, f32[512,512]{1,0:T(8,128)S(1)}, u32[]{:S(2)}, u32[]{:S(2)}) collective-permute-start(f32[512,512]{1,0:T(8,128)} %bitcast.20), channel_id=1, source_target_pairs={{0,8},{1,9},{2,10},{3,11},{4,12},{5,13},{6,14},{7,15},{8,0},{9,1},... | collective-permute-start | bytes 3145736 | tf_op jit(solution)/shard_map/ppermute | solution.py:47
  1.4 1.0 slice_bitcast_fusion
  2.4 1.4 %collective-permute-start.1 = (f32[16,2048]{1,0:T(8,128)S(1)}, f32[16,2048]{1,0:T(8,128)S(1)}, u32[]{:S(2)}, u32[]{:S(2)}) collective-permute-start(f32[16,2048]{1,0:T(8,128)S(1)} %pad_maximum_fusion), channel_id=1, source_target_pairs={{0,1},{1,2},{2,3},{3,4},{4,5},{5,6},{6,7},{7,0},{8,9},{9,10},{10,1... | collective-permute-start | bytes 393224 | tf_op jit(solution)/shard_map/ppermute | solution.py:56
  3.8 4.7 %collective-permute-start.2 = (f32[16,2048]{1,0:T(8,128)S(1)}, f32[16,2048]{1,0:T(8,128)S(1)}, u32[]{:S(2)}, u32[]{:S(2)}) collective-permute-start(f32[16,2048]{1,0:T(8,128)S(1)} %pad_maximum_fusion.1), channel_id=1, source_target_pairs={{0,7},{1,0},{2,1},{3,2},{4,3},{5,4},{6,5},{7,6},{8,15},{9,8},{10,9... | collective-permute-start | bytes 393224 | tf_op jit(solution)/shard_map/ppermute | solution.py:56
  8.4 4.0 %shard_map.55 = (f32[512,512]{1,0:T(8,128)S(1)}, f32[256,512]{1,0:T(8,128)S(1)}, f32[72,512]{1,0:T(8,128)}, f32[16,15,8,128]{3,2,1,0:T(8,128)S(1)}) custom-call(s32[8,16]{1,0:T(8,128)} %class_ref.1, f32[3,8]{1,0:T(4,128)} %sets_ref.1, f32[512,512]{1,0:T(8,128)} %bitcast.21, f32[512,512]{1,0:T(8,128)S(1)} %collective-permute-done.other_ref, f32[128,2048]{1,0:T(8,128)} %bitcast.18), custom_call_target="tpu_custom_call" | custom-call | bytes 10800000 | tf_op jit(solution)/shard_map/pallas_call | solution.py:165
  12.5 2.8 %collective-permute-start.3 = (f32[512,512]{1,0:T(8,128)S(1)}, f32[512,512]{1,0:T(8,128)S(1)}, u32[]{:S(2)}, u32[]{:S(2)}) collective-permute-start(f32[512,512]{1,0:T(8,128)S(1)} %get-tuple-element.40.refs_4_), channel_id=1, source_target_pairs={{0,16},{1,17},{2,18},{3,19},{4,20},{5,21},{6,22},{7,23},{8,56},{9,... | collective-permute-start | bytes 3145736 | tf_op jit(solution)/shard_map/ppermute | solution.py:47
  15.3 3.0 %collective-permute-start.4 = (f32[256,512]{1,0:T(8,128)S(1)}, f32[256,512]{1,0:T(8,128)S(1)}, u32[]{:S(2)}, u32[]{:S(2)}) collective-permute-start(f32[256,512]{1,0:T(8,128)S(1)} %get-tuple-element.41), channel_id=1, source_target_pairs={{0,64},{1,65},{2,66},{3,67},{4,68},{5,69},{6,70},{7,71},{8,76},{9,... | collective-permute-start | bytes 1572872 | tf_op jit(solution)/shard_map/ppermute | solution.py:47
  18.4 7.9 %shard_map.56 = (f32[16,128,128]{2,1,0:T(8,128)}, f32[1,128]{1,0:T(1,128)S(1)}, f32[8,2048]{1,0:T(8,128)S(1)}, f32[8,2048]{1,0:T(8,128)S(1)}, f32[1,128]{1,0:T(1,128)}, /*index=5*/f32[16,144,128]{2,1,0:T(8,128)}) custom-call(f32[16,15,8,128]{3,2,1,0:T(8,128)S(1)} %get-tuple-element.36.coef, f32[16,2048]{1,0:T(8,128)S(1)} %collective-permute-done.1.refs_0_, ...), custom_call_target="tpu_custom_call" | custom-call | bytes 36000000 | tf_op jit(solution)/shard_map/pallas_call | solution.py:347
  26.3 1.0 shard_map.57
  27.3 1.3 %collective-permute-done.3.refs_0_ = f32[512,512]{1,0:T(8,128)S(1)} collective-permute-done((f32[512,512]{1,0:T(8,128)S(1)}, f32[512,512]{1,0:T(8,128)S(1)}, u32[]{:S(2)}, u32[]{:S(2)}) %collective-permute-start.3) | collective-permute-done | bytes 1048608 | tf_op jit(solution)/shard_map/ppermute | solution.py:47
  28.7 3.0 %collective-permute-start.6 = (f32[512,512]{1,0:T(8,128)S(1)}, f32[512,512]{1,0:T(8,128)}, u32[]{:S(2)}, u32[]{:S(2)}) collective-permute-start(f32[512,512]{1,0:T(8,128)S(1)} %collective-permute-done.3.refs_0_), channel_id=1, source_target_pairs={{0,64},{1,65},{2,66},{3,67},{4,68},{5,69},{6,70},{7,71},{8,76},{9,... | collective-permute-start | bytes 3145736 | tf_op jit(solution)/shard_map/ppermute | solution.py:47
  31.7 0.8 constant_dynamic-slice_fusion
  32.5 3.0 %collective-permute-start.8 = (f32[256,512]{1,0:T(8,128)}, f32[256,512]{1,0:T(8,128)}, u32[]{:S(2)}, u32[]{:S(2)}) collective-permute-start(f32[256,512]{1,0:T(8,128)} %constant_dynamic-slice_fusion), channel_id=1, source_target_pairs={{0,80},{1,81},{2,82},{3,83},{4,84},{5,85},{6,86},{7,87},{8,124},{9... | collective-permute-start | bytes 1572872 | tf_op jit(solution)/shard_map/ppermute | solution.py:47
  35.5 0.2 collective-permute-start.7
  35.7 8.2 %all-to-all-start = ((f32[128,1,640]{2,1,0:T(1,128)}), f32[128,1,640]{2,1,0:T(1,128)S(1)}, u32[]{:S(2)}, u32[]{:S(2)}) async-start(f32[128,1,640]{2,1,0:T(1,128)} %bitcast.24), calls=%async_computation | async-start | bytes 655360 | tf_op jit(solution)/shard_map/all_to_all | solution.py:670
  43.9 1.1 %collective-permute-start.9 = (f32[512,512]{1,0:T(8,128)S(1)}, f32[512,512]{1,0:T(8,128)}, u32[]{:S(2)}, u32[]{:S(2)}) collective-permute-start(f32[512,512]{1,0:T(8,128)S(1)} %collective-permute-done.3.refs_0_), channel_id=1, source_target_pairs={{0,8},{1,9},{2,10},{3,11},{4,12},{5,13},{6,14},{7,15},{8,0},{9,1},... | collective-permute-start | bytes 3145736 | tf_op jit(solution)/shard_map/ppermute | solution.py:47
  45.0 0.1 collective-permute-start.12
  45.1 10.3 %all-to-all-done = f32[128,1,640]{2,1,0:T(1,128)S(1)} async-done(((f32[128,1,640]{2,1,0:T(1,128)}), f32[128,1,640]{2,1,0:T(1,128)S(1)}, u32[]{:S(2)}, u32[]{:S(2)}) %all-to-all-start) | async-done | bytes 327712 | tf_op jit(solution)/shard_map/all_to_all | solution.py:670
  55.4 0.9 collective-permute-start.10
  56.4 0.3 collective-permute-start.16
  56.7 0.2 collective-permute-start.11
  56.9 0.3 collective-permute-start.13
  57.2 0.6 collective-permute-start.15
  57.8 3.2 %collective-permute-done.11.refs_6_ = f32[256,512]{1,0:T(8,128)S(1)} collective-permute-done((f32[256,512]{1,0:T(8,128)}, f32[256,512]{1,0:T(8,128)S(1)}, u32[]{:S(2)}, u32[]{:S(2)}) %collective-permute-start.11) | collective-permute-done | bytes 524320 | tf_op jit(solution)/shard_map/ppermute | solution.py:47
  61.0 3.6 %collective-permute-start.17 = (f32[8,2048]{1,0:T(8,128)}, f32[8,2048]{1,0:T(8,128)S(1)}, u32[]{:S(2)}, u32[]{:S(2)}) collective-permute-start(f32[8,2048]{1,0:T(8,128)} %copy-done.1), channel_id=1, source_target_pairs={{0,15},{1,8},{2,9},{3,10},{4,11},{5,12},{6,13},{7,14},{8,23},{9,16... | collective-permute-start | bytes 196616 | tf_op jit(solution)/shard_map/ppermute | solution.py:56
  64.6 5.9 %shard_map.58 = (f32[1,640]{1,0:T(1,128)S(1)}, f32[9,512,512]{2,1,0:T(8,128)}) custom-call(f32[640,128]{1,0:T(8,128)S(1)} %bitcast.16, f32[512,512]{1,0:T(8,128)S(1)} %collective-permute-done.other_ref, f32[512,512]{1,0:T(8,128)S(1)} %collective-permute-done.3.refs_0_, f32[512,512]{1,0:T(8,128)} %collective-permute-done.9.refs_1_, ...), custom_call_target="tpu_custom_call" | custom-call | bytes 18000000 | tf_op jit(solution)/shard_map/pallas_call | solution.py:577
  70.6 1.1 %collective-permute-done.14 = f32[1,640]{1,0:T(1,128)S(1)} collective-permute-done((f32[1,640]{1,0:T(1,128)S(1)}, f32[1,640]{1,0:T(1,128)S(1)}, u32[]{:S(2)}, u32[]{:S(2)}) %collective-permute-start.14) | collective-permute-done | bytes 2592 | tf_op jit(solution)/shard_map/ppermute | solution.py:47
  71.8 8.2 %shard_map.59 = (f32[16,128,128]{2,1,0:T(8,128)}, f32[640,128]{1,0:T(8,128)}) custom-call(f32[16,15,8,128]{3,2,1,0:T(8,128)S(1)} %get-tuple-element.36.coef, f32[1,512]{1,0:T(1,128)S(1)} %slice.48.refs_0_.own_ref, f32[1,128]{1,0:T(1,128)} %get-tuple-element.58.refs_1_, f32[1,128]{1,0:T(1,128)S(1)} %slice.49.refs_2_, f32[1,128]{1,0:T(1,128)S(1)} %slice.53.refs_3_, ...), custom_call_target="tpu_custom_call" | custom-call | bytes 36000000 | tf_op jit(solution)/shard_map/pallas_call | solution.py:347
  80.0 2.1 %collective-permute-start.18 = (f32[16,128,128]{2,1,0:T(8,128)}, f32[16,128,128]{2,1,0:T(8,128)S(1)}, u32[]{:S(2)}, u32[]{:S(2)}) collective-permute-start(f32[16,128,128]{2,1,0:T(8,128)} %get-tuple-element.66), channel_id=1, source_target_pairs={{0,8},{1,9},{2,10},{3,11},{4,12},{5,13},{6,14},{7,15},{8,16},{9,17... | collective-permute-start | bytes 3145736 | tf_op jit(solution)/shard_map/ppermute | solution.py:56
  82.1 8.1 %all-to-all-start.1 = ((f32[128,1,640]{2,1,0:T(1,128)}), f32[128,1,640]{2,1,0:T(1,128)S(1)}, u32[]{:S(2)}, u32[]{:S(2)}) async-start(f32[128,1,640]{2,1,0:T(1,128)} %bitcast.9), calls=%async_computation.1 | async-start | bytes 655360 | tf_op jit(solution)/shard_map/all_to_all | solution.py:670
  90.2 12.2 %all-to-all-done.1 = f32[128,1,640]{2,1,0:T(1,128)S(1)} async-done(((f32[128,1,640]{2,1,0:T(1,128)}), f32[128,1,640]{2,1,0:T(1,128)S(1)}, u32[]{:S(2)}, u32[]{:S(2)}) %all-to-all-start.1) | async-done | bytes 327712 | tf_op jit(solution)/shard_map/all_to_all | solution.py:670
  102.4 6.3 %shard_map.60 = f32[128,2048]{1,0:T(8,128)} custom-call(f32[640,128]{1,0:T(8,128)S(1)} %bitcast.17, f32[1,512]{1,0:T(1,128)S(1)} %slice.48.refs_0_.own_ref, f32[1,512]{1,0:T(1,128)S(1)} %slice.54.partner_ref, f32[512,512]{1,0:T(8,128)} %bitcast.22, f32[9,512,512]{2,1,0:T(8,128)} %get-tuple-element.65.maps_ref, f32[16,128,128]{2,1,0:T(8,128)S(1)} %collective-permute-done.18.u_ref), custom_call_target="tpu_custom_call" | custom-call | bytes 21600000 | tf_op jit(solution)/shard_map/pallas_call | solution.py:649
  (33 shorter events, 0.2 us)
Async XLA Ops:
  0.0 8.4 %collective-permute-start = (f32[512,512]{1,0:T(8,128)}, f32[512,512]{1,0:T(8,128)S(1)}, u32[]{:S(2)}, u32[]{:S(2)}) collective-permute-start(f32[512,512]{1,0:T(8,128)} %bitcast.20), channel_id=1, source_target_pairs={{0,8},{1,9},{2,10},{3,11},{4,12},{5,13},{6,14},{7,15},{8,0},{9,1},... | collective-permute-start | bytes 3145736 | tf_op jit(solution)/shard_map/ppermute | solution.py:47
  2.4 10.1 %collective-permute-start.1 = (f32[16,2048]{1,0:T(8,128)S(1)}, f32[16,2048]{1,0:T(8,128)S(1)}, u32[]{:S(2)}, u32[]{:S(2)}) collective-permute-start(f32[16,2048]{1,0:T(8,128)S(1)} %pad_maximum_fusion), channel_id=1, source_target_pairs={{0,1},{1,2},{2,3},{3,4},{4,5},{5,6},{6,7},{7,0},{8,9},{9,10},{10,1... | collective-permute-start | bytes 393224 | tf_op jit(solution)/shard_map/ppermute | solution.py:56
  3.8 8.7 %collective-permute-start.2 = (f32[16,2048]{1,0:T(8,128)S(1)}, f32[16,2048]{1,0:T(8,128)S(1)}, u32[]{:S(2)}, u32[]{:S(2)}) collective-permute-start(f32[16,2048]{1,0:T(8,128)S(1)} %pad_maximum_fusion.1), channel_id=1, source_target_pairs={{0,7},{1,0},{2,1},{3,2},{4,3},{5,4},{6,5},{7,6},{8,15},{9,8},{10,9... | collective-permute-start | bytes 393224 | tf_op jit(solution)/shard_map/ppermute | solution.py:56
  12.5 16.2 %copy-start = (f32[512,512]{1,0:T(8,128)}, f32[512,512]{1,0:T(8,128)S(1)}, u32[]{:S(2)}) copy-start(f32[512,512]{1,0:T(8,128)S(1)} %get-tuple-element.40.refs_4_) | copy-start | bytes 3145732
  12.5 16.1 %collective-permute-start.3 = (f32[512,512]{1,0:T(8,128)S(1)}, f32[512,512]{1,0:T(8,128)S(1)}, u32[]{:S(2)}, u32[]{:S(2)}) collective-permute-start(f32[512,512]{1,0:T(8,128)S(1)} %get-tuple-element.40.refs_4_), channel_id=1, source_target_pairs={{0,16},{1,17},{2,18},{3,19},{4,20},{5,21},{6,22},{7,23},{8,56},{9,... | collective-permute-start | bytes 3145736 | tf_op jit(solution)/shard_map/ppermute | solution.py:47
  15.3 12.0 %collective-permute-start.4 = (f32[256,512]{1,0:T(8,128)S(1)}, f32[256,512]{1,0:T(8,128)S(1)}, u32[]{:S(2)}, u32[]{:S(2)}) collective-permute-start(f32[256,512]{1,0:T(8,128)S(1)} %get-tuple-element.41), channel_id=1, source_target_pairs={{0,64},{1,65},{2,66},{3,67},{4,68},{5,69},{6,70},{7,71},{8,76},{9,... | collective-permute-start | bytes 1572872 | tf_op jit(solution)/shard_map/ppermute | solution.py:47
  18.4 8.0 %collective-permute-start.5 = (f32[72,512]{1,0:T(8,128)}, f32[72,512]{1,0:T(8,128)S(1)}, u32[]{:S(2)}, u32[]{:S(2)}) collective-permute-start(f32[72,512]{1,0:T(8,128)} %get-tuple-element.42.refs_4_), channel_id=1, source_target_pairs={{0,120},{1,121},{2,122},{3,123},{4,124},{5,125},{6,126},{7,127},{8... | collective-permute-start | bytes 442376 | tf_op jit(solution)/shard_map/ppermute | solution.py:56
  26.3 2.4 %copy-start.1 = (f32[8,2048]{1,0:T(8,128)}, f32[8,2048]{1,0:T(8,128)S(1)}, u32[]{:S(2)}) copy-start(f32[8,2048]{1,0:T(8,128)S(1)} %get-tuple-element.62) | copy-start | bytes 196612
  26.3 5.4 %copy-start.2 = (f32[8,2048]{1,0:T(8,128)}, f32[8,2048]{1,0:T(8,128)S(1)}, u32[]{:S(2)}) copy-start(f32[8,2048]{1,0:T(8,128)S(1)} %get-tuple-element.60) | copy-start | bytes 196612
  27.3 4.4 %copy-start.3 = (f32[256,512]{1,0:T(8,128)}, f32[256,512]{1,0:T(8,128)S(1)}, u32[]{:S(2)}) copy-start(f32[256,512]{1,0:T(8,128)S(1)} %collective-permute-done.4.refs_7_) | copy-start | bytes 1572868
  28.7 26.8 %collective-permute-start.6 = (f32[512,512]{1,0:T(8,128)S(1)}, f32[512,512]{1,0:T(8,128)}, u32[]{:S(2)}, u32[]{:S(2)}) collective-permute-start(f32[512,512]{1,0:T(8,128)S(1)} %collective-permute-done.3.refs_0_), channel_id=1, source_target_pairs={{0,64},{1,65},{2,66},{3,67},{4,68},{5,69},{6,70},{7,71},{8,76},{9,... | collective-permute-start | bytes 3145736 | tf_op jit(solution)/shard_map/ppermute | solution.py:47
  32.5 22.9 %collective-permute-start.8 = (f32[256,512]{1,0:T(8,128)}, f32[256,512]{1,0:T(8,128)}, u32[]{:S(2)}, u32[]{:S(2)}) collective-permute-start(f32[256,512]{1,0:T(8,128)} %constant_dynamic-slice_fusion), channel_id=1, source_target_pairs={{0,80},{1,81},{2,82},{3,83},{4,84},{5,85},{6,86},{7,87},{8,124},{9... | collective-permute-start | bytes 1572872 | tf_op jit(solution)/shard_map/ppermute | solution.py:47
  35.5 19.9 %collective-permute-start.7 = (f32[256,512]{1,0:T(8,128)}, f32[256,512]{1,0:T(8,128)}, u32[]{:S(2)}, u32[]{:S(2)}) collective-permute-start(f32[256,512]{1,0:T(8,128)} %constant_dynamic-slice_fusion), channel_id=1, source_target_pairs={{0,16},{1,17},{2,18},{3,19},{4,20},{5,21},{6,22},{7,23},{8,56},{9,... | collective-permute-start | bytes 1572872 | tf_op jit(solution)/shard_map/ppermute | solution.py:47
  35.7 19.8 %all-to-all-start = ((f32[128,1,640]{2,1,0:T(1,128)}), f32[128,1,640]{2,1,0:T(1,128)S(1)}, u32[]{:S(2)}, u32[]{:S(2)}) async-start(f32[128,1,640]{2,1,0:T(1,128)} %bitcast.24), calls=%async_computation | async-start | bytes 655360 | tf_op jit(solution)/shard_map/all_to_all | solution.py:670
  43.9 13.3 %collective-permute-start.9 = (f32[512,512]{1,0:T(8,128)S(1)}, f32[512,512]{1,0:T(8,128)}, u32[]{:S(2)}, u32[]{:S(2)}) collective-permute-start(f32[512,512]{1,0:T(8,128)S(1)} %collective-permute-done.3.refs_0_), channel_id=1, source_target_pairs={{0,8},{1,9},{2,10},{3,11},{4,12},{5,13},{6,14},{7,15},{8,0},{9,1},... | collective-permute-start | bytes 3145736 | tf_op jit(solution)/shard_map/ppermute | solution.py:47
  45.0 11.8 %collective-permute-start.12 = (f32[256,512]{1,0:T(8,128)}, f32[256,512]{1,0:T(8,128)}, u32[]{:S(2)}, u32[]{:S(2)}) collective-permute-start(f32[256,512]{1,0:T(8,128)} %copy-done.3), channel_id=1, source_target_pairs={{0,8},{1,9},{2,10},{3,11},{4,12},{5,13},{6,14},{7,15},{8,0},{9,1},... | collective-permute-start | bytes 1572872 | tf_op jit(solution)/shard_map/ppermute | solution.py:47
  55.4 9.2 %collective-permute-start.10 = (f32[512,512]{1,0:T(8,128)}, f32[512,512]{1,0:T(8,128)S(1)}, u32[]{:S(2)}, u32[]{:S(2)}) collective-permute-start(f32[512,512]{1,0:T(8,128)} %collective-permute-done.6.refs_2_), channel_id=1, source_target_pairs={{0,8},{1,9},{2,10},{3,11},{4,12},{5,13},{6,14},{7,15},{8,0},{9,1},... | collective-permute-start | bytes 3145736 | tf_op jit(solution)/shard_map/ppermute | solution.py:47
  56.4 15.4 %collective-permute-start.16 = (f32[16,128,128]{2,1,0:T(8,128)}, f32[16,128,128]{2,1,0:T(8,128)S(1)}, u32[]{:S(2)}, u32[]{:S(2)}) collective-permute-start(f32[16,128,128]{2,1,0:T(8,128)} %get-tuple-element.61), channel_id=1, source_target_pairs={{0,8},{1,9},{2,10},{3,11},{4,12},{5,13},{6,14},{7,15},{8,16},{9,17... | collective-permute-start | bytes 3145736 | tf_op jit(solution)/shard_map/ppermute | solution.py:56
  56.7 4.3 %collective-permute-start.11 = (f32[256,512]{1,0:T(8,128)}, f32[256,512]{1,0:T(8,128)S(1)}, u32[]{:S(2)}, u32[]{:S(2)}) collective-permute-start(f32[256,512]{1,0:T(8,128)} %collective-permute-done.7.refs_5_), channel_id=1, source_target_pairs={{0,8},{1,9},{2,10},{3,11},{4,12},{5,13},{6,14},{7,15},{8,0},{9,1},... | collective-permute-start | bytes 1572872 | tf_op jit(solution)/shard_map/ppermute | solution.py:47
  56.9 7.7 %collective-permute-start.13 = (f32[256,512]{1,0:T(8,128)}, f32[256,512]{1,0:T(8,128)S(1)}, u32[]{:S(2)}, u32[]{:S(2)}) collective-permute-start(f32[256,512]{1,0:T(8,128)} %collective-permute-done.8.refs_9_), channel_id=1, source_target_pairs={{0,8},{1,9},{2,10},{3,11},{4,12},{5,13},{6,14},{7,15},{8,0},{9,1},... | collective-permute-start | bytes 1572872 | tf_op jit(solution)/shard_map/ppermute | solution.py:47
  57.2 14.6 %collective-permute-start.15 = (f32[8,2048]{1,0:T(8,128)}, f32[8,2048]{1,0:T(8,128)S(1)}, u32[]{:S(2)}, u32[]{:S(2)}) collective-permute-start(f32[8,2048]{1,0:T(8,128)} %copy-done.2), channel_id=1, source_target_pairs={{0,9},{1,10},{2,11},{3,12},{4,13},{5,14},{6,15},{7,8},{8,17},{9,18... | collective-permute-start | bytes 196616 | tf_op jit(solution)/shard_map/ppermute | solution.py:56
  61.0 10.8 %collective-permute-start.17 = (f32[8,2048]{1,0:T(8,128)}, f32[8,2048]{1,0:T(8,128)S(1)}, u32[]{:S(2)}, u32[]{:S(2)}) collective-permute-start(f32[8,2048]{1,0:T(8,128)} %copy-done.1), channel_id=1, source_target_pairs={{0,15},{1,8},{2,9},{3,10},{4,11},{5,12},{6,13},{7,14},{8,23},{9,16... | collective-permute-start | bytes 196616 | tf_op jit(solution)/shard_map/ppermute | solution.py:56
  70.5 1.2 %collective-permute-start.14 = (f32[1,640]{1,0:T(1,128)S(1)}, f32[1,640]{1,0:T(1,128)S(1)}, u32[]{:S(2)}, u32[]{:S(2)}) collective-permute-start(f32[1,640]{1,0:T(1,128)S(1)} %get-tuple-element.57), channel_id=1, source_target_pairs={{0,8},{1,9},{2,10},{3,11},{4,12},{5,13},{6,14},{7,15},{8,0},{9,1},... | collective-permute-start | bytes 7688 | tf_op jit(solution)/shard_map/ppermute | solution.py:47
  80.0 22.5 %collective-permute-start.18 = (f32[16,128,128]{2,1,0:T(8,128)}, f32[16,128,128]{2,1,0:T(8,128)S(1)}, u32[]{:S(2)}, u32[]{:S(2)}) collective-permute-start(f32[16,128,128]{2,1,0:T(8,128)} %get-tuple-element.66), channel_id=1, source_target_pairs={{0,8},{1,9},{2,10},{3,11},{4,12},{5,13},{6,14},{7,15},{8,16},{9,17... | collective-permute-start | bytes 3145736 | tf_op jit(solution)/shard_map/ppermute | solution.py:56
  82.1 20.3 %all-to-all-start.1 = ((f32[128,1,640]{2,1,0:T(1,128)}), f32[128,1,640]{2,1,0:T(1,128)S(1)}, u32[]{:S(2)}, u32[]{:S(2)}) async-start(f32[128,1,640]{2,1,0:T(1,128)} %bitcast.9), calls=%async_computation.1 | async-start | bytes 655360 | tf_op jit(solution)/shard_map/all_to_all | solution.py:670

commit v7 on v6

--- a/solution.py
+++ b/solution.py
@@ -592,30 +592,26 @@
     )(got, other, *whole, *halved)
 
 
-def last_chain_kernel(got_ref, own_ref, partner_ref, late_ref, maps_ref, u_ref, out_ref, late, maps, sems, u, whole, sem, out_sems):
+def last_chain_kernel(got_ref, partner_ref, maps_ref, u_ref, out_ref, maps, sems, u, whole, sem, out_sems):
     strip, core, chip, _ = position()
 
     def fetched(slot):
         return pltpu.make_async_copy(maps_ref.at[slot], maps.at[slot], sems.at[slot])
 
-    first = pltpu.make_async_copy(late_ref, late, sems.at[9])
-    first.start()
-    for slot in (1, 2, 3, 4, 5, 6, 7, 0, 8):
+    for slot in (0, 1, 2, 3, 4, 5, 6, 7, 8):
         fetched(slot).start()
     state = pltpu.make_async_copy(u_ref, u, sem)
     state.start()
-    own, partner = quarters(own_ref[...]), quarters(partner_ref[...])
-    even_start = pair_pushes(got_ref, chip)
-    odd_start = minus(gathered(got_ref, 2 * chip), own)
-    first.wait()
-    value = select(core == 1, applied(late[...], odd_start), even_start)
+    partner = quarters(partner_ref[...])
+    even_start, odd_pushes = pair_pushes(got_ref, chip), pushes(got_ref, 2 * chip)
+    fetched(0).wait()
+    value = select(core == 1, add(odd_pushes, applied(maps[0], partner)), even_start)
 
     def arriving(step, value):
         fetched(step).wait()
         return add(applied(maps[step], value), pair_pushes(got_ref, chip + step))
 
     value = lax.fori_loop(1, 8, arriving, value)
-    fetched(0).wait()
 
     def again(step, value):
         return add(applied(maps[step], value), pair_pushes(got_ref, chip + step))
@@ -644,25 +640,23 @@
         copy.wait()
 
 
-def last_chain(got, own, partner, late, maps, previous):
-    square = (COARSE, COARSE)
+def last_chain(got, partner, maps, previous):
     return pl.pallas_call(
         last_chain_kernel,
         cost_estimate=cost(6),
         out_shape=jax.ShapeDtypeStruct((ROWS, COLS), jnp.float32),
-        in_specs=[VMEM, VMEM, VMEM, HBM, HBM, ANY],
+        in_specs=[VMEM, VMEM, HBM, ANY],
         out_specs=HBM,
         scratch_shapes=[
-            pltpu.VMEM(square, jnp.float32),
-            pltpu.VMEM((9, *square), jnp.float32),
-            pltpu.SemaphoreType.DMA((10,)),
+            pltpu.VMEM((9, COARSE, COARSE), jnp.float32),
+            pltpu.SemaphoreType.DMA((9,)),
             pltpu.VMEM((TILES, ROWS, TILE), jnp.float32),
             pltpu.VMEM((ROWS, COLS), jnp.float32),
             pltpu.SemaphoreType.DMA,
             pltpu.SemaphoreType.DMA((4,)),
         ],
         compiler_params=pltpu.CompilerParams(vmem_limit_bytes=16 << 20),
-    )(got, own, partner, *in_hbm(late, maps), previous)
+    )(got, partner, *in_hbm(maps), previous)
 
 
 def exchanged(block):
@@ -725,7 +719,7 @@
     )
     previous = shifted(finished, 1)
     got = exchanged(block)
-    return last_chain(got, here, there, own_map, maps, previous)[None]
+    return last_chain(got, there, maps, previous)[None]
 
 
 def solution(mesh):

time: 109 us -> 109 us (level)
  no operation moved by 1% of the time
where the time goes in v7:
time: 109 us
  starting transfers between devices  45.2 us (41%)
  Pallas kernels  33.2 us (30%)
  waiting for transfers between devices  28.2 us (26%)
  local copies, waits for them, and re-layouts  1.83 us (2%)
    all_to_all x2, waiting for transfers between devices, exchanged(): lax.all_to_all(block, ('tm', 'space'), 0, 0, tiled=True)  22.5 us
    all_to_all x2, starting transfers between devices, exchanged(): lax.all_to_all(block, ('tm', 'space'), 0, 0, tiled=True)  16.4 us
    ppermute x12, starting transfers between devices, moved(): return lax.ppermute(value, ('tm', 'space'), pairs)  16.2 us
    pallas_call x2, Pallas kernels, fine_call(): pl.pallas_call(functools.partial(fine_kernel, corrected), cost_estimate=c...  16.1 us
    ppermute x7, starting transfers between devices, shifted(): return lax.ppermute(value, ('tm', 'space'), pairs)  12.7 us
    pallas_call x1, Pallas kernels, last_chain(): pl.pallas_call(last_chain_kernel, cost_estimate=cost(6), out_shape=jax.Sh...  6.17 us
    pallas_call x1, Pallas kernels, first_chain(): pl.pallas_call(first_chain_kernel, cost_estimate=cost(5), out_shape=(jax....  5.9 us
    ppermute x12, waiting for transfers between devices, moved(): return lax.ppermute(value, ('tm', 'space'), pairs)  5.68 us
  transfers between devices with their start and end apart: 21, of which 5 were waited for; matrix products, arithmetic and copies ran while one was open for 2% of the time, Pallas kernels for 17%

profile of v7, /device:TPU:1, one launch (start us, length us, event | category | flops | bytes accessed | tf_op | source)
XLA Modules:
  0.0 108.7 jit_solution(9919994083047861539)
XLA Ops:
  0.0 1.4 %collective-permute-start = (f32[512,512]{1,0:T(8,128)}, f32[512,512]{1,0:T(8,128)S(1)}, u32[]{:S(2)}, u32[]{:S(2)}) collective-permute-start(f32[512,512]{1,0:T(8,128)} %bitcast.22), channel_id=1, source_target_pairs={{0,8},{1,9},{2,10},{3,11},{4,12},{5,13},{6,14},{7,15},{8,0},{9,1},... | collective-permute-start | bytes 3145736 | tf_op jit(solution)/shard_map/ppermute | solution.py:47
  1.4 1.0 slice_bitcast_fusion
  2.4 1.4 %collective-permute-start.1 = (f32[16,2048]{1,0:T(8,128)S(1)}, f32[16,2048]{1,0:T(8,128)S(1)}, u32[]{:S(2)}, u32[]{:S(2)}) collective-permute-start(f32[16,2048]{1,0:T(8,128)S(1)} %pad_maximum_fusion), channel_id=1, source_target_pairs={{0,1},{1,2},{2,3},{3,4},{4,5},{5,6},{6,7},{7,0},{8,9},{9,10},{10,1... | collective-permute-start | bytes 393224 | tf_op jit(solution)/shard_map/ppermute | solution.py:56
  3.8 4.7 %collective-permute-start.2 = (f32[16,2048]{1,0:T(8,128)S(1)}, f32[16,2048]{1,0:T(8,128)S(1)}, u32[]{:S(2)}, u32[]{:S(2)}) collective-permute-start(f32[16,2048]{1,0:T(8,128)S(1)} %pad_maximum_fusion.1), channel_id=1, source_target_pairs={{0,7},{1,0},{2,1},{3,2},{4,3},{5,4},{6,5},{7,6},{8,15},{9,8},{10,9... | collective-permute-start | bytes 393224 | tf_op jit(solution)/shard_map/ppermute | solution.py:56
  8.4 4.0 %shard_map.55 = (f32[512,512]{1,0:T(8,128)S(1)}, f32[256,512]{1,0:T(8,128)S(1)}, f32[72,512]{1,0:T(8,128)}, f32[16,15,8,128]{3,2,1,0:T(8,128)S(1)}) custom-call(s32[8,16]{1,0:T(8,128)} %class_ref.1, f32[3,8]{1,0:T(4,128)} %sets_ref.1, f32[512,512]{1,0:T(8,128)} %bitcast.23, f32[512,512]{1,0:T(8,128)S(1)} %collective-permute-done.other_ref, f32[128,2048]{1,0:T(8,128)} %bitcast.18), custom_call_target="tpu_custom_call" | custom-call | bytes 10800000 | tf_op jit(solution)/shard_map/pallas_call | solution.py:165
  12.5 2.8 %collective-permute-start.3 = (f32[512,512]{1,0:T(8,128)S(1)}, f32[512,512]{1,0:T(8,128)S(1)}, u32[]{:S(2)}, u32[]{:S(2)}) collective-permute-start(f32[512,512]{1,0:T(8,128)S(1)} %get-tuple-element.40.refs_4_), channel_id=1, source_target_pairs={{0,16},{1,17},{2,18},{3,19},{4,20},{5,21},{6,22},{7,23},{8,56},{9,... | collective-permute-start | bytes 3145736 | tf_op jit(solution)/shard_map/ppermute | solution.py:47
  15.3 3.0 %collective-permute-start.4 = (f32[256,512]{1,0:T(8,128)S(1)}, f32[256,512]{1,0:T(8,128)S(1)}, u32[]{:S(2)}, u32[]{:S(2)}) collective-permute-start(f32[256,512]{1,0:T(8,128)S(1)} %get-tuple-element.41), channel_id=1, source_target_pairs={{0,64},{1,65},{2,66},{3,67},{4,68},{5,69},{6,70},{7,71},{8,76},{9,... | collective-permute-start | bytes 1572872 | tf_op jit(solution)/shard_map/ppermute | solution.py:47
  18.4 7.9 %shard_map.56 = (f32[16,128,128]{2,1,0:T(8,128)}, f32[1,128]{1,0:T(1,128)S(1)}, f32[8,2048]{1,0:T(8,128)S(1)}, f32[8,2048]{1,0:T(8,128)S(1)}, f32[1,128]{1,0:T(1,128)}, /*index=5*/f32[16,144,128]{2,1,0:T(8,128)}) custom-call(f32[16,15,8,128]{3,2,1,0:T(8,128)S(1)} %get-tuple-element.36.coef, f32[16,2048]{1,0:T(8,128)S(1)} %collective-permute-done.1.refs_0_, ...), custom_call_target="tpu_custom_call" | custom-call | bytes 36000000 | tf_op jit(solution)/shard_map/pallas_call | solution.py:347
  26.3 1.0 shard_map.57
  27.3 1.3 %collective-permute-done.3.refs_0_ = f32[512,512]{1,0:T(8,128)S(1)} collective-permute-done((f32[512,512]{1,0:T(8,128)S(1)}, f32[512,512]{1,0:T(8,128)S(1)}, u32[]{:S(2)}, u32[]{:S(2)}) %collective-permute-start.3) | collective-permute-done | bytes 1048608 | tf_op jit(solution)/shard_map/ppermute | solution.py:47
  28.7 3.0 %collective-permute-start.6 = (f32[512,512]{1,0:T(8,128)S(1)}, f32[512,512]{1,0:T(8,128)}, u32[]{:S(2)}, u32[]{:S(2)}) collective-permute-start(f32[512,512]{1,0:T(8,128)S(1)} %collective-permute-done.3.refs_0_), channel_id=1, source_target_pairs={{0,64},{1,65},{2,66},{3,67},{4,68},{5,69},{6,70},{7,71},{8,76},{9,... | collective-permute-start | bytes 3145736 | tf_op jit(solution)/shard_map/ppermute | solution.py:47
  31.7 0.8 constant_dynamic-slice_fusion
  32.5 3.0 %collective-permute-start.8 = (f32[256,512]{1,0:T(8,128)}, f32[256,512]{1,0:T(8,128)}, u32[]{:S(2)}, u32[]{:S(2)}) collective-permute-start(f32[256,512]{1,0:T(8,128)} %constant_dynamic-slice_fusion), channel_id=1, source_target_pairs={{0,80},{1,81},{2,82},{3,83},{4,84},{5,85},{6,86},{7,87},{8,124},{9... | collective-permute-start | bytes 1572872 | tf_op jit(solution)/shard_map/ppermute | solution.py:47
  35.5 0.2 collective-permute-start.7
  35.7 8.2 %all-to-all-start = ((f32[128,1,640]{2,1,0:T(1,128)}), f32[128,1,640]{2,1,0:T(1,128)S(1)}, u32[]{:S(2)}, u32[]{:S(2)}) async-start(f32[128,1,640]{2,1,0:T(1,128)} %bitcast.21), calls=%async_computation | async-start | bytes 655360 | tf_op jit(solution)/shard_map/all_to_all | solution.py:664
  43.9 1.1 %collective-permute-start.9 = (f32[512,512]{1,0:T(8,128)S(1)}, f32[512,512]{1,0:T(8,128)}, u32[]{:S(2)}, u32[]{:S(2)}) collective-permute-start(f32[512,512]{1,0:T(8,128)S(1)} %collective-permute-done.3.refs_0_), channel_id=1, source_target_pairs={{0,8},{1,9},{2,10},{3,11},{4,12},{5,13},{6,14},{7,15},{8,0},{9,1},... | collective-permute-start | bytes 3145736 | tf_op jit(solution)/shard_map/ppermute | solution.py:47
  45.0 0.1 collective-permute-start.12
  45.1 10.3 %all-to-all-done = f32[128,1,640]{2,1,0:T(1,128)S(1)} async-done(((f32[128,1,640]{2,1,0:T(1,128)}), f32[128,1,640]{2,1,0:T(1,128)S(1)}, u32[]{:S(2)}, u32[]{:S(2)}) %all-to-all-start) | async-done | bytes 327712 | tf_op jit(solution)/shard_map/all_to_all | solution.py:664
  55.4 0.9 collective-permute-start.10
  56.4 0.3 collective-permute-start.16
  56.7 0.2 collective-permute-start.11
  56.9 0.3 collective-permute-start.13
  57.2 0.6 collective-permute-start.15
  57.8 3.2 %collective-permute-done.11.refs_6_ = f32[256,512]{1,0:T(8,128)S(1)} collective-permute-done((f32[256,512]{1,0:T(8,128)}, f32[256,512]{1,0:T(8,128)S(1)}, u32[]{:S(2)}, u32[]{:S(2)}) %collective-permute-start.11) | collective-permute-done | bytes 524320 | tf_op jit(solution)/shard_map/ppermute | solution.py:47
  61.0 3.6 %collective-permute-start.17 = (f32[8,2048]{1,0:T(8,128)}, f32[8,2048]{1,0:T(8,128)S(1)}, u32[]{:S(2)}, u32[]{:S(2)}) collective-permute-start(f32[8,2048]{1,0:T(8,128)} %copy-done.1), channel_id=1, source_target_pairs={{0,15},{1,8},{2,9},{3,10},{4,11},{5,12},{6,13},{7,14},{8,23},{9,16... | collective-permute-start | bytes 196616 | tf_op jit(solution)/shard_map/ppermute | solution.py:56
  64.6 5.9 %shard_map.58 = (f32[1,640]{1,0:T(1,128)S(1)}, f32[9,512,512]{2,1,0:T(8,128)}) custom-call(f32[640,128]{1,0:T(8,128)S(1)} %bitcast.16, f32[512,512]{1,0:T(8,128)S(1)} %collective-permute-done.other_ref, f32[512,512]{1,0:T(8,128)S(1)} %collective-permute-done.3.refs_0_, f32[512,512]{1,0:T(8,128)} %collective-permute-done.9.refs_1_, ...), custom_call_target="tpu_custom_call" | custom-call | bytes 18000000 | tf_op jit(solution)/shard_map/pallas_call | solution.py:577
  70.6 1.1 %collective-permute-done.14 = f32[1,640]{1,0:T(1,128)S(1)} collective-permute-done((f32[1,640]{1,0:T(1,128)S(1)}, f32[1,640]{1,0:T(1,128)S(1)}, u32[]{:S(2)}, u32[]{:S(2)}) %collective-permute-start.14) | collective-permute-done | bytes 2592 | tf_op jit(solution)/shard_map/ppermute | solution.py:47
  71.8 8.2 %shard_map.59 = (f32[16,128,128]{2,1,0:T(8,128)}, f32[640,128]{1,0:T(8,128)}) custom-call(f32[16,15,8,128]{3,2,1,0:T(8,128)S(1)} %get-tuple-element.36.coef, f32[1,512]{1,0:T(1,128)S(1)} %slice.48.refs_0_, f32[1,128]{1,0:T(1,128)} %get-tuple-element.58.refs_1_, f32[1,128]{1,0:T(1,128)S(1)} %slice.49.refs_2_, f32[1,128]{1,0:T(1,128)S(1)} %slice.53.refs_3_, ...), custom_call_target="tpu_custom_call" | custom-call | bytes 36000000 | tf_op jit(solution)/shard_map/pallas_call | solution.py:347
  80.0 2.1 %collective-permute-start.18 = (f32[16,128,128]{2,1,0:T(8,128)}, f32[16,128,128]{2,1,0:T(8,128)S(1)}, u32[]{:S(2)}, u32[]{:S(2)}) collective-permute-start(f32[16,128,128]{2,1,0:T(8,128)} %get-tuple-element.66), channel_id=1, source_target_pairs={{0,8},{1,9},{2,10},{3,11},{4,12},{5,13},{6,14},{7,15},{8,16},{9,17... | collective-permute-start | bytes 3145736 | tf_op jit(solution)/shard_map/ppermute | solution.py:56
  82.1 8.1 %all-to-all-start.1 = ((f32[128,1,640]{2,1,0:T(1,128)}), f32[128,1,640]{2,1,0:T(1,128)S(1)}, u32[]{:S(2)}, u32[]{:S(2)}) async-start(f32[128,1,640]{2,1,0:T(1,128)} %bitcast.9), calls=%async_computation.1 | async-start | bytes 655360 | tf_op jit(solution)/shard_map/all_to_all | solution.py:664
  90.2 12.2 %all-to-all-done.1 = f32[128,1,640]{2,1,0:T(1,128)S(1)} async-done(((f32[128,1,640]{2,1,0:T(1,128)}), f32[128,1,640]{2,1,0:T(1,128)S(1)}, u32[]{:S(2)}, u32[]{:S(2)}) %all-to-all-start.1) | async-done | bytes 327712 | tf_op jit(solution)/shard_map/all_to_all | solution.py:664
  102.4 6.2 %shard_map.60 = f32[128,2048]{1,0:T(8,128)} custom-call(f32[640,128]{1,0:T(8,128)S(1)} %bitcast.17, f32[1,512]{1,0:T(1,128)S(1)} %slice.54.partner_ref, f32[9,512,512]{2,1,0:T(8,128)} %get-tuple-element.65.maps_ref, f32[16,128,128]{2,1,0:T(8,128)S(1)} %collective-permute-done.18.u_ref), custom_call_target="tpu_custom_call" | custom-call | bytes 21600000 | tf_op jit(solution)/shard_map/pallas_call | solution.py:644
  (33 shorter events, 0.2 us)
Async XLA Ops:
  0.0 8.4 %collective-permute-start = (f32[512,512]{1,0:T(8,128)}, f32[512,512]{1,0:T(8,128)S(1)}, u32[]{:S(2)}, u32[]{:S(2)}) collective-permute-start(f32[512,512]{1,0:T(8,128)} %bitcast.22), channel_id=1, source_target_pairs={{0,8},{1,9},{2,10},{3,11},{4,12},{5,13},{6,14},{7,15},{8,0},{9,1},... | collective-permute-start | bytes 3145736 | tf_op jit(solution)/shard_map/ppermute | solution.py:47
  2.4 10.1 %collective-permute-start.1 = (f32[16,2048]{1,0:T(8,128)S(1)}, f32[16,2048]{1,0:T(8,128)S(1)}, u32[]{:S(2)}, u32[]{:S(2)}) collective-permute-start(f32[16,2048]{1,0:T(8,128)S(1)} %pad_maximum_fusion), channel_id=1, source_target_pairs={{0,1},{1,2},{2,3},{3,4},{4,5},{5,6},{6,7},{7,0},{8,9},{9,10},{10,1... | collective-permute-start | bytes 393224 | tf_op jit(solution)/shard_map/ppermute | solution.py:56
  3.8 8.7 %collective-permute-start.2 = (f32[16,2048]{1,0:T(8,128)S(1)}, f32[16,2048]{1,0:T(8,128)S(1)}, u32[]{:S(2)}, u32[]{:S(2)}) collective-permute-start(f32[16,2048]{1,0:T(8,128)S(1)} %pad_maximum_fusion.1), channel_id=1, source_target_pairs={{0,7},{1,0},{2,1},{3,2},{4,3},{5,4},{6,5},{7,6},{8,15},{9,8},{10,9... | collective-permute-start | bytes 393224 | tf_op jit(solution)/shard_map/ppermute | solution.py:56
  12.5 16.2 %copy-start = (f32[512,512]{1,0:T(8,128)}, f32[512,512]{1,0:T(8,128)S(1)}, u32[]{:S(2)}) copy-start(f32[512,512]{1,0:T(8,128)S(1)} %get-tuple-element.40.refs_4_) | copy-start | bytes 3145732
  12.5 16.1 %collective-permute-start.3 = (f32[512,512]{1,0:T(8,128)S(1)}, f32[512,512]{1,0:T(8,128)S(1)}, u32[]{:S(2)}, u32[]{:S(2)}) collective-permute-start(f32[512,512]{1,0:T(8,128)S(1)} %get-tuple-element.40.refs_4_), channel_id=1, source_target_pairs={{0,16},{1,17},{2,18},{3,19},{4,20},{5,21},{6,22},{7,23},{8,56},{9,... | collective-permute-start | bytes 3145736 | tf_op jit(solution)/shard_map/ppermute | solution.py:47
  15.3 12.0 %collective-permute-start.4 = (f32[256,512]{1,0:T(8,128)S(1)}, f32[256,512]{1,0:T(8,128)S(1)}, u32[]{:S(2)}, u32[]{:S(2)}) collective-permute-start(f32[256,512]{1,0:T(8,128)S(1)} %get-tuple-element.41), channel_id=1, source_target_pairs={{0,64},{1,65},{2,66},{3,67},{4,68},{5,69},{6,70},{7,71},{8,76},{9,... | collective-permute-start | bytes 1572872 | tf_op jit(solution)/shard_map/ppermute | solution.py:47
  18.4 8.0 %collective-permute-start.5 = (f32[72,512]{1,0:T(8,128)}, f32[72,512]{1,0:T(8,128)S(1)}, u32[]{:S(2)}, u32[]{:S(2)}) collective-permute-start(f32[72,512]{1,0:T(8,128)} %get-tuple-element.42.refs_4_), channel_id=1, source_target_pairs={{0,120},{1,121},{2,122},{3,123},{4,124},{5,125},{6,126},{7,127},{8... | collective-permute-start | bytes 442376 | tf_op jit(solution)/shard_map/ppermute | solution.py:56
  26.3 2.4 %copy-start.1 = (f32[8,2048]{1,0:T(8,128)}, f32[8,2048]{1,0:T(8,128)S(1)}, u32[]{:S(2)}) copy-start(f32[8,2048]{1,0:T(8,128)S(1)} %get-tuple-element.62) | copy-start | bytes 196612
  26.3 5.4 %copy-start.2 = (f32[8,2048]{1,0:T(8,128)}, f32[8,2048]{1,0:T(8,128)S(1)}, u32[]{:S(2)}) copy-start(f32[8,2048]{1,0:T(8,128)S(1)} %get-tuple-element.60) | copy-start | bytes 196612
  27.3 4.4 %copy-start.3 = (f32[256,512]{1,0:T(8,128)}, f32[256,512]{1,0:T(8,128)S(1)}, u32[]{:S(2)}) copy-start(f32[256,512]{1,0:T(8,128)S(1)} %collective-permute-done.4.refs_7_) | copy-start | bytes 1572868
  28.7 26.8 %collective-permute-start.6 = (f32[512,512]{1,0:T(8,128)S(1)}, f32[512,512]{1,0:T(8,128)}, u32[]{:S(2)}, u32[]{:S(2)}) collective-permute-start(f32[512,512]{1,0:T(8,128)S(1)} %collective-permute-done.3.refs_0_), channel_id=1, source_target_pairs={{0,64},{1,65},{2,66},{3,67},{4,68},{5,69},{6,70},{7,71},{8,76},{9,... | collective-permute-start | bytes 3145736 | tf_op jit(solution)/shard_map/ppermute | solution.py:47
  32.5 22.9 %collective-permute-start.8 = (f32[256,512]{1,0:T(8,128)}, f32[256,512]{1,0:T(8,128)}, u32[]{:S(2)}, u32[]{:S(2)}) collective-permute-start(f32[256,512]{1,0:T(8,128)} %constant_dynamic-slice_fusion), channel_id=1, source_target_pairs={{0,80},{1,81},{2,82},{3,83},{4,84},{5,85},{6,86},{7,87},{8,124},{9... | collective-permute-start | bytes 1572872 | tf_op jit(solution)/shard_map/ppermute | solution.py:47
  35.5 19.9 %collective-permute-start.7 = (f32[256,512]{1,0:T(8,128)}, f32[256,512]{1,0:T(8,128)}, u32[]{:S(2)}, u32[]{:S(2)}) collective-permute-start(f32[256,512]{1,0:T(8,128)} %constant_dynamic-slice_fusion), channel_id=1, source_target_pairs={{0,16},{1,17},{2,18},{3,19},{4,20},{5,21},{6,22},{7,23},{8,56},{9,... | collective-permute-start | bytes 1572872 | tf_op jit(solution)/shard_map/ppermute | solution.py:47
  35.7 19.8 %all-to-all-start = ((f32[128,1,640]{2,1,0:T(1,128)}), f32[128,1,640]{2,1,0:T(1,128)S(1)}, u32[]{:S(2)}, u32[]{:S(2)}) async-start(f32[128,1,640]{2,1,0:T(1,128)} %bitcast.21), calls=%async_computation | async-start | bytes 655360 | tf_op jit(solution)/shard_map/all_to_all | solution.py:664
  43.9 13.3 %collective-permute-start.9 = (f32[512,512]{1,0:T(8,128)S(1)}, f32[512,512]{1,0:T(8,128)}, u32[]{:S(2)}, u32[]{:S(2)}) collective-permute-start(f32[512,512]{1,0:T(8,128)S(1)} %collective-permute-done.3.refs_0_), channel_id=1, source_target_pairs={{0,8},{1,9},{2,10},{3,11},{4,12},{5,13},{6,14},{7,15},{8,0},{9,1},... | collective-permute-start | bytes 3145736 | tf_op jit(solution)/shard_map/ppermute | solution.py:47
  45.0 11.8 %collective-permute-start.12 = (f32[256,512]{1,0:T(8,128)}, f32[256,512]{1,0:T(8,128)}, u32[]{:S(2)}, u32[]{:S(2)}) collective-permute-start(f32[256,512]{1,0:T(8,128)} %copy-done.3), channel_id=1, source_target_pairs={{0,8},{1,9},{2,10},{3,11},{4,12},{5,13},{6,14},{7,15},{8,0},{9,1},... | collective-permute-start | bytes 1572872 | tf_op jit(solution)/shard_map/ppermute | solution.py:47
  55.4 9.2 %collective-permute-start.10 = (f32[512,512]{1,0:T(8,128)}, f32[512,512]{1,0:T(8,128)S(1)}, u32[]{:S(2)}, u32[]{:S(2)}) collective-permute-start(f32[512,512]{1,0:T(8,128)} %collective-permute-done.6.refs_2_), channel_id=1, source_target_pairs={{0,8},{1,9},{2,10},{3,11},{4,12},{5,13},{6,14},{7,15},{8,0},{9,1},... | collective-permute-start | bytes 3145736 | tf_op jit(solution)/shard_map/ppermute | solution.py:47
  56.4 15.4 %collective-permute-start.16 = (f32[16,128,128]{2,1,0:T(8,128)}, f32[16,128,128]{2,1,0:T(8,128)S(1)}, u32[]{:S(2)}, u32[]{:S(2)}) collective-permute-start(f32[16,128,128]{2,1,0:T(8,128)} %get-tuple-element.61), channel_id=1, source_target_pairs={{0,8},{1,9},{2,10},{3,11},{4,12},{5,13},{6,14},{7,15},{8,16},{9,17... | collective-permute-start | bytes 3145736 | tf_op jit(solution)/shard_map/ppermute | solution.py:56
  56.7 4.3 %collective-permute-start.11 = (f32[256,512]{1,0:T(8,128)}, f32[256,512]{1,0:T(8,128)S(1)}, u32[]{:S(2)}, u32[]{:S(2)}) collective-permute-start(f32[256,512]{1,0:T(8,128)} %collective-permute-done.7.refs_5_), channel_id=1, source_target_pairs={{0,8},{1,9},{2,10},{3,11},{4,12},{5,13},{6,14},{7,15},{8,0},{9,1},... | collective-permute-start | bytes 1572872 | tf_op jit(solution)/shard_map/ppermute | solution.py:47
  56.9 7.7 %collective-permute-start.13 = (f32[256,512]{1,0:T(8,128)}, f32[256,512]{1,0:T(8,128)S(1)}, u32[]{:S(2)}, u32[]{:S(2)}) collective-permute-start(f32[256,512]{1,0:T(8,128)} %collective-permute-done.8.refs_9_), channel_id=1, source_target_pairs={{0,8},{1,9},{2,10},{3,11},{4,12},{5,13},{6,14},{7,15},{8,0},{9,1},... | collective-permute-start | bytes 1572872 | tf_op jit(solution)/shard_map/ppermute | solution.py:47
  57.2 14.6 %collective-permute-start.15 = (f32[8,2048]{1,0:T(8,128)}, f32[8,2048]{1,0:T(8,128)S(1)}, u32[]{:S(2)}, u32[]{:S(2)}) collective-permute-start(f32[8,2048]{1,0:T(8,128)} %copy-done.2), channel_id=1, source_target_pairs={{0,9},{1,10},{2,11},{3,12},{4,13},{5,14},{6,15},{7,8},{8,17},{9,18... | collective-permute-start | bytes 196616 | tf_op jit(solution)/shard_map/ppermute | solution.py:56
  61.0 10.8 %collective-permute-start.17 = (f32[8,2048]{1,0:T(8,128)}, f32[8,2048]{1,0:T(8,128)S(1)}, u32[]{:S(2)}, u32[]{:S(2)}) collective-permute-start(f32[8,2048]{1,0:T(8,128)} %copy-done.1), channel_id=1, source_target_pairs={{0,15},{1,8},{2,9},{3,10},{4,11},{5,12},{6,13},{7,14},{8,23},{9,16... | collective-permute-start | bytes 196616 | tf_op jit(solution)/shard_map/ppermute | solution.py:56
  70.5 1.2 %collective-permute-start.14 = (f32[1,640]{1,0:T(1,128)S(1)}, f32[1,640]{1,0:T(1,128)S(1)}, u32[]{:S(2)}, u32[]{:S(2)}) collective-permute-start(f32[1,640]{1,0:T(1,128)S(1)} %get-tuple-element.57), channel_id=1, source_target_pairs={{0,8},{1,9},{2,10},{3,11},{4,12},{5,13},{6,14},{7,15},{8,0},{9,1},... | collective-permute-start | bytes 7688 | tf_op jit(solution)/shard_map/ppermute | solution.py:47
  80.0 22.5 %collective-permute-start.18 = (f32[16,128,128]{2,1,0:T(8,128)}, f32[16,128,128]{2,1,0:T(8,128)S(1)}, u32[]{:S(2)}, u32[]{:S(2)}) collective-permute-start(f32[16,128,128]{2,1,0:T(8,128)} %get-tuple-element.66), channel_id=1, source_target_pairs={{0,8},{1,9},{2,10},{3,11},{4,12},{5,13},{6,14},{7,15},{8,16},{9,17... | collective-permute-start | bytes 3145736 | tf_op jit(solution)/shard_map/ppermute | solution.py:56
  82.1 20.3 %all-to-all-start.1 = ((f32[128,1,640]{2,1,0:T(1,128)}), f32[128,1,640]{2,1,0:T(1,128)S(1)}, u32[]{:S(2)}, u32[]{:S(2)}) async-start(f32[128,1,640]{2,1,0:T(1,128)} %bitcast.9), calls=%async_computation.1 | async-start | bytes 655360 | tf_op jit(solution)/shard_map/all_to_all | solution.py:664
